TPU v7x, 512 devices: a whole 4x4x16 slice. The times are simulated.
512 devices in a mesh: lon: 32 (over z_lo, x), lat: 16 (over y, z_hi, core).
Axes of the slice: x: 4, y: 4, z: 16 (z_hi: 2, z_lo: 8; z = z_hi * 8 + z_lo), core: 2. Of those that a mesh axis runs over, the one named last changes fastest.
Arguments:
- fields: bfloat16 [128, 1024, 256], P('lat', 'lon'), may hold values from -6 to 6
- cotangent: bfloat16 [128, 1024, 256], P('lat', 'lon'), may hold values from -6 to 6
- land_sea: int32 [128, 1024], P('lat', 'lon'), may hold values 0 or 1
- partner: int32 [1024], replicated, may hold values from 0 to 1023, as said below
- kernel: float32 [7, 7, 256], replicated, may hold values from -0.875 to 0.875
- gain: float32 [256], replicated, may hold values from 0.25 to 1.75
- w_in: bfloat16 [1024, 256], replicated, may hold values from -0.375 to 0.375
- w_out: bfloat16 [1024, 256], replicated, may hold values from -0.1875 to 0.1875
Outputs:
- block_out: bfloat16 [128, 1024, 256], P('lat', 'lon')
- grad_input: bfloat16 [128, 1024, 256], P('lat', 'lon')
- grad_w_in: float32 [1024, 256], P(('lon', 'lat'))
- grad_w_out: float32 [1024, 256], P(('lon', 'lat'))
- grad_kernel: float32 [7, 7, 256], replicated
- grad_gain: float32 [256], replicated
Inputs may be any that keep to these rules, and one draw needn't show every extreme that they name: partner[i] = (s - i) mod 1024 for one s per draw, so the table is its own inverse.
All inputs are finite; a program needn't handle non-finite values. No bound on the sum of `land_sea` on one device may be relied on, other than what follows from the above.
Results may differ from a plain program's by a relative error of at most 0.0055.
Values may be sent and summed in bfloat16 or wider, within the bound.
No kernel may reach another device: no remote copies, remote signals or barrier semaphores. Data moves between devices by JAX's collectives and lax.ppermute only.
A program may use at most 64 MiB of HBM per device.

v0:
```python
import math

import jax
import jax.numpy as jnp
from jax import lax
from jax.sharding import PartitionSpec as P

EPS = 1e-06


def extended(value, sides, width, wrap):
    for axis, dim in sides:
        peers, length = (lax.axis_size(axis), value.shape[dim])
        up = [(i, (i + 1) % peers) for i in range(peers if wrap else peers - 1)]
        down = [(j, i) for i, j in up]
        last = lax.slice_in_dim(value, length - width, length, axis=dim)
        leading = lax.slice_in_dim(value, 0, width, axis=dim)
        before = lax.ppermute(last, axis, up)
        after = lax.ppermute(leading, axis, down)
        value = jnp.concatenate([before, value, after], axis=dim)
    return value


def shifted(value, axis, steps):
    count = lax.axis_size(axis)
    pairs = [(source, (source + steps) % count) for source in range(count)]
    return lax.ppermute(value, axis, pairs)


def from_behind(value, axis, steps):
    count = lax.axis_size(axis)
    leading, last = (max(0, -steps), min(count, count - steps))
    return lax.ppermute(value, axis, [(source, source + steps) for source in range(leading, last)])


def gelu_slope(values):
    result, pullback = jax.vjp(lambda inner: jax.nn.gelu(inner, approximate=True), values)
    return pullback(jnp.ones_like(values))[0]


def body(fields, cotangent, land_sea, partner, kernel, gain, w_in, w_out):
    rows, cols, width = fields.shape
    lat_count = lax.axis_size("lat")
    lon_count = lax.axis_size("lon")
    total_cols = cols * lon_count
    col_start = lax.axis_index("lon") * cols
    at_top = lax.axis_index("lat") == lat_count - 1
    tall = extended(fields, (("lat", 0),), 3, False)
    padded = extended(tall, (("lon", 1),), 3, True)
    summit = lax.all_gather(fields[rows - 3 :][::-1], "lon", axis=1, tiled=True)
    ext_cols = (col_start - 3 + jnp.arange(cols + 6, dtype=jnp.int32)) % total_cols
    mirrored = jnp.take(summit, partner[ext_cols], axis=1)
    upper = jnp.where(at_top, mirrored, padded[rows + 3 :])
    padded = jnp.concatenate([padded[: rows + 3], upper], 0)
    source = padded.astype(jnp.float32)
    conved = jnp.zeros((rows, cols, width), jnp.float32)
    for row_tap in range(7):
        for col_tap in range(7):
            conved = (
                conved
                + source[row_tap : row_tap + rows, col_tap : col_tap + cols]
                * kernel[row_tap, col_tap]
            )
    cells = rows * cols
    flat = conved.reshape(cells, width)
    average = jnp.mean(flat, -1, keepdims=True)
    centred = flat - average
    rstd = lax.rsqrt(jnp.mean(centred * centred, -1, keepdims=True) + EPS)
    normed = centred * rstd
    scaled = (normed * gain).astype(jnp.bfloat16)
    before = lax.dot_general(
        scaled, w_in, (((1,), (1,)), ((), ())), preferred_element_type=jnp.float32
    )
    hidden = jax.nn.gelu(before, approximate=True).astype(jnp.bfloat16)
    branch = jnp.dot(hidden, w_out, preferred_element_type=jnp.float32)
    keeper = land_sea.reshape(cells, 1).astype(jnp.float32)
    block_out = (keeper * (fields.reshape(cells, width).astype(jnp.float32) + branch)).astype(
        jnp.bfloat16
    )
    upstream = keeper * cotangent.reshape(cells, width).astype(jnp.float32)
    upstream_b = upstream.astype(jnp.bfloat16)
    dhidden = lax.dot_general(
        upstream_b, w_out, (((1,), (1,)), ((), ())), preferred_element_type=jnp.float32
    )
    dbefore = (dhidden * gelu_slope(before)).astype(jnp.bfloat16)
    dscaled = jnp.dot(dbefore, w_in, preferred_element_type=jnp.float32)
    gain_local = jnp.sum(dscaled * normed, 0)
    dnormed = dscaled * gain
    dconved = rstd * (
        dnormed
        - jnp.mean(dnormed, -1, keepdims=True)
        - normed * jnp.mean(dnormed * normed, -1, keepdims=True)
    )
    first = lax.dot_general(
        dbefore, scaled, (((0,), (0,)), ((), ())), preferred_element_type=jnp.float32
    )
    second = lax.dot_general(
        hidden, upstream_b, (((0,), (0,)), ((), ())), preferred_element_type=jnp.float32
    )
    shares = lax.psum_scatter(
        jnp.concatenate([first, second], 1), ("lon", "lat"), scatter_dimension=0, tiled=True
    )
    dgrid = dconved.reshape(rows, cols, width)
    kernel_terms = []
    dpadded = jnp.zeros((rows + 6, cols + 6, width), jnp.float32)
    for row_tap in range(7):
        for col_tap in range(7):
            kernel_terms.append(
                jnp.sum(source[row_tap : row_tap + rows, col_tap : col_tap + cols] * dgrid, (0, 1))
            )
            dpadded = dpadded.at[row_tap : row_tap + rows, col_tap : col_tap + cols].add(
                kernel[row_tap, col_tap] * dgrid
            )
    kernel_sum, gain_sum = lax.psum(
        (jnp.stack(kernel_terms).reshape(7, 7, width), gain_local), ("lon", "lat")
    )
    from_right = shifted(dpadded[:, :3].astype(jnp.bfloat16), "lon", -1).astype(jnp.float32)
    from_left = shifted(dpadded[:, cols + 3 :].astype(jnp.bfloat16), "lon", 1).astype(jnp.float32)
    core = dpadded[:, 3 : cols + 3]
    core = core.at[:, :3].add(from_left)
    core = core.at[:, cols - 3 :].add(from_right)
    from_above = from_behind(core[:3].astype(jnp.bfloat16), "lat", -1).astype(jnp.float32)
    from_below = from_behind(core[rows + 3 :].astype(jnp.bfloat16), "lat", 1).astype(jnp.float32)
    inner = core[3 : rows + 3]
    inner = inner.at[rows - 3 :].add(from_above)
    inner = inner.at[:3].add(from_below)
    own_cols = col_start + jnp.arange(cols, dtype=jnp.int32)
    rim_all = lax.all_gather(
        core[rows + 3 :].astype(jnp.bfloat16), "lon", axis=1, tiled=True
    ).astype(jnp.float32)
    picked = jnp.take(rim_all, partner[own_cols], axis=1)[::-1]
    inner = inner.at[rows - 3 :].add(jnp.where(at_top, picked, jnp.zeros_like(picked)))
    grad_input = (upstream.reshape(rows, cols, width) + inner).astype(jnp.bfloat16)
    factor = 1.0 / math.sqrt(rows * lat_count * total_cols)
    return (
        block_out.reshape(rows, cols, width),
        grad_input,
        shares[:, :width] * factor,
        shares[:, width:] * factor,
        kernel_sum * factor,
        gain_sum * factor,
    )


def solution(mesh):
    in_specs = (
        P("lat", "lon", None),
        P("lat", "lon", None),
        P("lat", "lon"),
        P(),
        P(),
        P(),
        P(),
        P(),
    )
    out_specs = (
        P("lat", "lon", None),
        P("lat", "lon", None),
        P(("lon", "lat"), None),
        P(("lon", "lat"), None),
        P(),
        P(),
    )
    return jax.shard_map(body, mesh=mesh, in_specs=in_specs, out_specs=out_specs, check_vma=False)
```

profile of v0, /device:TPU:8, one launch (start us, length us, event | category | flops | bytes accessed | tf_op | source)
XLA Modules:
  0.0 1015.3 jit_solution(15969827663455688333)
XLA Ops:
  7.3 1.0 copy.347
  8.3 1.9 collective-permute-start
  11.2 15.0 %collective-permute-start.1 = (bf16[3,32,256]{2,0,1:T(4,128)(2,1)S(1)}, bf16[3,32,256]{2,0,1:T(4,128)(2,1)S(1)}, u32[]{:S(2)}, u32[]{:S(2)}) collective-permute-start(bf16[3,32,256]{2,0,1:T(4,128)(2,1)S(1)} %get-tuple-element.754), channel_id=1, source_target_pairs={{1,0},{2,1},{3,2},{4,3},{5,4},{6,5},{7,6},{8,7},{9,8},{10,9},{11,1... | collective-permute-start | bytes 147464 | tf_op jit(solution)/shard_map/ppermute | solution.py:19
  26.2 0.7 convert_element_type.68
  27.0 1.0 copy_convert_fusion
  28.2 0.7 gather_fusion
  30.1 0.7 fusion.29
  32.0 0.8 and_reduce_fusion
  35.4 3.4 collective-permute-start.2
  38.9 12.1 %collective-permute-start.3 = (bf16[14,3,256]{2,0,1:T(8,128)(2,1)S(1)}, bf16[14,3,256]{2,0,1:T(8,128)(2,1)S(1)}, u32[]{:S(2)}, u32[]{:S(2)}) collective-permute-start(bf16[14,3,256]{2,0,1:T(8,128)(2,1)S(1)} %get-tuple-element.752), channel_id=1, source_target_pairs={{16,0},{32,16},{48,32},{64,48},{80,64},{96,80},{112,96},{128,112},... | collective-permute-start | bytes 64520 | tf_op jit(solution)/shard_map/ppermute | solution.py:19
  51.0 1.5 collective-permute-done.3
  52.4 0.9 pad_maximum_fusion.1
  53.3 189.1 %all-gather.3.cloned.1.call-done = bf16[3,1024,256]{2,1,0:T(8,128)(2,1)} async-done(((bf16[3,32,256]{2,1,0:T(8,128)(2,1)}), bf16[3,1024,256]{2,1,0:T(8,128)(2,1)}) %all-gather.3.cloned.1.call-update) | async-done | bytes 1572880 | tf_op jit(solution)/shard_map/all_gather | solution.py:50
  242.4 2.8 copy.351
  245.9 1.1 maximum_convert_fusion
  247.0 3.1 fusion.19
  251.3 1.5 fusion.18
  252.9 0.8 fusion
  253.7 0.9 multiply_reduce_fusion
  255.5 1.5 multiply_add_fusion
  257.0 1.6 scatter-add.181
  258.7 1.9 add_select_fusion.4
  260.6 1.5 scatter-add.184
  262.2 2.0 add_select_fusion.3
  264.2 1.5 scatter-add.185
  265.7 2.1 add_select_fusion.2
  267.9 1.5 scatter-add.186
  269.4 2.0 add_select_fusion.1
  271.5 1.5 scatter-add.189
  273.0 2.0 add_select_fusion
  275.0 1.6 scatter-add.190
  298.3 2.9 pad_maximum_fusion
  301.9 3.2 collective-permute-start.4
  305.1 11.4 %collective-permute-start.5 = (bf16[14,3,256]{2,0,1:T(8,128)(2,1)S(1)}, bf16[14,3,256]{2,0,1:T(8,128)(2,1)S(1)}, u32[]{:S(2)}, u32[]{:S(2)}) collective-permute-start(bf16[14,3,256]{2,0,1:T(8,128)(2,1)S(1)} %get-tuple-element.746), channel_id=1, source_target_pairs={{0,496},{16,0},{32,16},{48,32},{64,48},{80,64},{96,80},{112,96},{1... | collective-permute-start | bytes 64520 | tf_op jit(solution)/shard_map/ppermute | solution.py:27
  316.5 1.5 collective-permute-done.5
  318.9 0.7 gather_fusion.2
  320.9 110.1 %all-reduce.2 = (f32[7,7,256]{2,1,0:T(8,128)S(1)}, f32[256]{0:T(256)S(1)}) all-reduce(f32[7,7,256]{2,1,0:T(8,128)S(1)} %reshape.2069, f32[256]{0:T(256)S(1)} %copy-done.16), channel_id=1, replica_groups=mesh['lon'=32,'lat'=16] {'lon','lat'}, use_global_device_ids=true, to_apply=%region_59.60 | all-reduce | flops 12800 | bytes 102400 | tf_op jit(solution)/shard_map/psum | solution.py:114
  431.7 2.4 fusion.2
  434.0 4.6 collective-permute-start.6
  439.2 1.9 collective-permute-start.7
  441.8 12.7 %collective-permute-done.7 = bf16[3,32,256]{2,0,1:T(4,128)(2,1)S(1)} collective-permute-done((bf16[3,32,256]{2,0,1:T(4,128)(2,1)S(1)}, bf16[3,32,256]{2,0,1:T(4,128)(2,1)S(1)}, u32[]{:S(2)}, u32[]{:S(2)}) %collective-permute-start.7) | collective-permute-done | bytes 49184 | tf_op jit(solution)/shard_map/ppermute | solution.py:33
  454.8 321.2 %all-reduce.5.cloned.1.call-done = f32[1024,512]{0,1:T(8,128)} async-done(((f32[1024,512]{0,1:T(8,128)}), f32[1024,512]{0,1:T(8,128)}) %all-reduce.5.cloned.1.call-update) | async-done | bytes 2097168
  776.1 1.1 dynamic-slice_multiply_fusion
  777.2 0.7 copy.461
  778.5 221.2 %all-gather.5.cloned.1.call-done = bf16[3,1024,256]{2,1,0:T(8,128)(2,1)} async-done(((bf16[3,32,256]{2,1,0:T(8,128)(2,1)}), bf16[3,1024,256]{2,1,0:T(8,128)(2,1)}) %all-gather.5.cloned.1.call-update) | async-done | bytes 1572880 | tf_op jit(solution)/shard_map/all_gather | solution.py:128
  999.7 4.7 copy.409
  1004.4 2.8 gather_fusion.3
  1008.0 0.7 copy.459
  (208 shorter events, 36.5 us)
Async XLA Ops:
  7.2 243.8 %copy-start = (bf16[1024,256]{1,0:T(8,128)(2,1)S(1)}, bf16[1024,256]{1,0:T(8,128)(2,1)}, u32[]{:S(2)}) copy-start(bf16[1024,256]{1,0:T(8,128)(2,1)} %param.122) | copy-start | bytes 1572868
  7.2 24.8 %copy-start.17 = (s32[3]{0:T(128)S(1)}, s32[3]{0:T(128)}, u32[]{:S(2)}) copy-start(s32[3]{0:T(128)} %constant.1674.clone.1) | copy-start | bytes 40
  7.2 21.0 %copy-start.1 = (s32[1024]{0:T(1024)S(1)}, s32[1024]{0:T(1024)}, u32[]{:S(2)}) copy-start(s32[1024]{0:T(1024)} %param.119) | copy-start | bytes 12292
  7.2 25.7 %copy-start.5 = (f32[7,7,256]{2,1,0:T(8,128)S(1)}, f32[7,7,256]{2,1,0:T(8,128)}, u32[]{:S(2)}) copy-start(f32[7,7,256]{2,1,0:T(8,128)} %param.120) | copy-start | bytes 150532
  7.2 235.2 %all-gather.3.cloned.1.call-start = ((), (), s32[]{:S(2)}) async-start(), calls=%async_computation | async-start | bytes 1622016 | tf_op jit(solution)/shard_map/all_gather | solution.py:50
  8.3 27.1 %collective-permute-start = (bf16[3,32,256]{2,0,1:T(4,128)(2,1)S(1)}, bf16[3,32,256]{2,0,1:T(4,128)(2,1)S(1)}, u32[]{:S(2)}, u32[]{:S(2)}) collective-permute-start(bf16[3,32,256]{2,0,1:T(4,128)(2,1)S(1)} %get-tuple-element.753), channel_id=1, source_target_pairs={{0,1},{1,2},{2,3},{3,4},{4,5},{5,6},{6,7},{7,8},{8,9},{9,10},{10,1... | collective-permute-start | bytes 147464 | tf_op jit(solution)/shard_map/ppermute | solution.py:18
  11.1 764.9 %all-reduce.5.cloned.1.call-start = ((), (), s32[]{:S(2)}) async-start(), calls=%async_computation.2 | async-start | bytes 4194304
  11.2 24.2 %collective-permute-start.1 = (bf16[3,32,256]{2,0,1:T(4,128)(2,1)S(1)}, bf16[3,32,256]{2,0,1:T(4,128)(2,1)S(1)}, u32[]{:S(2)}, u32[]{:S(2)}) collective-permute-start(bf16[3,32,256]{2,0,1:T(4,128)(2,1)S(1)} %get-tuple-element.754), channel_id=1, source_target_pairs={{1,0},{2,1},{3,2},{4,3},{5,4},{6,5},{7,6},{8,7},{9,8},{10,9},{11,1... | collective-permute-start | bytes 147464 | tf_op jit(solution)/shard_map/ppermute | solution.py:19
  27.0 218.1 %copy-start.14 = (f32[256]{0:T(256)}, f32[256]{0:T(256)S(1)}, u32[]{:S(2)}) copy-start(f32[256]{0:T(256)S(1)} %convert_element_type.69) | copy-start | bytes 3076
  35.4 15.5 %collective-permute-start.2 = (bf16[14,3,256]{2,0,1:T(8,128)(2,1)S(1)}, bf16[14,3,256]{2,0,1:T(8,128)(2,1)S(1)}, u32[]{:S(2)}, u32[]{:S(2)}) collective-permute-start(bf16[14,3,256]{2,0,1:T(8,128)(2,1)S(1)} %get-tuple-element.751), channel_id=1, source_target_pairs={{0,16},{16,32},{32,48},{48,64},{64,80},{80,96},{96,112},{112,128},... | collective-permute-start | bytes 64520 | tf_op jit(solution)/shard_map/ppermute | solution.py:18
  38.9 13.6 %collective-permute-start.3 = (bf16[14,3,256]{2,0,1:T(8,128)(2,1)S(1)}, bf16[14,3,256]{2,0,1:T(8,128)(2,1)S(1)}, u32[]{:S(2)}, u32[]{:S(2)}) collective-permute-start(bf16[14,3,256]{2,0,1:T(8,128)(2,1)S(1)} %get-tuple-element.752), channel_id=1, source_target_pairs={{16,0},{32,16},{48,32},{64,48},{80,64},{96,80},{112,96},{128,112},... | collective-permute-start | bytes 64520 | tf_op jit(solution)/shard_map/ppermute | solution.py:19
  247.0 3.8 copy-start.13
  251.0 1.9 copy-start.18
  251.3 2.4 copy-start.2
  253.7 1.5 copy-start.11
  254.6 0.8 copy-start.12
  255.0 3.7 copy-start.10
  255.2 6.9 copy-start.9
  255.5 10.3 %copy-start.8 = (f32[1,1,256]{2,1,0:T(1,128)S(1)}, f32[1,1,256]{2,1,0:T(1,128)}, u32[]{:S(2)}) copy-start(f32[1,1,256]{2,1,0:T(1,128)} %get-tuple-element.800) | copy-start | bytes 3076
  258.7 10.8 %copy-start.7 = (f32[1,1,256]{2,1,0:T(1,128)S(1)}, f32[1,1,256]{2,1,0:T(1,128)}, u32[]{:S(2)}) copy-start(f32[1,1,256]{2,1,0:T(1,128)} %get-tuple-element.799) | copy-start | bytes 3076
  277.1 1.6 copy-start.6
  301.3 698.4 %all-gather.5.cloned.1.call-start = ((), (), s32[]{:S(2)}) async-start(), calls=%async_computation.1 | async-start | bytes 1622016 | tf_op jit(solution)/shard_map/all_gather | solution.py:128
  301.9 14.6 %collective-permute-start.4 = (bf16[14,3,256]{2,0,1:T(8,128)(2,1)S(1)}, bf16[14,3,256]{2,0,1:T(8,128)(2,1)S(1)}, u32[]{:S(2)}, u32[]{:S(2)}) collective-permute-start(bf16[14,3,256]{2,0,1:T(8,128)(2,1)S(1)} %get-tuple-element.747), channel_id=1, source_target_pairs={{0,16},{16,32},{32,48},{48,64},{64,80},{80,96},{96,112},{112,128},... | collective-permute-start | bytes 64520 | tf_op jit(solution)/shard_map/ppermute | solution.py:27
  305.1 12.9 %collective-permute-start.5 = (bf16[14,3,256]{2,0,1:T(8,128)(2,1)S(1)}, bf16[14,3,256]{2,0,1:T(8,128)(2,1)S(1)}, u32[]{:S(2)}, u32[]{:S(2)}) collective-permute-start(bf16[14,3,256]{2,0,1:T(8,128)(2,1)S(1)} %get-tuple-element.746), channel_id=1, source_target_pairs={{0,496},{16,0},{32,16},{48,32},{64,48},{80,64},{96,80},{112,96},{1... | collective-permute-start | bytes 64520 | tf_op jit(solution)/shard_map/ppermute | solution.py:27
  320.2 0.7 copy-start.16
  320.2 111.5 %copy-start.4 = (bf16[8,32,256]{2,1,0:T(8,128)(2,1)S(1)}, bf16[8,32,256]{2,1,0:T(8,128)(2,1)}, u32[]{:S(2)}) copy-start(bf16[8,32,256]{2,1,0:T(8,128)(2,1)} %param.116) | copy-start | bytes 393220
  320.2 111.5 %copy-start.15 = (f32[256]{0:T(256)S(1)}, f32[256]{0:T(256)}, u32[]{:S(2)}) copy-start(f32[256]{0:T(256)} %copy-done.14) | copy-start | bytes 3076
  320.2 111.5 %copy-start.19 = (bf16[1024,256]{1,0:T(8,128)(2,1)S(1)}, bf16[1024,256]{1,0:T(8,128)(2,1)}, u32[]{:S(2)}) copy-start(bf16[1024,256]{1,0:T(8,128)(2,1)} %param.123) | copy-start | bytes 1572868
  434.0 7.1 collective-permute-start.6
  439.2 15.3 %collective-permute-start.7 = (bf16[3,32,256]{2,0,1:T(4,128)(2,1)S(1)}, bf16[3,32,256]{2,0,1:T(4,128)(2,1)S(1)}, u32[]{:S(2)}, u32[]{:S(2)}) collective-permute-start(bf16[3,32,256]{2,0,1:T(4,128)(2,1)S(1)} %get-tuple-element.749), channel_id=1, source_target_pairs={{0,1},{1,2},{2,3},{3,4},{4,5},{5,6},{6,7},{7,8},{8,9},{9,10},{10,1... | collective-permute-start | bytes 147464 | tf_op jit(solution)/shard_map/ppermute | solution.py:33
  778.5 229.4 %copy-start.3 = (bf16[8,32,256]{2,1,0:T(8,128)(2,1)S(1)}, bf16[8,32,256]{2,1,0:T(8,128)(2,1)}, u32[]{:S(2)}) copy-start(bf16[8,32,256]{2,1,0:T(8,128)(2,1)} %param.117) | copy-start | bytes 393220
Sparse Core Ops, SparseCore 0:
  11.3 231.0 all-gather.2
  301.4 474.6 all-reduce.4
  778.7 220.8 all-gather.4
where the time goes:
time: 1020 us
  waiting for transfers between devices  747 us (73%)
  blocking collectives  110 us (11%)
  starting transfers between devices  53.6 us (5%)
  local copies, waits for them, and re-layouts  48.2 us (5%)
  other arithmetic  34.7 us (3%)
  between operations  15 us (1%)
    unnamed x4, waiting for transfers between devices  321 us
    all_gather x1, waiting for transfers between devices, body(): lax.all_gather(core[rows + 3:].astype(jnp.bfloat16), 'lon', axis=1, tiled...  221 us
    all_gather x1, waiting for transfers between devices, body(): summit = lax.all_gather(fields[rows - 3:][::-1], 'lon', axis=1, tiled=True)  189 us
    psum x1, blocking collectives, body(): lax.psum((jnp.stack(kernel_terms).reshape(7, 7, width), gain_local), ('lo...  110 us
    ppermute x2, starting transfers between devices, extended(): after = lax.ppermute(leading, axis, down)  27.1 us
    scatter-add x49, local copies, waits for them, and re-layouts, body(): dpadded.at[row_tap:row_tap + rows, col_tap:col_tap + cols]  23.3 us
  transfers between devices with their start and end apart: 11, of which 6 were waited for; matrix products, arithmetic and copies ran while one was open for 2% of the time, Pallas kernels for 0%

commit v1 on v0

v1 whole, which is shorter than its diff:
```python
import functools
import math

import jax
import jax.numpy as jnp
from jax import lax
from jax.experimental import pallas as pl
from jax.experimental.pallas import tpu as pltpu
from jax.sharding import PartitionSpec as P

EPS = 1e-06
ROWS, COLS, WIDTH, HIDDEN = 8, 32, 256, 1024
CELLS = ROWS * COLS
LANES = 128
CHUNK = 256
LEFT = 8
SMALL = 64
FOLD = 4
GELU_A = math.sqrt(2.0 / math.pi)
GELU_B = 0.044715
STAGES = ((0,), (3, 2), (5, 4), (1, 8), (7, 6))
SPLIT_STAGE = 2

f32, bf16 = jnp.float32, jnp.bfloat16


def dot(left, right, dims):
    return lax.dot_general(left, right, (dims, ((), ())), preferred_element_type=f32)


def packed(value):
    high = value.astype(bf16)
    low = (value - high.astype(f32)).astype(bf16)
    return high, low


def unpacked(high, low):
    return high.astype(f32) + low.astype(f32)


def assemble(info, own, south, north, west, east, folds, wide, fold):
    wide[pl.ds(3, ROWS), pl.ds(LEFT, COLS), :] = own[...].astype(f32)
    wide[pl.ds(0, 3), pl.ds(LEFT, COLS), :] = south[...].astype(f32)
    wide[:, pl.ds(LEFT - 3, 3), :] = west[...].astype(f32)
    wide[:, pl.ds(LEFT + COLS, 3), :] = east[...].astype(f32)

    @pl.when(info[0] == 0)
    def _():
        wide[pl.ds(ROWS + 3, 3), pl.ds(LEFT, COLS), :] = north[...].astype(f32)

    @pl.when(info[0] == 1)
    def _():
        for place, part in enumerate(folds):
            fold[:, pl.ds(place * COLS, COLS), :] = part[...].astype(f32)
        for column in range(COLS + 6):
            source = 2 * COLS + info[1] - column
            for row in range(3):
                wide[ROWS + 3 + row, pl.ds(LEFT - 3 + column, 1), :] = fold[2 - row, pl.ds(source, 1), :]


def main_kernel(
    info, own, south, north, west, east, fold0, fold1, fold2, cot, land, taps, gain, w_in, w_out,
    block_out, dconv, keep, message, sums, wide, fold, grid,
):
    assemble(info, own, south, north, west, east, (fold0, fold1, fold2), wide, fold)
    for half in range(WIDTH // LANES):
        lanes = pl.ds(half * LANES, LANES)
        for tile in range(COLS // 8):
            total = jnp.zeros((ROWS, 8, LANES), f32)
            for b in range(7):
                block = wide[:, pl.ds(LEFT - 3 + tile * 8 + b, 8), lanes]
                for a in range(7):
                    total = total + block[a : a + ROWS] * taps[pl.ds(7 * a + b, 1), lanes][None]
            grid[:, pl.ds(tile * 8, 8), lanes] = total
    flat = grid[...].reshape(CELLS, WIDTH)
    average = jnp.mean(flat, -1, keepdims=True)
    centred = flat - average
    rstd = lax.rsqrt(jnp.mean(centred * centred, -1, keepdims=True) + EPS)
    normed = centred * rstd
    gains = gain[...]
    scaled = (normed * gains).astype(bf16)
    keeper = land[...].astype(f32)
    upstream = (keeper * cot[...].reshape(CELLS, WIDTH).astype(f32)).astype(bf16)
    branch = jnp.zeros((CELLS, WIDTH), f32)
    dscaled = jnp.zeros((CELLS, WIDTH), f32)
    for part in range(2):
        for chunk in range(HIDDEN // 2 // CHUNK):
            start = pl.multiple_of((info[2] ^ part) * (HIDDEN // 2) + chunk * CHUNK, CHUNK)
            w_in_part, w_out_part = w_in[pl.ds(start, CHUNK), :], w_out[pl.ds(start, CHUNK), :]
            before = dot(scaled, w_in_part, ((1,), (1,)))
            square = before * before
            bend = jnp.tanh(before * (GELU_A + (GELU_A * GELU_B) * square))
            gate = 0.5 + 0.5 * bend
            hidden = (before * gate).astype(bf16)
            slope = gate + (0.5 * before) * (1.0 - bend * bend) * (GELU_A + (3.0 * GELU_A * GELU_B) * square)
            branch = branch + dot(hidden, w_out_part, ((1,), (0,)))
            dbefore = (dot(upstream, w_out_part, ((1,), (1,))) * slope).astype(bf16)
            dscaled = dscaled + dot(dbefore, w_in_part, ((1,), (0,)))
            target = message if part else keep
            units = pl.ds(chunk * CHUNK + SMALL * part, CHUNK)
            target[units, pl.ds(0, WIDTH)] = dot(dbefore, scaled, ((0,), (0,))).astype(target.dtype)
            target[units, pl.ds(WIDTH, WIDTH)] = dot(hidden, upstream, ((0,), (0,))).astype(target.dtype)
    centre = own[...].reshape(CELLS, WIDTH).astype(f32)
    block_out[...] = (keeper * (centre + branch)).astype(bf16).reshape(ROWS, COLS, WIDTH)
    dnormed = dscaled * gains
    dconved = rstd * (
        dnormed - jnp.mean(dnormed, -1, keepdims=True) - normed * jnp.mean(dnormed * normed, -1, keepdims=True)
    )
    dconv[...] = dconved.astype(bf16).reshape(ROWS, COLS, WIDTH)
    grid[...] = dconved.reshape(ROWS, COLS, WIDTH)
    sums[pl.ds(48, 16), :] = jnp.zeros((16, WIDTH), f32)
    sums[pl.ds(49, 1), :] = jnp.sum(dscaled * normed, 0, keepdims=True)
    for half in range(WIDTH // LANES):
        lanes = pl.ds(half * LANES, LANES)
        for b in range(7):
            totals = [jnp.zeros((8, LANES), f32) for _ in range(7)]
            for tile in range(COLS // 8):
                block = wide[:, pl.ds(LEFT - 3 + tile * 8 + b, 8), lanes]
                here = grid[:, pl.ds(tile * 8, 8), lanes]
                for a in range(7):
                    totals[a] = totals[a] + jnp.sum(block[a : a + ROWS] * here, 0)
            for a in range(7):
                sums[pl.ds(7 * a + b, 1), lanes] = jnp.sum(totals[a], 0, keepdims=True)
    high, low = packed(sums[...])
    message[pl.ds(0, SMALL), pl.ds(0, WIDTH)] = high
    message[pl.ds(0, SMALL), pl.ds(WIDTH, WIDTH)] = low
    sums[...] = unpacked(high, low)


def grad_input_kernel(
    info, own, south, north, west, east, fold0, fold1, fold2, cot, land, taps, grad_input, wide, fold, upstream
):
    assemble(info, own, south, north, west, east, (fold0, fold1, fold2), wide, fold)
    folded = info[0] == 1
    masked = land[...].astype(f32) * cot[...].reshape(CELLS, WIDTH).astype(f32)
    upstream[...] = masked.reshape(ROWS, COLS, WIDTH)
    for half in range(WIDTH // LANES):
        lanes = pl.ds(half * LANES, LANES)
        for tile in range(COLS // 8):
            total = upstream[:, pl.ds(tile * 8, 8), lanes]
            for b in range(7):
                block = wide[:, pl.ds(LEFT - 3 + tile * 8 + b, 8), lanes]
                for a in range(7):
                    weight = taps[pl.ds(48 - (7 * a + b), 1), lanes][None]
                    if a > 3:
                        rim = jnp.where(folded, taps[pl.ds(7 * a + b, 1), lanes][None], weight)
                        weight = jnp.concatenate(
                            [
                                jnp.broadcast_to(weight, (11 - a, 1, LANES)),
                                jnp.broadcast_to(rim, (a - 3, 1, LANES)),
                            ],
                            0,
                        )
                    total = total + block[a : a + ROWS] * weight
            grid_part = total.astype(bf16)
            grad_input[:, pl.ds(tile * 8, 8), lanes] = grid_part


def pairwise(parts):
    while len(parts) > 1:
        parts = [left + right for left, right in zip(parts[::2], parts[1::2])]
    return parts[0]


def padded(span):
    return max(span, 16)


def combined(rows, keep, sums, received):
    large, small = pl.ds(sums.shape[0], padded(rows)), pl.ds(0, sums.shape[0])
    total = pairwise([keep[...]] + [part[large, :].astype(f32)[:rows] for part in received])
    others = [unpacked(part[small, pl.ds(0, WIDTH)], part[small, pl.ds(WIDTH, WIDTH)]) for part in received]
    return total, pairwise([sums[...]] + others)


def stage_kernel(have, want, split, index, keep, sums, *refs):
    received, messages = refs[: have - 1], refs[have - 1 : have - 1 + want - 1]
    keep_out, sums_out, stack, small = refs[have - 1 + want - 1 :]
    rows = keep.shape[0]
    span = rows // want
    total, total_sums = combined(rows, keep, sums, received)
    height = sums_out.shape[0]
    for part in range(want):
        stack[part] = total[part * span : part * span + span]
    high, low = packed(total_sums)
    if split:
        both = jnp.concatenate([high.astype(f32), low.astype(f32)], 1)
        for part in range(want):
            small[part] = both[part * height : part * height + height]
    for mask in range(1, want):
        message = messages[mask - 1]
        large = stack[index[0] ^ mask]
        if span < padded(span):
            large = jnp.concatenate([large, jnp.zeros((padded(span) - span, 2 * WIDTH), f32)], 0)
        message[pl.ds(height, padded(span)), :] = large.astype(bf16)
        if split:
            message[pl.ds(0, height), :] = small[index[0] ^ mask].astype(bf16)
        else:
            message[pl.ds(0, height), pl.ds(0, WIDTH)] = high
            message[pl.ds(0, height), pl.ds(WIDTH, WIDTH)] = low
    keep_out[...] = stack[index[0]]
    if split:
        mine = small[index[0]]
        sums_out[...] = mine[:, :WIDTH] + mine[:, WIDTH:]
    else:
        sums_out[...] = unpacked(high, low)


def last_kernel(factor, have, keep, sums, *refs):
    received, (first, second, small) = refs[: have - 1], refs[have - 1 :]
    total, total_sums = combined(keep.shape[0], keep, sums, received)
    first[...] = total[:, :WIDTH] * factor
    second[...] = total[:, WIDTH:] * factor
    small[...] = total_sums * factor


def gather_kernel(index, own, *refs):
    others, (grad_kernel, grad_gain, stack) = refs[:-3], refs[-3:]
    height = own.shape[0]
    for mask, part in enumerate((own,) + others):
        place = pl.multiple_of((index[0] ^ mask) * height, height)
        stack[pl.ds(place, height), :] = part[...]
    for row in range(7):
        grad_kernel[row] = stack[pl.ds(7 * row, 7), :]
    grad_gain[...] = stack[pl.ds(49, 1), :]


def run(kernel, out, scratch, scalars, *args):
    whole = pl.BlockSpec(memory_space=pltpu.VMEM)
    specs = [pl.BlockSpec(memory_space=pltpu.SMEM)] * (scalars is not None) + [whole] * len(args)
    call = pl.pallas_call(
        kernel,
        out_shape=out,
        in_specs=specs,
        out_specs=jax.tree.map(lambda _: whole, out),
        scratch_shapes=scratch,
        compiler_params=pltpu.CompilerParams(vmem_limit_bytes=48 * 1024 * 1024),
    )
    return call(*(() if scalars is None else (scalars,)), *args)


def fold_reflect(step, lat_count, lon_count):
    pairs = [
        (((step - lon) % lon_count + 1) * lat_count - 1, (lon + 1) * lat_count - 1) for lon in range(lon_count)
    ]
    return lambda last: lax.ppermute(last, ("lon", "lat"), pairs)


def fold_rotate(step, lat_count, lon_count):
    def moved(value, offset):
        if offset == 0:
            return value
        pairs = [
            (((lon + offset) % lon_count + 1) * lat_count - 1, (lon + 1) * lat_count - 1) for lon in range(lon_count)
        ]
        return lax.ppermute(value, ("lon", "lat"), pairs)

    return lambda value: tuple(moved(value, offset - step) for offset in (2, 1, 0))


def halo(value, shift):
    rows, cols, width = value.shape
    lat_count, lon_count = lax.axis_size("lat"), lax.axis_size("lon")
    first, last = value[:3], value[rows - 3 :]
    block = shift // cols
    south = lax.ppermute(last, "lat", [(i, i + 1) for i in range(lat_count - 1)])
    north = lax.ppermute(first, "lat", [(i + 1, i) for i in range(lat_count - 1)])
    reflected = lax.switch(
        block // FOLD, [fold_reflect(FOLD * k, lat_count, lon_count) for k in range(lon_count // FOLD)], last
    )
    ring = [(i, (i + 1) % lon_count) for i in range(lon_count)]
    right = jnp.concatenate([south[:, cols - 3 :], value[:, cols - 3 :], north[:, cols - 3 :]], 0)
    left = jnp.concatenate([south[:, :3], value[:, :3], north[:, :3]], 0)
    west = lax.ppermute(right, "lon", ring)
    east = lax.ppermute(left, "lon", [(j, i) for i, j in ring])
    folds = lax.switch(block % FOLD, [fold_rotate(k, lat_count, lon_count) for k in range(FOLD)], reflected)
    return (value, south, north, west, east) + tuple(folds)


def exchange(bits, messages):
    count = lax.axis_size("lat") * lax.axis_size("lon")
    out = []
    for mask, message in enumerate(messages, 1):
        flips = sum(1 << bit for place, bit in enumerate(reversed(bits)) if mask >> place & 1)
        out.append(lax.ppermute(message, ("lon", "lat"), [(i, i ^ flips) for i in range(count)]))
    return out


def stage_index(bits):
    flat = lax.axis_index("lon") * lax.axis_size("lat") + lax.axis_index("lat")
    index = 0
    for bit in bits:
        index = 2 * index + (flat >> bit & 1)
    return index


def reordered(weights):
    count = sum(len(bits) for bits in STAGES)
    order = [count - 1 - bit for bits in STAGES for bit in bits]
    split = weights.reshape((2,) * count + (weights.shape[0] >> count, weights.shape[1]))
    return split.transpose(order + [count, count + 1]).reshape(weights.shape)


def body(fields, cotangent, land_sea, partner, kernel, gain, w_in, w_out):
    shape = jax.ShapeDtypeStruct
    total_cols = COLS * lax.axis_size("lon")
    shift = (partner[0] + 3) % total_cols
    at_top = lax.axis_index("lat") == lax.axis_size("lat") - 1
    info = jnp.stack([at_top.astype(jnp.int32), shift % COLS, stage_index(STAGES[0])])
    taps = kernel.reshape(49, WIDTH)
    land = land_sea.reshape(CELLS, 1)
    grid_shape = shape((ROWS, COLS, WIDTH), bf16)
    wide = pltpu.VMEM((ROWS + 6, COLS + 16, WIDTH), f32)
    fold = pltpu.VMEM((3, 3 * COLS, WIDTH), f32)
    grid = pltpu.VMEM((ROWS, COLS, WIDTH), f32)
    rows = HIDDEN // 2
    block_out, dconved, keep, message, sums = run(
        main_kernel,
        (
            grid_shape,
            grid_shape,
            shape((rows, 2 * WIDTH), f32),
            shape((rows + SMALL, 2 * WIDTH), bf16),
            shape((SMALL, WIDTH), f32),
        ),
        [wide, fold, grid],
        info,
        *halo(fields, shift),
        cotangent,
        land,
        taps,
        gain.reshape(1, WIDTH),
        reordered(w_in),
        reordered(w_out),
    )
    messages = [message]
    height = SMALL
    for stage in range(len(STAGES) - 1):
        received = exchange(STAGES[stage], messages)
        want, split = 1 << len(STAGES[stage + 1]), stage + 1 == SPLIT_STAGE
        span = rows // want
        height = height // want if split else height
        *messages, keep, sums = run(
            functools.partial(stage_kernel, len(received) + 1, want, split),
            tuple([shape((padded(span) + height, 2 * WIDTH), bf16)] * (want - 1))
            + (shape((span, 2 * WIDTH), f32), shape((height, WIDTH), f32)),
            [pltpu.VMEM((want, span, 2 * WIDTH), f32), pltpu.VMEM((want, height, 2 * WIDTH), f32)],
            stage_index(STAGES[stage + 1]).reshape(1),
            keep,
            sums,
            *received,
        )
        rows = span
    received = exchange(STAGES[-1], messages)
    factor = 1.0 / math.sqrt(CELLS * lax.axis_size("lat") * lax.axis_size("lon"))
    share = shape((rows, WIDTH), f32)
    grad_w_in, grad_w_out, small = run(
        functools.partial(last_kernel, factor, len(received) + 1),
        (share, share, shape((height, WIDTH), f32)),
        [],
        None,
        keep,
        sums,
        *received,
    )
    bits = STAGES[SPLIT_STAGE]
    grad_kernel, grad_gain = run(
        gather_kernel,
        (shape((7, 7, WIDTH), f32), shape((1, WIDTH), f32)),
        [pltpu.VMEM((SMALL, WIDTH), f32)],
        stage_index(bits).reshape(1),
        small,
        *exchange(bits, [small] * ((1 << len(bits)) - 1)),
    )
    grad_input = run(
        grad_input_kernel, grid_shape, [wide, fold, grid], info, *halo(dconved, shift), cotangent, land, taps
    )
    return block_out, grad_input, grad_w_in, grad_w_out, grad_kernel, grad_gain.reshape(WIDTH)


def solution(mesh):
    cells = P("lat", "lon", None)
    share = P(("lon", "lat"), None)
    return jax.shard_map(
        body,
        mesh=mesh,
        in_specs=(cells, cells, P("lat", "lon"), P(), P(), P(), P(), P()),
        out_specs=(cells, cells, share, share, P(), P()),
        check_vma=False,
    )
```

time: 1020 us -> 179 us (0.18)
  the two profiles are of different devices: /device:TPU:8 before, /device:TPU:1 now
where the time goes in v1:
time: 179 us; the launch traced here: 178 us
  starting transfers between devices  124 us (69%)
  waiting for transfers between devices  27.1 us (15%)
  Pallas kernels  13.2 us (7%)
  local copies, waits for them, and re-layouts  11.1 us (6%)
  between operations  1.86 us (1%)
    ppermute x16, starting transfers between devices, exchange(): lax.ppermute(message, ('lon', 'lat'), [(i, i ^ flips) for i in range(coun...  75.4 us
    ppermute x2, starting transfers between devices, halo(): lax.ppermute(last, 'lat', [(i, i + 1) for i in range(lat_count - 1)])  25.2 us
    ppermute x16, waiting for transfers between devices, exchange(): lax.ppermute(message, ('lon', 'lat'), [(i, i ^ flips) for i in range(coun...  13.8 us
    pallas_call x8, Pallas kernels, run(): return call(*(() if scalars is None else (scalars,)), *args)  13.2 us
    ppermute x2, waiting for transfers between devices, halo(): lax.ppermute(first, 'lat', [(i + 1, i) for i in range(lat_count - 1)])  10.2 us
    ppermute x2, starting transfers between devices, halo(): east = lax.ppermute(left, 'lon', [(j, i) for i, j in ring])  9.49 us
    cond x4, local copies, waits for them, and re-layouts  4.06 us
    ppermute x4, starting transfers between devices, moved(): return lax.ppermute(value, ('lon', 'lat'), pairs)  3.98 us
  transfers between devices with their start and end apart: 30, of which 7 were waited for; matrix products, arithmetic and copies ran while one was open for 5% of the time, Pallas kernels for 3%

profile of v1, /device:TPU:1, one launch (start us, length us, event | category | flops | bytes accessed | tf_op | source)
XLA Modules:
  0.0 177.8 jit_solution(935908623903028430)
XLA Ops:
  0.7 0.9 fusion.3
  1.5 16.8 %collective-permute-start.34 = (bf16[3,32,256]{2,1,0:T(8,128)(2,1)S(1)}, bf16[3,32,256]{2,1,0:T(8,128)(2,1)S(1)}, u32[]{:S(2)}, u32[]{:S(2)}) collective-permute-start(bf16[3,32,256]{2,1,0:T(8,128)(2,1)S(1)} %get-tuple-element.127), channel_id=1, source_target_pairs={{0,1},{1,2},{2,3},{3,4},{4,5},{5,6},{6,7},{7,8},{8,9},{9,10},{10,1... | collective-permute-start | bytes 147464 | tf_op jit(solution)/shard_map/ppermute | solution.py:266
  18.4 1.9 %collective-permute-start.35 = (bf16[3,32,256]{2,1,0:T(8,128)(2,1)S(1)}, bf16[3,32,256]{2,1,0:T(8,128)(2,1)S(1)}, u32[]{:S(2)}, u32[]{:S(2)}) collective-permute-start(bf16[3,32,256]{2,1,0:T(8,128)(2,1)S(1)} %get-tuple-element.126), channel_id=1, source_target_pairs={{1,0},{2,1},{3,2},{4,3},{5,4},{6,5},{7,6},{8,7},{9,8},{10,9},{11,1... | collective-permute-start | bytes 147464 | tf_op jit(solution)/shard_map/ppermute | solution.py:267
  20.3 1.2 slice.99
  22.3 10.2 %collective-permute-done.35.north = bf16[3,32,256]{2,1,0:T(8,128)(2,1)S(1)} collective-permute-done((bf16[3,32,256]{2,1,0:T(8,128)(2,1)S(1)}, bf16[3,32,256]{2,1,0:T(8,128)(2,1)S(1)}, u32[]{:S(2)}, u32[]{:S(2)}) %collective-permute-start.35) | collective-permute-done | bytes 49184 | tf_op jit(solution)/shard_map/ppermute | solution.py:267
  32.5 7.6 %collective-permute-start.37 = (bf16[14,3,256]{2,1,0:T(4,128)(2,1)S(1)}, bf16[14,3,256]{2,1,0:T(4,128)(2,1)S(1)}, u32[]{:S(2)}, u32[]{:S(2)}) collective-permute-start(bf16[14,3,256]{2,1,0:T(4,128)(2,1)S(1)} %pad_maximum_fusion.1), channel_id=1, source_target_pairs={{16,0},{32,16},{48,32},{64,48},{80,64},{96,80},{112,96},{128,112},... | collective-permute-start | bytes 64520 | tf_op jit(solution)/shard_map/ppermute | solution.py:275
  40.2 1.9 %collective-permute-start.36 = (bf16[14,3,256]{2,1,0:T(4,128)(2,1)S(1)}, bf16[14,3,256]{2,1,0:T(4,128)(2,1)S(1)}, u32[]{:S(2)}, u32[]{:S(2)}) collective-permute-start(bf16[14,3,256]{2,1,0:T(4,128)(2,1)S(1)} %pad_maximum_fusion), channel_id=1, source_target_pairs={{0,16},{16,32},{32,48},{48,64},{64,80},{80,96},{96,112},{112,128},... | collective-permute-start | bytes 64520 | tf_op jit(solution)/shard_map/ppermute | solution.py:274
  42.2 1.3 conditional.4
  42.2 1.3 collective-permute-start
  43.5 0.8 reshape.64.land
  45.3 0.8 copy-done.4
  47.1 4.1 %conditional.5 = (bf16[3,32,256]{2,1,0:T(8,128)(2,1)}, bf16[3,32,256]{2,1,0:T(8,128)(2,1)}, bf16[3,32,256]{2,1,0:T(8,128)(2,1)}) conditional(s32[]{:T(128)} %clamp.8, bf16[3,32,256]{2,1,0:T(8,128)(2,1)} %get-tuple-element.160, bf16[3,32,256]{2,1,0:T(8,128)(2,1)} %get-tuple-element.160, ...), branch_computations={%region_8.9_spmd, %region_9.10_spmd, %region_10.11_spmd, %region_1... | conditional | bytes 688272 | solution.py:276
  47.1 1.4 collective-permute-start.12
  49.2 1.4 copy.38
  51.2 2.3 %collective-permute-done.36.west = bf16[14,3,256]{2,1,0:T(4,128)(2,1)S(1)} collective-permute-done((bf16[14,3,256]{2,1,0:T(4,128)(2,1)S(1)}, bf16[14,3,256]{2,1,0:T(4,128)(2,1)S(1)}, u32[]{:S(2)}, u32[]{:S(2)}) %collective-permute-start.36) | collective-permute-done | bytes 21536 | tf_op jit(solution)/shard_map/ppermute | solution.py:274
  53.5 0.7 copy-done.2
  54.2 7.7 %shard_map.127 = (bf16[8,32,256]{2,1,0:T(8,128)(2,1)}, bf16[8,32,256]{2,1,0:T(8,128)(2,1)S(1)}, f32[512,512]{1,0:T(8,128)S(1)}, bf16[576,512]{1,0:T(8,128)(2,1)S(1)}, f32[64,256]{1,0:T(8,128)S(1)}) custom-call(s32[3]{0:T(128)S(1)} %pad_add_fusion.info, bf16[8,32,256]{2,1,0:T(8,128)(2,1)S(1)} %copy-done, ...), custom_call_target="tpu_custom_call" | custom-call | tf_op jit(solution)/shard_map/pallas_call | solution.py:239
  61.9 1.9 %collective-permute-start.42 = (bf16[576,512]{1,0:T(8,128)(2,1)S(1)}, bf16[576,512]{1,0:T(8,128)(2,1)S(1)}, u32[]{:S(2)}, u32[]{:S(2)}) collective-permute-start(bf16[576,512]{1,0:T(8,128)(2,1)S(1)} %get-tuple-element.94), channel_id=1, source_target_pairs={{0,1},{1,0},{2,3},{3,2},{4,5},{5,4},{6,7},{7,6},{8,9},{9,8},{10,11... | collective-permute-start | bytes 1769480 | tf_op jit(solution)/shard_map/ppermute | solution.py:285
  64.4 8.3 %collective-permute-start.38 = (bf16[3,32,256]{2,1,0:T(8,128)(2,1)}, bf16[3,32,256]{2,1,0:T(8,128)(2,1)S(1)}, u32[]{:S(2)}, u32[]{:S(2)}) collective-permute-start(bf16[3,32,256]{2,1,0:T(8,128)(2,1)} %get-tuple-element.123), channel_id=1, source_target_pairs={{0,1},{1,2},{2,3},{3,4},{4,5},{5,6},{6,7},{7,8},{8,9},{9,10},{10,1... | collective-permute-start | bytes 147464 | tf_op jit(solution)/shard_map/ppermute | solution.py:266
  72.8 1.3 conditional.6
  72.8 1.3 collective-permute-start.17
  74.1 4.0 %conditional.7 = (bf16[3,32,256]{2,1,0:T(8,128)(2,1)}, bf16[3,32,256]{2,1,0:T(8,128)(2,1)}, bf16[3,32,256]{2,1,0:T(8,128)(2,1)}) conditional(s32[]{:T(128)} %clamp.8, bf16[3,32,256]{2,1,0:T(8,128)(2,1)} %get-tuple-element.161, bf16[3,32,256]{2,1,0:T(8,128)(2,1)} %get-tuple-element.161, ...), branch_computations={%region_20.21_spmd, %region_21.22_spmd, %region_22.23_spmd, %regio... | conditional | bytes 688272 | solution.py:276
  74.1 1.3 collective-permute-start.29
  76.0 1.4 copy.58
  78.1 1.9 %collective-permute-start.39 = (bf16[3,32,256]{2,1,0:T(8,128)(2,1)S(1)}, bf16[3,32,256]{2,1,0:T(8,128)(2,1)S(1)}, u32[]{:S(2)}, u32[]{:S(2)}) collective-permute-start(bf16[3,32,256]{2,1,0:T(8,128)(2,1)S(1)} %get-tuple-element.122), channel_id=1, source_target_pairs={{1,0},{2,1},{3,2},{4,3},{5,4},{6,5},{7,6},{8,7},{9,8},{10,9},{11,1... | collective-permute-start | bytes 147464 | tf_op jit(solution)/shard_map/ppermute | solution.py:267
  80.2 3.2 %collective-permute-start.43 = (bf16[192,512]{1,0:T(8,128)(2,1)S(1)}, bf16[192,512]{1,0:T(8,128)(2,1)S(1)}, u32[]{:S(2)}, u32[]{:S(2)}) collective-permute-start(bf16[192,512]{1,0:T(8,128)(2,1)S(1)} %get-tuple-element.97), channel_id=1, source_target_pairs={{0,4},{1,5},{2,6},{3,7},{4,0},{5,1},{6,2},{7,3},{8,12},{9,13},{10,... | collective-permute-start | bytes 589832 | tf_op jit(solution)/shard_map/ppermute | solution.py:285
  83.4 12.4 %collective-permute-start.44 = (bf16[192,512]{1,0:T(8,128)(2,1)S(1)}, bf16[192,512]{1,0:T(8,128)(2,1)S(1)}, u32[]{:S(2)}, u32[]{:S(2)}) collective-permute-start(bf16[192,512]{1,0:T(8,128)(2,1)S(1)} %get-tuple-element.98), channel_id=1, source_target_pairs={{0,8},{1,9},{2,10},{3,11},{4,12},{5,13},{6,14},{7,15},{8,0},{9,1},... | collective-permute-start | bytes 589832 | tf_op jit(solution)/shard_map/ppermute | solution.py:285
  95.8 1.9 %collective-permute-start.45 = (bf16[192,512]{1,0:T(8,128)(2,1)S(1)}, bf16[192,512]{1,0:T(8,128)(2,1)S(1)}, u32[]{:S(2)}, u32[]{:S(2)}) collective-permute-start(bf16[192,512]{1,0:T(8,128)(2,1)S(1)} %get-tuple-element.99), channel_id=1, source_target_pairs={{0,12},{1,13},{2,14},{3,15},{4,8},{5,9},{6,10},{7,11},{8,4},{9,5},... | collective-permute-start | bytes 589832 | tf_op jit(solution)/shard_map/ppermute | solution.py:285
  97.8 3.6 %collective-permute-done.44.refs_1_ = bf16[192,512]{1,0:T(8,128)(2,1)S(1)} collective-permute-done((bf16[192,512]{1,0:T(8,128)(2,1)S(1)}, bf16[192,512]{1,0:T(8,128)(2,1)S(1)}, u32[]{:S(2)}, u32[]{:S(2)}) %collective-permute-start.44) | collective-permute-done | bytes 196640 | tf_op jit(solution)/shard_map/ppermute | solution.py:285
  101.4 4.3 %collective-permute-done.45.refs_2_ = bf16[192,512]{1,0:T(8,128)(2,1)S(1)} collective-permute-done((bf16[192,512]{1,0:T(8,128)(2,1)S(1)}, bf16[192,512]{1,0:T(8,128)(2,1)S(1)}, u32[]{:S(2)}, u32[]{:S(2)}) %collective-permute-start.45) | collective-permute-done | bytes 196640 | tf_op jit(solution)/shard_map/ppermute | solution.py:285
  105.9 1.9 %collective-permute-start.46 = (bf16[48,512]{1,0:T(8,128)(2,1)S(1)}, bf16[48,512]{1,0:T(8,128)(2,1)S(1)}, u32[]{:S(2)}, u32[]{:S(2)}) collective-permute-start(bf16[48,512]{1,0:T(8,128)(2,1)S(1)} %get-tuple-element.102), channel_id=1, source_target_pairs={{0,16},{1,17},{2,18},{3,19},{4,20},{5,21},{6,22},{7,23},{8,24},{9,... | collective-permute-start | bytes 147464 | tf_op jit(solution)/shard_map/ppermute | solution.py:285
  107.8 1.9 %collective-permute-start.47 = (bf16[48,512]{1,0:T(8,128)(2,1)S(1)}, bf16[48,512]{1,0:T(8,128)(2,1)S(1)}, u32[]{:S(2)}, u32[]{:S(2)}) collective-permute-start(bf16[48,512]{1,0:T(8,128)(2,1)S(1)} %get-tuple-element.103), channel_id=1, source_target_pairs={{0,32},{1,33},{2,34},{3,35},{4,36},{5,37},{6,38},{7,39},{8,40},{9,... | collective-permute-start | bytes 147464 | tf_op jit(solution)/shard_map/ppermute | solution.py:285
  109.7 5.7 %collective-permute-start.48 = (bf16[48,512]{1,0:T(8,128)(2,1)S(1)}, bf16[48,512]{1,0:T(8,128)(2,1)S(1)}, u32[]{:S(2)}, u32[]{:S(2)}) collective-permute-start(bf16[48,512]{1,0:T(8,128)(2,1)S(1)} %get-tuple-element.104), channel_id=1, source_target_pairs={{0,48},{1,49},{2,50},{3,51},{4,52},{5,53},{6,54},{7,55},{8,56},{9,... | collective-permute-start | bytes 147464 | tf_op jit(solution)/shard_map/ppermute | solution.py:285
  115.5 1.4 collective-permute-done.48.refs_2_
  117.0 1.9 %collective-permute-start.49 = (bf16[32,512]{1,0:T(8,128)(2,1)S(1)}, bf16[32,512]{1,0:T(8,128)(2,1)S(1)}, u32[]{:S(2)}, u32[]{:S(2)}) collective-permute-start(bf16[32,512]{1,0:T(8,128)(2,1)S(1)} %get-tuple-element.107), channel_id=1, source_target_pairs={{0,256},{1,257},{2,258},{3,259},{4,260},{5,261},{6,262},{7,263},{8... | collective-permute-start | bytes 98312 | tf_op jit(solution)/shard_map/ppermute | solution.py:285
  118.9 23.0 %collective-permute-start.50 = (bf16[32,512]{1,0:T(8,128)(2,1)S(1)}, bf16[32,512]{1,0:T(8,128)(2,1)S(1)}, u32[]{:S(2)}, u32[]{:S(2)}) collective-permute-start(bf16[32,512]{1,0:T(8,128)(2,1)S(1)} %get-tuple-element.108), channel_id=1, source_target_pairs={{0,2},{1,3},{2,0},{3,1},{4,6},{5,7},{6,4},{7,5},{8,10},{9,11},{10,... | collective-permute-start | bytes 98312 | tf_op jit(solution)/shard_map/ppermute | solution.py:285
  141.9 2.2 %collective-permute-start.51 = (bf16[32,512]{1,0:T(8,128)(2,1)S(1)}, bf16[32,512]{1,0:T(8,128)(2,1)S(1)}, u32[]{:S(2)}, u32[]{:S(2)}) collective-permute-start(bf16[32,512]{1,0:T(8,128)(2,1)S(1)} %get-tuple-element.109), channel_id=1, source_target_pairs={{0,258},{1,259},{2,256},{3,257},{4,262},{5,263},{6,260},{7,261},{8... | collective-permute-start | bytes 98312 | tf_op jit(solution)/shard_map/ppermute | solution.py:285
  144.2 1.9 %collective-permute-start.41 = (bf16[14,3,256]{2,1,0:T(4,128)(2,1)S(1)}, bf16[14,3,256]{2,1,0:T(4,128)(2,1)S(1)}, u32[]{:S(2)}, u32[]{:S(2)}) collective-permute-start(bf16[14,3,256]{2,1,0:T(4,128)(2,1)S(1)} %pad_maximum_fusion.3), channel_id=1, source_target_pairs={{16,0},{32,16},{48,32},{64,48},{80,64},{96,80},{112,96},{128,112},... | collective-permute-start | bytes 64520 | tf_op jit(solution)/shard_map/ppermute | solution.py:275
  146.1 4.4 %collective-permute-done.51.refs_2_ = bf16[32,512]{1,0:T(8,128)(2,1)S(1)} collective-permute-done((bf16[32,512]{1,0:T(8,128)(2,1)S(1)}, bf16[32,512]{1,0:T(8,128)(2,1)S(1)}, u32[]{:S(2)}, u32[]{:S(2)}) %collective-permute-start.51) | collective-permute-done | bytes 32800 | tf_op jit(solution)/shard_map/ppermute | solution.py:285
  150.5 1.9 %collective-permute-start.52 = (bf16[32,512]{1,0:T(8,128)(2,1)S(1)}, bf16[32,512]{1,0:T(8,128)(2,1)S(1)}, u32[]{:S(2)}, u32[]{:S(2)}) collective-permute-start(bf16[32,512]{1,0:T(8,128)(2,1)S(1)} %get-tuple-element.112), channel_id=1, source_target_pairs={{0,64},{1,65},{2,66},{3,67},{4,68},{5,69},{6,70},{7,71},{8,72},{9,... | collective-permute-start | bytes 98312 | tf_op jit(solution)/shard_map/ppermute | solution.py:285
  152.5 1.9 %collective-permute-start.53 = (bf16[32,512]{1,0:T(8,128)(2,1)S(1)}, bf16[32,512]{1,0:T(8,128)(2,1)S(1)}, u32[]{:S(2)}, u32[]{:S(2)}) collective-permute-start(bf16[32,512]{1,0:T(8,128)(2,1)S(1)} %get-tuple-element.113), channel_id=1, source_target_pairs={{0,128},{1,129},{2,130},{3,131},{4,132},{5,133},{6,134},{7,135},{8... | collective-permute-start | bytes 98312 | tf_op jit(solution)/shard_map/ppermute | solution.py:285
  154.4 5.4 %collective-permute-start.54 = (bf16[32,512]{1,0:T(8,128)(2,1)S(1)}, bf16[32,512]{1,0:T(8,128)(2,1)S(1)}, u32[]{:S(2)}, u32[]{:S(2)}) collective-permute-start(bf16[32,512]{1,0:T(8,128)(2,1)S(1)} %get-tuple-element.114), channel_id=1, source_target_pairs={{0,192},{1,193},{2,194},{3,195},{4,196},{5,197},{6,198},{7,199},{8... | collective-permute-start | bytes 98312 | tf_op jit(solution)/shard_map/ppermute | solution.py:285
  159.9 1.9 %collective-permute-start.40 = (bf16[14,3,256]{2,1,0:T(4,128)(2,1)S(1)}, bf16[14,3,256]{2,1,0:T(4,128)(2,1)S(1)}, u32[]{:S(2)}, u32[]{:S(2)}) collective-permute-start(bf16[14,3,256]{2,1,0:T(4,128)(2,1)S(1)} %pad_maximum_fusion.2), channel_id=1, source_target_pairs={{0,16},{16,32},{32,48},{48,64},{64,80},{80,96},{96,112},{112,128},... | collective-permute-start | bytes 64520 | tf_op jit(solution)/shard_map/ppermute | solution.py:274
  162.4 2.0 %collective-permute-start.55 = (f32[16,256]{1,0:T(8,128)S(1)}, f32[16,256]{1,0:T(8,128)S(1)}, u32[]{:S(2)}, u32[]{:S(2)}) collective-permute-start(f32[16,256]{1,0:T(8,128)S(1)} %get-tuple-element.117.own), channel_id=1, source_target_pairs={{0,16},{1,17},{2,18},{3,19},{4,20},{5,21},{6,22},{7,23},{8,24},{9,... | collective-permute-start | bytes 49160 | tf_op jit(solution)/shard_map/ppermute | solution.py:285
  164.4 5.8 %collective-permute-start.56 = (f32[16,256]{1,0:T(8,128)S(1)}, f32[16,256]{1,0:T(8,128)S(1)}, u32[]{:S(2)}, u32[]{:S(2)}) collective-permute-start(f32[16,256]{1,0:T(8,128)S(1)} %get-tuple-element.117.own), channel_id=1, source_target_pairs={{0,32},{1,33},{2,34},{3,35},{4,36},{5,37},{6,38},{7,39},{8,40},{9,... | collective-permute-start | bytes 49160 | tf_op jit(solution)/shard_map/ppermute | solution.py:285
  170.2 2.2 %collective-permute-start.57 = (f32[16,256]{1,0:T(8,128)S(1)}, f32[16,256]{1,0:T(8,128)S(1)}, u32[]{:S(2)}, u32[]{:S(2)}) collective-permute-start(f32[16,256]{1,0:T(8,128)S(1)} %get-tuple-element.117.own), channel_id=1, source_target_pairs={{0,48},{1,49},{2,50},{3,51},{4,52},{5,53},{6,54},{7,55},{8,56},{9,... | collective-permute-start | bytes 49160 | tf_op jit(solution)/shard_map/ppermute | solution.py:285
  172.4 0.8 collective-permute-done.40.west
  173.2 3.9 %shard_map.128 = bf16[8,32,256]{2,1,0:T(8,128)(2,1)} custom-call(s32[3]{0:T(128)S(1)} %pad_add_fusion.info, bf16[8,32,256]{2,1,0:T(8,128)(2,1)S(1)} %get-tuple-element.88.own, bf16[3,32,256]{2,1,0:T(8,128)(2,1)S(1)} %collective-permute-done.38.south, bf16[3,32,256]{2,1,0:T(8,128)(2,1)S(1)} %collective-permute-done.39.north, ...), custom_call_target="tpu_custom_call" | custom-call | tf_op jit(solution)/shard_map/pallas_call | solution.py:239
  (62 shorter events, 7.0 us)
Async XLA Ops:
  0.6 19.7 %copy-start = (bf16[8,32,256]{2,1,0:T(8,128)(2,1)S(1)}, bf16[8,32,256]{2,1,0:T(8,128)(2,1)}, u32[]{:S(2)}) copy-start(bf16[8,32,256]{2,1,0:T(8,128)(2,1)} %own.1) | copy-start | bytes 393220
  0.6 43.7 %copy-start.3 = (bf16[1024,256]{1,0:T(8,128)(2,1)S(1)}, bf16[1024,256]{1,0:T(8,128)(2,1)}, u32[]{:S(2)}) copy-start(bf16[1024,256]{1,0:T(8,128)(2,1)} %param.38) | copy-start | bytes 1572868
  1.5 20.7 %collective-permute-start.34 = (bf16[3,32,256]{2,1,0:T(8,128)(2,1)S(1)}, bf16[3,32,256]{2,1,0:T(8,128)(2,1)S(1)}, u32[]{:S(2)}, u32[]{:S(2)}) collective-permute-start(bf16[3,32,256]{2,1,0:T(8,128)(2,1)S(1)} %get-tuple-element.127), channel_id=1, source_target_pairs={{0,1},{1,2},{2,3},{3,4},{4,5},{5,6},{6,7},{7,8},{8,9},{9,10},{10,1... | collective-permute-start | bytes 147464 | tf_op jit(solution)/shard_map/ppermute | solution.py:266
  18.4 14.1 %collective-permute-start.35 = (bf16[3,32,256]{2,1,0:T(8,128)(2,1)S(1)}, bf16[3,32,256]{2,1,0:T(8,128)(2,1)S(1)}, u32[]{:S(2)}, u32[]{:S(2)}) collective-permute-start(bf16[3,32,256]{2,1,0:T(8,128)(2,1)S(1)} %get-tuple-element.126), channel_id=1, source_target_pairs={{1,0},{2,1},{3,2},{4,3},{5,4},{6,5},{7,6},{8,7},{9,8},{10,9},{11,1... | collective-permute-start | bytes 147464 | tf_op jit(solution)/shard_map/ppermute | solution.py:267
  32.5 18.7 %collective-permute-start.37 = (bf16[14,3,256]{2,1,0:T(4,128)(2,1)S(1)}, bf16[14,3,256]{2,1,0:T(4,128)(2,1)S(1)}, u32[]{:S(2)}, u32[]{:S(2)}) collective-permute-start(bf16[14,3,256]{2,1,0:T(4,128)(2,1)S(1)} %pad_maximum_fusion.1), channel_id=1, source_target_pairs={{16,0},{32,16},{48,32},{64,48},{80,64},{96,80},{112,96},{128,112},... | collective-permute-start | bytes 64520 | tf_op jit(solution)/shard_map/ppermute | solution.py:275
  40.2 13.3 %collective-permute-start.36 = (bf16[14,3,256]{2,1,0:T(4,128)(2,1)S(1)}, bf16[14,3,256]{2,1,0:T(4,128)(2,1)S(1)}, u32[]{:S(2)}, u32[]{:S(2)}) collective-permute-start(bf16[14,3,256]{2,1,0:T(4,128)(2,1)S(1)} %pad_maximum_fusion), channel_id=1, source_target_pairs={{0,16},{16,32},{32,48},{48,64},{64,80},{80,96},{96,112},{112,128},... | collective-permute-start | bytes 64520 | tf_op jit(solution)/shard_map/ppermute | solution.py:274
  42.2 1.3 collective-permute-start
  43.4 0.8 copy-start.5
  45.1 1.0 copy-start.4
  47.1 6.4 %copy-start.1 = (bf16[8,32,256]{2,1,0:T(8,128)(2,1)S(1)}, bf16[8,32,256]{2,1,0:T(8,128)(2,1)}, u32[]{:S(2)}) copy-start(bf16[8,32,256]{2,1,0:T(8,128)(2,1)} %cot.3) | copy-start | bytes 393220
  47.1 3.5 %collective-permute-start.12 = (bf16[3,32,256]{2,1,0:T(8,128)(2,1)}, bf16[3,32,256]{2,1,0:T(8,128)(2,1)}, u32[]{:S(2)}, u32[]{:S(2)}) collective-permute-start(bf16[3,32,256]{2,1,0:T(8,128)(2,1)} %param.10), channel_id=1, source_target_pairs={{511,15},{15,31},{31,47},{47,63},{63,79},{79,95},{95,111},{111,127... | collective-permute-start | bytes 147464 | tf_op jit(solution)/shard_map/cond/branch_2_fun/ppermute | solution.py:256
  48.5 2.1 %collective-permute-start.13 = (bf16[3,32,256]{2,1,0:T(8,128)(2,1)}, bf16[3,32,256]{2,1,0:T(8,128)(2,1)S(1)}, u32[]{:S(2)}, u32[]{:S(2)}) collective-permute-start(bf16[3,32,256]{2,1,0:T(8,128)(2,1)} %param.10), channel_id=1, source_target_pairs={{495,15},{511,31},{15,47},{31,63},{47,79},{63,95},{79,111},{95,127... | collective-permute-start | bytes 147464 | tf_op jit(solution)/shard_map/cond/branch_2_fun/ppermute | solution.py:256
  53.5 0.7 copy-start.2
  61.9 18.1 %collective-permute-start.42 = (bf16[576,512]{1,0:T(8,128)(2,1)S(1)}, bf16[576,512]{1,0:T(8,128)(2,1)S(1)}, u32[]{:S(2)}, u32[]{:S(2)}) collective-permute-start(bf16[576,512]{1,0:T(8,128)(2,1)S(1)} %get-tuple-element.94), channel_id=1, source_target_pairs={{0,1},{1,0},{2,3},{3,2},{4,5},{5,4},{6,7},{7,6},{8,9},{9,8},{10,11... | collective-permute-start | bytes 1769480 | tf_op jit(solution)/shard_map/ppermute | solution.py:285
  64.4 33.3 %collective-permute-start.38 = (bf16[3,32,256]{2,1,0:T(8,128)(2,1)}, bf16[3,32,256]{2,1,0:T(8,128)(2,1)S(1)}, u32[]{:S(2)}, u32[]{:S(2)}) collective-permute-start(bf16[3,32,256]{2,1,0:T(8,128)(2,1)} %get-tuple-element.123), channel_id=1, source_target_pairs={{0,1},{1,2},{2,3},{3,4},{4,5},{5,6},{6,7},{7,8},{8,9},{9,10},{10,1... | collective-permute-start | bytes 147464 | tf_op jit(solution)/shard_map/ppermute | solution.py:266
  72.8 1.3 collective-permute-start.17
  74.1 3.3 %collective-permute-start.29 = (bf16[3,32,256]{2,1,0:T(8,128)(2,1)}, bf16[3,32,256]{2,1,0:T(8,128)(2,1)}, u32[]{:S(2)}, u32[]{:S(2)}) collective-permute-start(bf16[3,32,256]{2,1,0:T(8,128)(2,1)} %param.22), channel_id=1, source_target_pairs={{511,15},{15,31},{31,47},{47,63},{63,79},{79,95},{95,111},{111,127... | collective-permute-start | bytes 147464 | tf_op jit(solution)/shard_map/cond/branch_2_fun/ppermute | solution.py:256
  75.4 2.1 %collective-permute-start.30 = (bf16[3,32,256]{2,1,0:T(8,128)(2,1)}, bf16[3,32,256]{2,1,0:T(8,128)(2,1)S(1)}, u32[]{:S(2)}, u32[]{:S(2)}) collective-permute-start(bf16[3,32,256]{2,1,0:T(8,128)(2,1)} %param.22), channel_id=1, source_target_pairs={{495,15},{511,31},{15,47},{31,63},{47,79},{63,95},{79,111},{95,127... | collective-permute-start | bytes 147464 | tf_op jit(solution)/shard_map/cond/branch_2_fun/ppermute | solution.py:256
  78.1 37.4 %collective-permute-start.39 = (bf16[3,32,256]{2,1,0:T(8,128)(2,1)S(1)}, bf16[3,32,256]{2,1,0:T(8,128)(2,1)S(1)}, u32[]{:S(2)}, u32[]{:S(2)}) collective-permute-start(bf16[3,32,256]{2,1,0:T(8,128)(2,1)S(1)} %get-tuple-element.122), channel_id=1, source_target_pairs={{1,0},{2,1},{3,2},{4,3},{5,4},{6,5},{7,6},{8,7},{9,8},{10,9},{11,1... | collective-permute-start | bytes 147464 | tf_op jit(solution)/shard_map/ppermute | solution.py:267
  80.2 17.5 %collective-permute-start.43 = (bf16[192,512]{1,0:T(8,128)(2,1)S(1)}, bf16[192,512]{1,0:T(8,128)(2,1)S(1)}, u32[]{:S(2)}, u32[]{:S(2)}) collective-permute-start(bf16[192,512]{1,0:T(8,128)(2,1)S(1)} %get-tuple-element.97), channel_id=1, source_target_pairs={{0,4},{1,5},{2,6},{3,7},{4,0},{5,1},{6,2},{7,3},{8,12},{9,13},{10,... | collective-permute-start | bytes 589832 | tf_op jit(solution)/shard_map/ppermute | solution.py:285
  83.4 18.0 %collective-permute-start.44 = (bf16[192,512]{1,0:T(8,128)(2,1)S(1)}, bf16[192,512]{1,0:T(8,128)(2,1)S(1)}, u32[]{:S(2)}, u32[]{:S(2)}) collective-permute-start(bf16[192,512]{1,0:T(8,128)(2,1)S(1)} %get-tuple-element.98), channel_id=1, source_target_pairs={{0,8},{1,9},{2,10},{3,11},{4,12},{5,13},{6,14},{7,15},{8,0},{9,1},... | collective-permute-start | bytes 589832 | tf_op jit(solution)/shard_map/ppermute | solution.py:285
  95.8 9.9 %collective-permute-start.45 = (bf16[192,512]{1,0:T(8,128)(2,1)S(1)}, bf16[192,512]{1,0:T(8,128)(2,1)S(1)}, u32[]{:S(2)}, u32[]{:S(2)}) collective-permute-start(bf16[192,512]{1,0:T(8,128)(2,1)S(1)} %get-tuple-element.99), channel_id=1, source_target_pairs={{0,12},{1,13},{2,14},{3,15},{4,8},{5,9},{6,10},{7,11},{8,4},{9,5},... | collective-permute-start | bytes 589832 | tf_op jit(solution)/shard_map/ppermute | solution.py:285
  105.9 9.6 %collective-permute-start.46 = (bf16[48,512]{1,0:T(8,128)(2,1)S(1)}, bf16[48,512]{1,0:T(8,128)(2,1)S(1)}, u32[]{:S(2)}, u32[]{:S(2)}) collective-permute-start(bf16[48,512]{1,0:T(8,128)(2,1)S(1)} %get-tuple-element.102), channel_id=1, source_target_pairs={{0,16},{1,17},{2,18},{3,19},{4,20},{5,21},{6,22},{7,23},{8,24},{9,... | collective-permute-start | bytes 147464 | tf_op jit(solution)/shard_map/ppermute | solution.py:285
  107.8 7.7 %collective-permute-start.47 = (bf16[48,512]{1,0:T(8,128)(2,1)S(1)}, bf16[48,512]{1,0:T(8,128)(2,1)S(1)}, u32[]{:S(2)}, u32[]{:S(2)}) collective-permute-start(bf16[48,512]{1,0:T(8,128)(2,1)S(1)} %get-tuple-element.103), channel_id=1, source_target_pairs={{0,32},{1,33},{2,34},{3,35},{4,36},{5,37},{6,38},{7,39},{8,40},{9,... | collective-permute-start | bytes 147464 | tf_op jit(solution)/shard_map/ppermute | solution.py:285
  109.7 7.2 %collective-permute-start.48 = (bf16[48,512]{1,0:T(8,128)(2,1)S(1)}, bf16[48,512]{1,0:T(8,128)(2,1)S(1)}, u32[]{:S(2)}, u32[]{:S(2)}) collective-permute-start(bf16[48,512]{1,0:T(8,128)(2,1)S(1)} %get-tuple-element.104), channel_id=1, source_target_pairs={{0,48},{1,49},{2,50},{3,51},{4,52},{5,53},{6,54},{7,55},{8,56},{9,... | collective-permute-start | bytes 147464 | tf_op jit(solution)/shard_map/ppermute | solution.py:285
  117.0 29.1 %collective-permute-start.49 = (bf16[32,512]{1,0:T(8,128)(2,1)S(1)}, bf16[32,512]{1,0:T(8,128)(2,1)S(1)}, u32[]{:S(2)}, u32[]{:S(2)}) collective-permute-start(bf16[32,512]{1,0:T(8,128)(2,1)S(1)} %get-tuple-element.107), channel_id=1, source_target_pairs={{0,256},{1,257},{2,258},{3,259},{4,260},{5,261},{6,262},{7,263},{8... | collective-permute-start | bytes 98312 | tf_op jit(solution)/shard_map/ppermute | solution.py:285
  118.9 27.2 %collective-permute-start.50 = (bf16[32,512]{1,0:T(8,128)(2,1)S(1)}, bf16[32,512]{1,0:T(8,128)(2,1)S(1)}, u32[]{:S(2)}, u32[]{:S(2)}) collective-permute-start(bf16[32,512]{1,0:T(8,128)(2,1)S(1)} %get-tuple-element.108), channel_id=1, source_target_pairs={{0,2},{1,3},{2,0},{3,1},{4,6},{5,7},{6,4},{7,5},{8,10},{9,11},{10,... | collective-permute-start | bytes 98312 | tf_op jit(solution)/shard_map/ppermute | solution.py:285
  141.9 8.6 %collective-permute-start.51 = (bf16[32,512]{1,0:T(8,128)(2,1)S(1)}, bf16[32,512]{1,0:T(8,128)(2,1)S(1)}, u32[]{:S(2)}, u32[]{:S(2)}) collective-permute-start(bf16[32,512]{1,0:T(8,128)(2,1)S(1)} %get-tuple-element.109), channel_id=1, source_target_pairs={{0,258},{1,259},{2,256},{3,257},{4,262},{5,263},{6,260},{7,261},{8... | collective-permute-start | bytes 98312 | tf_op jit(solution)/shard_map/ppermute | solution.py:285
  144.2 28.3 %collective-permute-start.41 = (bf16[14,3,256]{2,1,0:T(4,128)(2,1)S(1)}, bf16[14,3,256]{2,1,0:T(4,128)(2,1)S(1)}, u32[]{:S(2)}, u32[]{:S(2)}) collective-permute-start(bf16[14,3,256]{2,1,0:T(4,128)(2,1)S(1)} %pad_maximum_fusion.3), channel_id=1, source_target_pairs={{16,0},{32,16},{48,32},{64,48},{80,64},{96,80},{112,96},{128,112},... | collective-permute-start | bytes 64520 | tf_op jit(solution)/shard_map/ppermute | solution.py:275
  150.5 11.3 %collective-permute-start.52 = (bf16[32,512]{1,0:T(8,128)(2,1)S(1)}, bf16[32,512]{1,0:T(8,128)(2,1)S(1)}, u32[]{:S(2)}, u32[]{:S(2)}) collective-permute-start(bf16[32,512]{1,0:T(8,128)(2,1)S(1)} %get-tuple-element.112), channel_id=1, source_target_pairs={{0,64},{1,65},{2,66},{3,67},{4,68},{5,69},{6,70},{7,71},{8,72},{9,... | collective-permute-start | bytes 98312 | tf_op jit(solution)/shard_map/ppermute | solution.py:285
  152.5 9.3 %collective-permute-start.53 = (bf16[32,512]{1,0:T(8,128)(2,1)S(1)}, bf16[32,512]{1,0:T(8,128)(2,1)S(1)}, u32[]{:S(2)}, u32[]{:S(2)}) collective-permute-start(bf16[32,512]{1,0:T(8,128)(2,1)S(1)} %get-tuple-element.113), channel_id=1, source_target_pairs={{0,128},{1,129},{2,130},{3,131},{4,132},{5,133},{6,134},{7,135},{8... | collective-permute-start | bytes 98312 | tf_op jit(solution)/shard_map/ppermute | solution.py:285
  154.4 7.4 %collective-permute-start.54 = (bf16[32,512]{1,0:T(8,128)(2,1)S(1)}, bf16[32,512]{1,0:T(8,128)(2,1)S(1)}, u32[]{:S(2)}, u32[]{:S(2)}) collective-permute-start(bf16[32,512]{1,0:T(8,128)(2,1)S(1)} %get-tuple-element.114), channel_id=1, source_target_pairs={{0,192},{1,193},{2,194},{3,195},{4,196},{5,197},{6,198},{7,199},{8... | collective-permute-start | bytes 98312 | tf_op jit(solution)/shard_map/ppermute | solution.py:285
  159.9 13.3 %collective-permute-start.40 = (bf16[14,3,256]{2,1,0:T(4,128)(2,1)S(1)}, bf16[14,3,256]{2,1,0:T(4,128)(2,1)S(1)}, u32[]{:S(2)}, u32[]{:S(2)}) collective-permute-start(bf16[14,3,256]{2,1,0:T(4,128)(2,1)S(1)} %pad_maximum_fusion.2), channel_id=1, source_target_pairs={{0,16},{16,32},{32,48},{48,64},{64,80},{80,96},{96,112},{112,128},... | collective-permute-start | bytes 64520 | tf_op jit(solution)/shard_map/ppermute | solution.py:274
  162.4 14.7 %collective-permute-start.55 = (f32[16,256]{1,0:T(8,128)S(1)}, f32[16,256]{1,0:T(8,128)S(1)}, u32[]{:S(2)}, u32[]{:S(2)}) collective-permute-start(f32[16,256]{1,0:T(8,128)S(1)} %get-tuple-element.117.own), channel_id=1, source_target_pairs={{0,16},{1,17},{2,18},{3,19},{4,20},{5,21},{6,22},{7,23},{8,24},{9,... | collective-permute-start | bytes 49160 | tf_op jit(solution)/shard_map/ppermute | solution.py:285
  164.4 12.7 %collective-permute-start.56 = (f32[16,256]{1,0:T(8,128)S(1)}, f32[16,256]{1,0:T(8,128)S(1)}, u32[]{:S(2)}, u32[]{:S(2)}) collective-permute-start(f32[16,256]{1,0:T(8,128)S(1)} %get-tuple-element.117.own), channel_id=1, source_target_pairs={{0,32},{1,33},{2,34},{3,35},{4,36},{5,37},{6,38},{7,39},{8,40},{9,... | collective-permute-start | bytes 49160 | tf_op jit(solution)/shard_map/ppermute | solution.py:285
  170.2 6.9 %collective-permute-start.57 = (f32[16,256]{1,0:T(8,128)S(1)}, f32[16,256]{1,0:T(8,128)S(1)}, u32[]{:S(2)}, u32[]{:S(2)}) collective-permute-start(f32[16,256]{1,0:T(8,128)S(1)} %get-tuple-element.117.own), channel_id=1, source_target_pairs={{0,48},{1,49},{2,50},{3,51},{4,52},{5,53},{6,54},{7,55},{8,56},{9,... | collective-permute-start | bytes 49160 | tf_op jit(solution)/shard_map/ppermute | solution.py:285

commit v2 on v1

v2 whole, which is shorter than its diff:
```python
import functools
import math

import jax
import jax.numpy as jnp
import numpy as np
from jax import lax
from jax.experimental import pallas as pl
from jax.experimental.pallas import tpu as pltpu
from jax.sharding import PartitionSpec as P

EPS = 1e-06
ROWS, COLS, WIDTH, HIDDEN = 8, 32, 256, 1024
CELLS = ROWS * COLS
LANES = 128
CHUNK = 256
LEFT = 8
ACROSS = 4
EDGE = 8
SPAN = COLS + EDGE
FOLD = 2
BEYOND = 5
GELU_A = math.sqrt(2.0 / math.pi)
GELU_B = 0.044715
f32, bf16 = jnp.float32, jnp.bfloat16


def dot(left, right, dims):
    return lax.dot_general(left, right, (dims, ((), ())), preferred_element_type=f32)


def edges(info, grid, messages):
    block = grid[ROWS - 3 :].reshape(3 * COLS, WIDTH).astype(bf16)
    left, right = [
        grid[:, start : start + EDGE].reshape(ROWS * EDGE, WIDTH).astype(bf16) for start in (0, COLS - EDGE)
    ]
    even = info[1] == 0
    for message, here, there in zip(messages, (right, left), (left, right)):
        message[pl.ds(0, ROWS * EDGE), :] = jnp.where(even, here.astype(f32), there.astype(f32)).astype(bf16)
        message[pl.ds(ROWS * EDGE, 3 * COLS), :] = block


def edge_kernel(info, own, *messages):
    edges(info, own[...].astype(f32), messages)


def middle(info, wide, first, own, sides):
    wide[pl.ds(first, ROWS), pl.ds(LEFT, COLS), :] = own[...].astype(f32)
    margin = pl.ds(0, ROWS * EDGE)
    for parity, starts in enumerate(((LEFT + COLS, 0), (0, LEFT + COLS))):

        @pl.when(info[1] == parity)
        def _():
            for start, side in zip(starts, sides):
                part = side[margin, :].astype(f32).reshape(ROWS, EDGE, WIDTH)
                wide[pl.ds(first, ROWS), pl.ds(start, EDGE), :] = part


def rows_kernel(info, turn, own, side0, side1, *refs):
    near, far, window, extra, wide, line = refs[-6:]
    middle(info, wide, 0, own, (side0, side1))
    columns = pl.ds(LEFT - 3, SPAN)
    for parity, order in enumerate(((near, far), (far, near))):

        @pl.when(info[2] == parity)
        def _():
            for message, start in zip(order, (ROWS - 3, 0)):
                message[...] = wide[pl.ds(start, 3), columns, :].reshape(3 * SPAN, WIDTH).astype(bf16)

    @pl.when(info[0] == 1)
    def _():
        block = pl.ds(ROWS * EDGE, 3 * COLS)
        line[:, pl.ds(COLS, COLS), :] = own[pl.ds(ROWS - 3, 3)].astype(f32)
        for parity, starts in enumerate(((2 * COLS, 0), (0, 2 * COLS))):

            @pl.when(info[1] == parity)
            def _():
                for start, side in zip(starts, (side0, side1)):
                    line[:, pl.ds(start, COLS), :] = side[block, :].astype(f32).reshape(3, COLS, WIDTH)

        for column in range(COLS + 6):
            source = jnp.maximum(COLS + turn[0] - column, 0)
            for row in range(3):
                wide[row, pl.ds(column, 1), :] = line[2 - row, pl.ds(source, 1), :]
            if column > COLS:
                source = jnp.minimum((FOLD + 1) * COLS + turn[0] - column, 3 * COLS - 1)
                for row in range(3):
                    wide[3 + row, pl.ds(column - COLS - 1, 1), :] = line[2 - row, pl.ds(source, 1), :]
        extra[pl.ds(0, 3 * EDGE), :] = wide[pl.ds(3, 3), pl.ds(0, EDGE), :].reshape(3 * EDGE, WIDTH).astype(bf16)
        window[...] = wide[pl.ds(0, 3), pl.ds(0, SPAN), :].reshape(3 * SPAN, WIDTH).astype(bf16)


def assemble(info, turn, own, side0, side1, near, far, window, extra, wide):
    middle(info, wide, 3, own, (side0, side1))
    columns = pl.ds(LEFT - 3, SPAN)
    for parity, (below, above) in enumerate(((far, near), (near, far))):

        @pl.when(info[2] == parity)
        def _():
            for part, start in ((below, 0), (above, ROWS + 3)):
                wide[pl.ds(start, 3), columns, :] = part[...].astype(f32).reshape(3, SPAN, WIDTH)

    @pl.when(info[0] == 1)
    def _():
        wide[pl.ds(ROWS + 3, 3), columns, :] = window[...].astype(f32).reshape(3, SPAN, WIDTH)
        rest = extra[pl.ds(0, 3 * EDGE), :].astype(f32).reshape(3, EDGE, WIDTH)
        for place in range(BEYOND):
            column = COLS + 1 + place

            @pl.when(turn[0] - column < -COLS)
            def _():
                wide[pl.ds(ROWS + 3, 3), pl.ds(LEFT - 3 + column, 1), :] = rest[:, place : place + 1]


def keepers(land):
    spot = lax.broadcasted_iota(jnp.int32, (1, COLS, COLS), 1) == lax.broadcasted_iota(jnp.int32, (1, COLS, COLS), 2)
    values = land[...].astype(f32)[:, None, :]
    return jnp.sum(jnp.where(spot, values, 0.0), -1, keepdims=True)


def main_kernel(
    info, turn, own, side0, side1, near, far, window, extra, cot, land, taps, gain, w_in, w_out,
    block_out, dconv, message0, message1, message, wide, grid, sums,
):
    assemble(info, turn, own, side0, side1, near, far, window, extra, wide)
    for half in range(WIDTH // LANES):
        lanes = pl.ds(half * LANES, LANES)
        for tile in range(COLS // 8):
            total = jnp.zeros((ROWS, 8, LANES), f32)
            for b in range(7):
                block = wide[:, pl.ds(LEFT - 3 + tile * 8 + b, 8), lanes]
                for a in range(7):
                    total = total + block[a : a + ROWS] * taps[a, pl.ds(b, 1), lanes][None]
            grid[:, pl.ds(tile * 8, 8), lanes] = total
    flat = grid[...].reshape(CELLS, WIDTH)
    average = jnp.mean(flat, -1, keepdims=True)
    centred = flat - average
    rstd = lax.rsqrt(jnp.mean(centred * centred, -1, keepdims=True) + EPS)
    normed = centred * rstd
    gains = gain[...]
    scaled = (normed * gains).astype(bf16)
    keeper = keepers(land)
    upstream = (keeper * cot[...].astype(f32)).astype(bf16).reshape(CELLS, WIDTH)
    branch = jnp.zeros((CELLS, WIDTH), f32)
    dscaled = jnp.zeros((CELLS, WIDTH), f32)
    plane, span = message.shape[0], HIDDEN // message.shape[0]
    for chunk in range(HIDDEN // CHUNK):
        units = pl.ds(chunk * CHUNK, CHUNK)
        w_in_part, w_out_part = w_in[units, :], w_out[units, :]
        before = dot(scaled, w_in_part, ((1,), (1,)))
        square = before * before
        bend = jnp.tanh(before * (GELU_A + (GELU_A * GELU_B) * square))
        gate = 0.5 + 0.5 * bend
        hidden = (before * gate).astype(bf16)
        slope = gate + (0.5 * before) * (1.0 - bend * bend) * (GELU_A + (3.0 * GELU_A * GELU_B) * square)
        branch = branch + dot(hidden, w_out_part, ((1,), (0,)))
        dbefore = (dot(upstream, w_out_part, ((1,), (1,))) * slope).astype(bf16)
        dscaled = dscaled + dot(dbefore, w_in_part, ((1,), (0,)))
        places = pl.ds(chunk * CHUNK // span, CHUNK // span)
        for pair, (units_of, cells_of) in enumerate(((dbefore, scaled), (hidden, upstream))):
            product = dot(units_of, cells_of, ((0,), (0,))).astype(bf16)
            for half in range(2):
                part = product[:, half * LANES : half * LANES + LANES]
                message[places, pl.ds((2 * pair + half) * span, span), :] = part.reshape(CHUNK // span, span, LANES)
    block_out[...] = (keeper * (own[...].astype(f32) + branch.reshape(ROWS, COLS, WIDTH))).astype(bf16)
    dnormed = dscaled * gains
    dconved = rstd * (
        dnormed - jnp.mean(dnormed, -1, keepdims=True) - normed * jnp.mean(dnormed * normed, -1, keepdims=True)
    )
    dconv[...] = dconved.astype(bf16).reshape(ROWS, COLS, WIDTH)
    grid[...] = dconved.reshape(ROWS, COLS, WIDTH)
    edges(info, grid[...], (message0, message1))
    gain_row = jnp.sum(dscaled * normed, 0, keepdims=True)
    sums[...] = jnp.zeros(sums.shape, f32)
    for half in range(WIDTH // LANES):
        lanes = pl.ds(half * LANES, LANES)
        sums[49 // 2, pl.ds(2 + half, 1), :] = gain_row[:, half * LANES : half * LANES + LANES]
        for b in range(7):
            totals = [jnp.zeros((8, LANES), f32) for _ in range(7)]
            for tile in range(COLS // 8):
                block = wide[:, pl.ds(LEFT - 3 + tile * 8 + b, 8), lanes]
                here = grid[:, pl.ds(tile * 8, 8), lanes]
                for a in range(7):
                    totals[a] = totals[a] + jnp.sum(block[a : a + ROWS] * here, 0)
            for a in range(7):
                tap = 7 * a + b
                sums[tap // 2, pl.ds(2 * (tap % 2) + half, 1), :] = jnp.sum(totals[a], 0, keepdims=True)
    message[:, pl.ds(4 * span, 16), :] = small_pack(sums[...]).astype(bf16)


def small_pack(sums):
    high = sums.astype(bf16).astype(f32)
    low = sums - high
    return jnp.concatenate([high[:, :4], low[:, :4], jnp.zeros_like(sums)], 1)


def grad_input_kernel(
    info, turn, own, side0, side1, near, far, window, extra, cot, land, taps, grad_input, wide, upstream
):
    assemble(info, turn, own, side0, side1, near, far, window, extra, wide)
    folded = info[0] == 1
    upstream[...] = keepers(land) * cot[...].astype(f32)
    for half in range(WIDTH // LANES):
        lanes = pl.ds(half * LANES, LANES)
        for tile in range(COLS // 8):
            total = upstream[:, pl.ds(tile * 8, 8), lanes]
            for b in range(7):
                block = wide[:, pl.ds(LEFT - 3 + tile * 8 + b, 8), lanes]
                for a in range(7):
                    weight = taps[6 - a, pl.ds(6 - b, 1), lanes][None]
                    if a > 3:
                        rim = jnp.where(folded, taps[a, pl.ds(b, 1), lanes][None], weight)
                        weight = jnp.concatenate(
                            [
                                jnp.broadcast_to(weight, (11 - a, 1, LANES)),
                                jnp.broadcast_to(rim, (a - 3, 1, LANES)),
                            ],
                            0,
                        )
                    total = total + block[a : a + ROWS] * weight
            grid_part = total.astype(bf16)
            grad_input[:, pl.ds(tile * 8, 8), lanes] = grid_part


def plane_kernel(received, *refs):
    message, total = refs[-2:]
    plane, lines = received.shape[0], received.shape[1] - 16
    depth = message.shape[0]
    each = lines // 4 // depth
    large = received[0, pl.ds(0, lines), :].astype(f32)
    small = received[0, pl.ds(lines, 16), :].astype(f32)
    for source in range(1, plane):
        large = large + received[source, pl.ds(0, lines), :].astype(f32)
        small = small + received[source, pl.ds(lines, 16), :].astype(f32)
    total[...] = large
    sums = small[:8]
    both = sums + jnp.concatenate([sums[4:], sums[:4]], 0)
    packed = small_pack(both[None])[0, :8]
    for place in range(depth):
        parts = [total[pl.ds(line * (lines // 4) + place * each, each), :] for line in range(4)]
        message[place] = jnp.concatenate(parts + [packed], 0).astype(bf16)


def depth_kernel(factor, received, *refs):
    first, second, message = refs[-3:]
    depth, lines = received.shape[0], received.shape[1] - 8
    total = received[0].astype(f32)
    for source in range(1, depth):
        total = total + received[source].astype(f32)
    total = total * factor
    each = lines // 4
    for half in range(2):
        lanes = pl.ds(half * LANES, LANES)
        first[:, lanes] = total[half * each : half * each + each]
        second[:, lanes] = total[(2 + half) * each : (3 + half) * each]
    sums = total[lines:]
    both = sums + jnp.concatenate([sums[4:], sums[:4]], 0)
    message[...] = jnp.broadcast_to(both[None], message.shape)


def gather_kernel(received, grad_kernel, grad_gain):
    for tap in range(50):
        for half in range(WIDTH // LANES):
            lanes = pl.ds(half * LANES, LANES)
            row = received[tap // 2, pl.ds(2 * (tap % 2) + half, 1), :]
            if tap == 49:
                grad_gain[:, lanes] = row
            else:
                grad_kernel[tap // 7, pl.ds(tap % 7, 1), lanes] = row


def run(kernel, out, scratch, scalars, *args, waits=()):
    whole = pl.BlockSpec(memory_space=pltpu.VMEM)
    specs = [pl.BlockSpec(memory_space=pltpu.SMEM)] * len(scalars) + [whole] * len(args)
    specs += [pl.BlockSpec(memory_space=pl.ANY)] * len(waits)
    call = pl.pallas_call(
        kernel,
        out_shape=out,
        in_specs=specs,
        out_specs=jax.tree.map(lambda _: whole, out),
        scratch_shapes=scratch,
        compiler_params=pltpu.CompilerParams(vmem_limit_bytes=48 * 1024 * 1024),
    )
    return call(*scalars, *args, *waits)


def swapped(value, axis, start, wrap):
    count = lax.axis_size(axis)
    pairs = [(i, (i + 1) % count) for i in range(start, count if wrap else count - 1, 2)]
    return lax.ppermute(value, axis, pairs + [(j, i) for i, j in pairs])


def fold_stage(step, lat_count, lon_count):
    pairs = [
        (((step - lon) % lon_count + 1) * lat_count - 1, (lon + 1) * lat_count - 1) for lon in range(lon_count)
    ]
    return lambda value: lax.ppermute(value, ("lon", "lat"), pairs)


def halo(info, turn, value, messages, shift, waits=()):
    sides = [swapped(message, "lon", start, True) for start, message in enumerate(messages)]
    rows = jax.ShapeDtypeStruct((3 * SPAN, WIDTH), bf16)
    near, far, window, extra = run(
        rows_kernel,
        (rows, rows, rows, jax.ShapeDtypeStruct((4 * EDGE, WIDTH), bf16)),
        [pltpu.VMEM((ROWS, COLS + 16, WIDTH), f32), pltpu.VMEM((3, 3 * COLS, WIDTH), f32)],
        (info, turn),
        value,
        *sides,
        waits=waits,
    )
    far = swapped(far, "lat", 1, False)
    near = swapped(near, "lat", 0, False)
    lat_count, lon_count = lax.axis_size("lat"), lax.axis_size("lon")
    moves = [fold_stage(FOLD * k, lat_count, lon_count) for k in range(lon_count // FOLD)]

    def branch(k, whole):
        return lambda window, extra: (moves[k](window), extra if whole else moves[k - 1](extra))

    branches = [branch(k, whole) for k in range(len(moves)) for whole in (True, False)]
    chosen = 2 * (shift // (FOLD * COLS)) + (turn[0] < BEYOND)
    return value, *sides, near, far, *lax.switch(chosen, branches, window, extra)


def layout():
    lat_count, lon_count = lax.axis_size("lat"), lax.axis_size("lon")
    high = 2 if lat_count > 2 else 1
    return (lon_count // ACROSS, ACROSS, lat_count // (2 * high), high, 2)


def device_groups():
    numbers = np.arange(math.prod(layout())).reshape(layout()).transpose(4, 2, 1, 3, 0)
    plane = math.prod(numbers.shape[:3])
    lines = numbers.reshape(plane, -1)
    return lines.T.tolist(), lines.tolist()


def spread(value, groups):
    return lax.all_to_all(value, ("lon", "lat"), 0, 0, axis_index_groups=groups, tiled=True)


def reordered(weights):
    split = weights.reshape(layout() + (-1, weights.shape[1]))
    return split.transpose(4, 2, 1, 3, 0, 5, 6).reshape(weights.shape)


def body(fields, cotangent, land_sea, partner, kernel, gain, w_in, w_out):
    shape = jax.ShapeDtypeStruct
    total_cols = COLS * lax.axis_size("lon")
    shift = (partner[0] + 3) % total_cols
    turn = (shift % (FOLD * COLS)).reshape(1)
    at_top = lax.axis_index("lat") == lax.axis_size("lat") - 1
    info = jnp.stack([at_top.astype(jnp.int32), lax.axis_index("lon") % 2, lax.axis_index("lat") % 2])
    grid_shape = shape((ROWS, COLS, WIDTH), bf16)
    side = shape((ROWS * EDGE + 3 * COLS, WIDTH), bf16)
    edge_shapes = (side, side)
    wide = pltpu.VMEM((ROWS + 6, COLS + 16, WIDTH), f32)
    grid = pltpu.VMEM((ROWS, COLS, WIDTH), f32)
    planes, lines = device_groups()
    plane, depth = len(planes[0]), len(lines[0])
    span = HIDDEN // plane
    weights = reordered(w_in), reordered(w_out)
    sent = run(edge_kernel, edge_shapes, [], (info,), fields)
    block_out, dconved, message0, message1, message = run(
        main_kernel,
        (grid_shape, grid_shape) + edge_shapes + (shape((plane, 4 * span + 16, LANES), bf16),),
        [wide, grid, pltpu.VMEM((plane, 8, LANES), f32)],
        (info, turn),
        *halo(info, turn, fields, sent, shift, weights),
        cotangent,
        land_sea,
        kernel,
        gain.reshape(1, WIDTH),
        *weights,
    )
    rims = halo(info, turn, dconved, (message0, message1), shift)
    message = run(
        plane_kernel,
        shape((depth, 4 * span // depth + 8, LANES), bf16),
        [pltpu.VMEM((4 * span, LANES), f32)],
        (),
        spread(message, planes),
        waits=rims[1:3],
    )
    factor = 1.0 / math.sqrt(CELLS * lax.axis_size("lat") * lax.axis_size("lon"))
    share = shape((span // depth, WIDTH), f32)
    grad_w_in, grad_w_out, message = run(
        functools.partial(depth_kernel, factor),
        (share, share, shape((plane, 8, LANES), f32)),
        [],
        (),
        spread(message, lines),
        waits=rims[3:],
    )
    grad_kernel, grad_gain = run(
        gather_kernel,
        (shape((7, 7, WIDTH), f32), shape((1, WIDTH), f32)),
        [],
        (),
        spread(message, planes),
    )
    grad_input = run(grad_input_kernel, grid_shape, [wide, grid], (info, turn), *rims, cotangent, land_sea, kernel)
    return block_out, grad_input, grad_w_in, grad_w_out, grad_kernel, grad_gain.reshape(WIDTH)


def solution(mesh):
    cells = P("lat", "lon", None)
    share = P(("lon", "lat"), None)
    return jax.shard_map(
        body,
        mesh=mesh,
        in_specs=(cells, cells, P("lat", "lon"), P(), P(), P(), P(), P()),
        out_specs=(cells, cells, share, share, P(), P()),
        check_vma=False,
    )
```

time: 179 us -> 125 us (0.70)
  starting transfers between devices: 124 us -> 84.5 us
  waiting for transfers between devices: 27.1 us -> 15 us
  local copies, waits for them, and re-layouts: 11.1 us -> 5.4 us
  Pallas kernels: 13.2 us -> 17.1 us
    ppermute x30 -> x10, starting transfers between devices: 124 us -> 62.1 us  [the longest x8 59.5 us: swapped(): return lax.ppermute(value, axis, pairs + [(j, i) for i, j in pairs])]
    all_to_all x0 -> x3, starting transfers between devices: none -> 22.4 us  [spread(): lax.all_to_all(value, ('lon', 'lat'), 0, 0, axis_index_groups=groups, til...]
    ppermute x30 -> x10, waiting for transfers between devices: 27.1 us -> 10.5 us  [the longest x8 10.4 us: swapped(): return lax.ppermute(value, axis, pairs + [(j, i) for i, j in pairs])]
    all_to_all x0 -> x3, waiting for transfers between devices: none -> 4.58 us  [spread(): lax.all_to_all(value, ('lon', 'lat'), 0, 0, axis_index_groups=groups, til...]
    cond x4 -> x0, local copies, waits for them, and re-layouts: 4.06 us -> none
    pallas_call x8, Pallas kernels: 13.2 us -> 17.1 us  [run(): return call(*scalars, *args, *waits)]
  transfers between devices with their start and end apart: 30 -> 13, of which waited for: 7 -> 6; matrix products, arithmetic and copies ran while one was open for 5% -> 3% of each run, Pallas kernels for 3% -> 4%
where the time goes in v2:
time: 125 us; the launch traced here: 124 us
  starting transfers between devices  84.5 us (68%)
  Pallas kernels  17.1 us (14%)
  waiting for transfers between devices  15 us (12%)
  local copies, waits for them, and re-layouts  5.4 us (4%)
  between operations  1.61 us (1%)
    ppermute x8, starting transfers between devices, swapped(): return lax.ppermute(value, axis, pairs + [(j, i) for i, j in pairs])  59.5 us
    all_to_all x3, starting transfers between devices, spread(): lax.all_to_all(value, ('lon', 'lat'), 0, 0, axis_index_groups=groups, til...  22.4 us
    pallas_call x8, Pallas kernels, run(): return call(*scalars, *args, *waits)  17.1 us
    ppermute x8, waiting for transfers between devices, swapped(): return lax.ppermute(value, axis, pairs + [(j, i) for i, j in pairs])  10.4 us
    all_to_all x3, waiting for transfers between devices, spread(): lax.all_to_all(value, ('lon', 'lat'), 0, 0, axis_index_groups=groups, til...  4.58 us
    ppermute x2, starting transfers between devices, fold_stage(): return lambda value: lax.ppermute(value, ('lon', 'lat'), pairs)  2.58 us
    reshape x4, local copies, waits for them, and re-layouts, reordered(): split = weights.reshape(layout() + (-1, weights.shape[1]))  2.51 us
  transfers between devices with their start and end apart: 13, of which 6 were waited for; matrix products, arithmetic and copies ran while one was open for 3% of the time, Pallas kernels for 4%

profile of v2, /device:TPU:1, one launch (start us, length us, event | category | flops | bytes accessed | tf_op | source)
XLA Modules:
  0.0 123.8 jit_solution(13305246217739824213)
XLA Ops:
  0.7 0.1 pad_add_fusion.info
  0.7 0.9 copy-done
  1.6 0.6 shard_map.127
  2.2 3.9 %collective-permute-start.96 = (bf16[160,256]{1,0:T(8,128)(2,1)S(1)}, bf16[160,256]{1,0:T(8,128)(2,1)S(1)}, u32[]{:S(2)}, u32[]{:S(2)}) collective-permute-start(bf16[160,256]{1,0:T(8,128)(2,1)S(1)} %get-tuple-element.414), channel_id=1, source_target_pairs={{0,16},{32,48},{64,80},{96,112},{128,144},{160,176},{192,208},{224... | collective-permute-start | bytes 245768 | tf_op jit(solution)/shard_map/ppermute | solution.py:290
  6.2 14.4 %collective-permute-start.97 = (bf16[160,256]{1,0:T(8,128)(2,1)S(1)}, bf16[160,256]{1,0:T(8,128)(2,1)S(1)}, u32[]{:S(2)}, u32[]{:S(2)}) collective-permute-start(bf16[160,256]{1,0:T(8,128)(2,1)S(1)} %get-tuple-element.415), channel_id=1, source_target_pairs={{16,32},{48,64},{80,96},{112,128},{144,160},{176,192},{208,224},{2... | collective-permute-start | bytes 245768 | tf_op jit(solution)/shard_map/ppermute | solution.py:290
  20.6 1.2 slice.3
  22.5 1.2 %reshape.36 = bf16[8,4,4,2,2,2,256]{6,5,4,3,2,1,0:T(2,128)(2,1)S(1)} reshape(bf16[1024,256]{1,0:T(8,128)(2,1)} %param.78) | data formatting | bytes 1048576 | tf_op jit(solution)/shard_map/reshape | solution.py:343
  23.7 0.0 copy-start.6
  23.7 0.5 copy.19
  24.3 0.2 reshape.37.refs_0_.w_in
  24.5 0.3 copy-done.6
  24.7 0.2 reshape.38
  24.9 0.0 copy-start.1
  25.0 0.5 copy.18
  25.5 0.2 reshape.39.refs_1_.w_out
  25.7 0.0 copy-start.2
  25.7 0.0 copy-start.3
  25.7 0.0 copy-start.4
  25.8 0.0 copy-start.5
  25.8 0.1 copy-done.1
  25.9 0.6 shard_map.128
  26.5 3.1 %collective-permute-start.98 = (bf16[120,256]{1,0:T(8,128)(2,1)S(1)}, bf16[120,256]{1,0:T(8,128)(2,1)S(1)}, u32[]{:S(2)}, u32[]{:S(2)}) collective-permute-start(bf16[120,256]{1,0:T(8,128)(2,1)S(1)} %get-tuple-element.416), channel_id=1, source_target_pairs={{0,1},{2,3},{4,5},{6,7},{8,9},{10,11},{12,13},{14,15},{1,0},{3,2},... | collective-permute-start | bytes 184328 | tf_op jit(solution)/shard_map/ppermute | solution.py:290
  29.6 10.4 %collective-permute-start.99 = (bf16[120,256]{1,0:T(8,128)(2,1)S(1)}, bf16[120,256]{1,0:T(8,128)(2,1)S(1)}, u32[]{:S(2)}, u32[]{:S(2)}) collective-permute-start(bf16[120,256]{1,0:T(8,128)(2,1)S(1)} %get-tuple-element.417), channel_id=1, source_target_pairs={{1,2},{3,4},{5,6},{7,8},{9,10},{11,12},{13,14},{2,1},{4,3},{6,5},{... | collective-permute-start | bytes 184328 | tf_op jit(solution)/shard_map/ppermute | solution.py:290
  40.1 1.3 %conditional.2 = (bf16[120,256]{1,0:T(8,128)(2,1)}, bf16[32,256]{1,0:T(8,128)(2,1)S(1)}) conditional(s32[]{:T(128)} %clamp.4, (bf16[120,256]{1,0:T(8,128)(2,1)S(1)}, bf16[32,256]{1,0:T(8,128)(2,1)S(1)}) %tuple.264, (bf16[120,256]{1,0:T(8,128)(2,1)S(1)}, bf16[32,256]{1,0:T(8,128)(2,1)S(1)}) %tuple.264, ...), branch_computations={%region_0.1_spmd, %region_1.2_spmd, %region_2.3_spmd, %region_3.4_... | conditional | bytes 344160 | solution.py:322
  40.1 1.3 %collective-permute-start.39 = (bf16[120,256]{1,0:T(8,128)(2,1)S(1)}, bf16[120,256]{1,0:T(8,128)(2,1)}, u32[]{:S(2)}, u32[]{:S(2)}) collective-permute-start(bf16[120,256]{1,0:T(8,128)(2,1)S(1)} %get-tuple-element.308), channel_id=1, source_target_pairs={{431,15},{415,31},{399,47},{383,63},{367,79},{351,95},{335,111},{3... | collective-permute-start | bytes 184328 | tf_op jit(solution)/shard_map/cond/branch_26_fun/ppermute | solution.py:297
  41.4 0.0 collective-permute-done.39
  41.4 4.1 %collective-permute-done.99.far = bf16[120,256]{1,0:T(8,128)(2,1)S(1)} collective-permute-done((bf16[120,256]{1,0:T(8,128)(2,1)S(1)}, bf16[120,256]{1,0:T(8,128)(2,1)S(1)}, u32[]{:S(2)}, u32[]{:S(2)}) %collective-permute-start.99) | collective-permute-done | bytes 61472 | tf_op jit(solution)/shard_map/ppermute | solution.py:290
  45.5 9.2 %shard_map.129 = (bf16[8,32,256]{2,1,0:T(8,128)(2,1)}, bf16[8,32,256]{2,1,0:T(8,128)(2,1)S(1)}, bf16[160,256]{1,0:T(8,128)(2,1)S(1)}, bf16[160,256]{1,0:T(8,128)(2,1)S(1)}, bf16[32,144,128]{2,1,0:T(8,128)(2,1)}) custom-call(s32[3]{0:T(128)S(1)} %pad_add_fusion.info, s32[1]{0:T(128)} %bitcast.4.turn, bf16[8,32,256]{2,1,0:T(8,128)(2,1)S(1)} %copy-done.1, ...), custom_call_target="tpu_custom_call" | custom-call | tf_op jit(solution)/shard_map/pallas_call | solution.py:284
  54.7 7.0 %all-to-all-start = ((bf16[32,144,128]{2,1,0:T(8,128)(2,1)}), bf16[32,144,128]{2,1,0:T(8,128)(2,1)S(1)}, u32[]{:S(2)}, u32[]{:S(2)}) async-start(bf16[32,144,128]{2,1,0:T(8,128)(2,1)} %get-tuple-element.432), calls=%async_computation | async-start | bytes 2359296 | tf_op jit(solution)/shard_map/all_to_all | solution.py:339
  61.7 3.3 %collective-permute-start.100 = (bf16[160,256]{1,0:T(8,128)(2,1)S(1)}, bf16[160,256]{1,0:T(8,128)(2,1)S(1)}, u32[]{:S(2)}, u32[]{:S(2)}) collective-permute-start(bf16[160,256]{1,0:T(8,128)(2,1)S(1)} %get-tuple-element.424), channel_id=1, source_target_pairs={{0,16},{32,48},{64,80},{96,112},{128,144},{160,176},{192,208},{224... | collective-permute-start | bytes 245768 | tf_op jit(solution)/shard_map/ppermute | solution.py:290
  65.0 8.8 %collective-permute-start.101 = (bf16[160,256]{1,0:T(8,128)(2,1)S(1)}, bf16[160,256]{1,0:T(8,128)(2,1)S(1)}, u32[]{:S(2)}, u32[]{:S(2)}) collective-permute-start(bf16[160,256]{1,0:T(8,128)(2,1)S(1)} %get-tuple-element.425), channel_id=1, source_target_pairs={{16,32},{48,64},{80,96},{112,128},{144,160},{176,192},{208,224},{2... | collective-permute-start | bytes 245768 | tf_op jit(solution)/shard_map/ppermute | solution.py:290
  73.9 4.5 %collective-permute-done.100.side0.refs_0_ = bf16[160,256]{1,0:T(8,128)(2,1)S(1)} collective-permute-done((bf16[160,256]{1,0:T(8,128)(2,1)S(1)}, bf16[160,256]{1,0:T(8,128)(2,1)S(1)}, u32[]{:S(2)}, u32[]{:S(2)}) %collective-permute-start.100) | collective-permute-done | bytes 81952 | tf_op jit(solution)/shard_map/ppermute | solution.py:290
  78.4 0.6 collective-permute-done.101.side1.refs_1_
  78.9 1.0 all-to-all-done.received
  79.9 0.8 shard_map.132
  80.7 8.7 %all-to-all-start.1 = ((bf16[16,16,128]{2,1,0:T(8,128)(2,1)}), bf16[16,16,128]{2,1,0:T(8,128)(2,1)S(1)}, u32[]{:S(2)}, u32[]{:S(2)}) async-start(bf16[16,16,128]{2,1,0:T(8,128)(2,1)} %shard_map.132), calls=%async_computation.1 | async-start | bytes 131072 | tf_op jit(solution)/shard_map/all_to_all | solution.py:339
  89.3 0.6 shard_map.130
  90.0 3.3 %collective-permute-start.102 = (bf16[120,256]{1,0:T(8,128)(2,1)S(1)}, bf16[120,256]{1,0:T(8,128)(2,1)S(1)}, u32[]{:S(2)}, u32[]{:S(2)}) collective-permute-start(bf16[120,256]{1,0:T(8,128)(2,1)S(1)} %get-tuple-element.426), channel_id=1, source_target_pairs={{0,1},{2,3},{4,5},{6,7},{8,9},{10,11},{12,13},{14,15},{1,0},{3,2},... | collective-permute-start | bytes 184328 | tf_op jit(solution)/shard_map/ppermute | solution.py:290
  93.3 12.2 %collective-permute-start.103 = (bf16[120,256]{1,0:T(8,128)(2,1)S(1)}, bf16[120,256]{1,0:T(8,128)(2,1)S(1)}, u32[]{:S(2)}, u32[]{:S(2)}) collective-permute-start(bf16[120,256]{1,0:T(8,128)(2,1)S(1)} %get-tuple-element.427), channel_id=1, source_target_pairs={{1,2},{3,4},{5,6},{7,8},{9,10},{11,12},{13,14},{2,1},{4,3},{6,5},{... | collective-permute-start | bytes 184328 | tf_op jit(solution)/shard_map/ppermute | solution.py:290
  105.5 1.3 %conditional.3 = (bf16[120,256]{1,0:T(8,128)(2,1)}, bf16[32,256]{1,0:T(8,128)(2,1)S(1)}) conditional(s32[]{:T(128)} %clamp.4, (bf16[120,256]{1,0:T(8,128)(2,1)S(1)}, bf16[32,256]{1,0:T(8,128)(2,1)S(1)}) %tuple.265, (bf16[120,256]{1,0:T(8,128)(2,1)S(1)}, bf16[32,256]{1,0:T(8,128)(2,1)S(1)}) %tuple.265, ...), branch_computations={%region_32.33_spmd, %region_33.34_spmd, %region_34.35_spmd, %regio... | conditional | bytes 344160 | solution.py:322
  105.5 1.3 %collective-permute-start.87 = (bf16[120,256]{1,0:T(8,128)(2,1)S(1)}, bf16[120,256]{1,0:T(8,128)(2,1)}, u32[]{:S(2)}, u32[]{:S(2)}) collective-permute-start(bf16[120,256]{1,0:T(8,128)(2,1)S(1)} %get-tuple-element.372), channel_id=1, source_target_pairs={{431,15},{415,31},{399,47},{383,63},{367,79},{351,95},{335,111},{3... | collective-permute-start | bytes 184328 | tf_op jit(solution)/shard_map/cond/branch_26_fun/ppermute | solution.py:297
  106.8 0.0 collective-permute-done.102.near.refs_0_
  106.8 1.3 %collective-permute-done.103.far.refs_1_ = bf16[120,256]{1,0:T(8,128)(2,1)S(1)} collective-permute-done((bf16[120,256]{1,0:T(8,128)(2,1)S(1)}, bf16[120,256]{1,0:T(8,128)(2,1)S(1)}, u32[]{:S(2)}, u32[]{:S(2)}) %collective-permute-start.103) | collective-permute-done | bytes 61472 | tf_op jit(solution)/shard_map/ppermute | solution.py:290
  108.1 0.7 shard_map.133
  108.8 6.8 %all-to-all-start.2 = ((f32[32,8,128]{2,1,0:T(8,128)}), f32[32,8,128]{2,1,0:T(8,128)S(1)}, u32[]{:S(2)}, u32[]{:S(2)}) async-start(f32[32,8,128]{2,1,0:T(8,128)} %get-tuple-element.435), calls=%async_computation.2 | async-start | bytes 262144 | tf_op jit(solution)/shard_map/all_to_all | solution.py:339
  115.6 3.9 %shard_map.131 = bf16[8,32,256]{2,1,0:T(8,128)(2,1)} custom-call(s32[3]{0:T(128)S(1)} %pad_add_fusion.info, s32[1]{0:T(128)} %bitcast.4.turn, bf16[8,32,256]{2,1,0:T(8,128)(2,1)S(1)} %get-tuple-element.423.own, bf16[160,256]{1,0:T(8,128)(2,1)S(1)} %collective-permute-done.100.side0.refs_0_, bf16[160,256]{1,0:T(8,128)(2,1)S(1)} %collective-permute-done.101.side1.refs_1_, ...), custom_call_target="tpu_custom_call" | custom-call | tf_op jit(solution)/shard_map/pallas_call | solution.py:284
  119.6 3.6 %all-to-all-done.2.received = f32[32,8,128]{2,1,0:T(8,128)S(1)} async-done(((f32[32,8,128]{2,1,0:T(8,128)}), f32[32,8,128]{2,1,0:T(8,128)S(1)}, u32[]{:S(2)}, u32[]{:S(2)}) %all-to-all-start.2) | async-done | bytes 131104 | tf_op jit(solution)/shard_map/all_to_all | solution.py:339
  123.2 0.7 shard_map.134
  (10 shorter events, 0.0 us)
Async XLA Ops:
  0.7 0.9 copy-start
  2.2 23.6 %collective-permute-start.96 = (bf16[160,256]{1,0:T(8,128)(2,1)S(1)}, bf16[160,256]{1,0:T(8,128)(2,1)S(1)}, u32[]{:S(2)}, u32[]{:S(2)}) collective-permute-start(bf16[160,256]{1,0:T(8,128)(2,1)S(1)} %get-tuple-element.414), channel_id=1, source_target_pairs={{0,16},{32,48},{64,80},{96,112},{128,144},{160,176},{192,208},{224... | collective-permute-start | bytes 245768 | tf_op jit(solution)/shard_map/ppermute | solution.py:290
  6.2 19.6 %collective-permute-start.97 = (bf16[160,256]{1,0:T(8,128)(2,1)S(1)}, bf16[160,256]{1,0:T(8,128)(2,1)S(1)}, u32[]{:S(2)}, u32[]{:S(2)}) collective-permute-start(bf16[160,256]{1,0:T(8,128)(2,1)S(1)} %get-tuple-element.415), channel_id=1, source_target_pairs={{16,32},{48,64},{80,96},{112,128},{144,160},{176,192},{208,224},{2... | collective-permute-start | bytes 245768 | tf_op jit(solution)/shard_map/ppermute | solution.py:290
  23.7 1.0 copy-start.6
  24.9 0.9 copy-start.1
  25.7 19.8 %copy-start.2 = (bf16[8,32,256]{2,1,0:T(8,128)(2,1)S(1)}, bf16[8,32,256]{2,1,0:T(8,128)(2,1)}, u32[]{:S(2)}) copy-start(bf16[8,32,256]{2,1,0:T(8,128)(2,1)} %cot.3) | copy-start | bytes 393220
  25.7 19.8 %copy-start.3 = (f32[7,7,256]{2,1,0:T(8,128)S(1)}, f32[7,7,256]{2,1,0:T(8,128)}, u32[]{:S(2)}) copy-start(f32[7,7,256]{2,1,0:T(8,128)} %taps.3) | copy-start | bytes 150532
  25.7 19.8 %copy-start.4 = (s32[8,32]{1,0:T(8,128)S(1)}, s32[8,32]{1,0:T(8,128)}, u32[]{:S(2)}) copy-start(s32[8,32]{1,0:T(8,128)} %land.3) | copy-start | bytes 3076
  25.8 19.8 %copy-start.5 = (f32[256]{0:T(256)S(1)}, f32[256]{0:T(256)}, u32[]{:S(2)}) copy-start(f32[256]{0:T(256)} %param.77) | copy-start | bytes 3076
  26.5 15.0 %collective-permute-start.98 = (bf16[120,256]{1,0:T(8,128)(2,1)S(1)}, bf16[120,256]{1,0:T(8,128)(2,1)S(1)}, u32[]{:S(2)}, u32[]{:S(2)}) collective-permute-start(bf16[120,256]{1,0:T(8,128)(2,1)S(1)} %get-tuple-element.416), channel_id=1, source_target_pairs={{0,1},{2,3},{4,5},{6,7},{8,9},{10,11},{12,13},{14,15},{1,0},{3,2},... | collective-permute-start | bytes 184328 | tf_op jit(solution)/shard_map/ppermute | solution.py:290
  29.6 15.9 %collective-permute-start.99 = (bf16[120,256]{1,0:T(8,128)(2,1)S(1)}, bf16[120,256]{1,0:T(8,128)(2,1)S(1)}, u32[]{:S(2)}, u32[]{:S(2)}) collective-permute-start(bf16[120,256]{1,0:T(8,128)(2,1)S(1)} %get-tuple-element.417), channel_id=1, source_target_pairs={{1,2},{3,4},{5,6},{7,8},{9,10},{11,12},{13,14},{2,1},{4,3},{6,5},{... | collective-permute-start | bytes 184328 | tf_op jit(solution)/shard_map/ppermute | solution.py:290
  40.1 1.3 %collective-permute-start.39 = (bf16[120,256]{1,0:T(8,128)(2,1)S(1)}, bf16[120,256]{1,0:T(8,128)(2,1)}, u32[]{:S(2)}, u32[]{:S(2)}) collective-permute-start(bf16[120,256]{1,0:T(8,128)(2,1)S(1)} %get-tuple-element.308), channel_id=1, source_target_pairs={{431,15},{415,31},{399,47},{383,63},{367,79},{351,95},{335,111},{3... | collective-permute-start | bytes 184328 | tf_op jit(solution)/shard_map/cond/branch_26_fun/ppermute | solution.py:297
  54.7 25.1 %all-to-all-start = ((bf16[32,144,128]{2,1,0:T(8,128)(2,1)}), bf16[32,144,128]{2,1,0:T(8,128)(2,1)S(1)}, u32[]{:S(2)}, u32[]{:S(2)}) async-start(bf16[32,144,128]{2,1,0:T(8,128)(2,1)} %get-tuple-element.432), calls=%async_computation | async-start | bytes 2359296 | tf_op jit(solution)/shard_map/all_to_all | solution.py:339
  61.7 16.6 %collective-permute-start.100 = (bf16[160,256]{1,0:T(8,128)(2,1)S(1)}, bf16[160,256]{1,0:T(8,128)(2,1)S(1)}, u32[]{:S(2)}, u32[]{:S(2)}) collective-permute-start(bf16[160,256]{1,0:T(8,128)(2,1)S(1)} %get-tuple-element.424), channel_id=1, source_target_pairs={{0,16},{32,48},{64,80},{96,112},{128,144},{160,176},{192,208},{224... | collective-permute-start | bytes 245768 | tf_op jit(solution)/shard_map/ppermute | solution.py:290
  65.0 13.9 %collective-permute-start.101 = (bf16[160,256]{1,0:T(8,128)(2,1)S(1)}, bf16[160,256]{1,0:T(8,128)(2,1)S(1)}, u32[]{:S(2)}, u32[]{:S(2)}) collective-permute-start(bf16[160,256]{1,0:T(8,128)(2,1)S(1)} %get-tuple-element.425), channel_id=1, source_target_pairs={{16,32},{48,64},{80,96},{112,128},{144,160},{176,192},{208,224},{2... | collective-permute-start | bytes 245768 | tf_op jit(solution)/shard_map/ppermute | solution.py:290
  80.7 27.5 %all-to-all-start.1 = ((bf16[16,16,128]{2,1,0:T(8,128)(2,1)}), bf16[16,16,128]{2,1,0:T(8,128)(2,1)S(1)}, u32[]{:S(2)}, u32[]{:S(2)}) async-start(bf16[16,16,128]{2,1,0:T(8,128)(2,1)} %shard_map.132), calls=%async_computation.1 | async-start | bytes 131072 | tf_op jit(solution)/shard_map/all_to_all | solution.py:339
  90.0 16.9 %collective-permute-start.102 = (bf16[120,256]{1,0:T(8,128)(2,1)S(1)}, bf16[120,256]{1,0:T(8,128)(2,1)S(1)}, u32[]{:S(2)}, u32[]{:S(2)}) collective-permute-start(bf16[120,256]{1,0:T(8,128)(2,1)S(1)} %get-tuple-element.426), channel_id=1, source_target_pairs={{0,1},{2,3},{4,5},{6,7},{8,9},{10,11},{12,13},{14,15},{1,0},{3,2},... | collective-permute-start | bytes 184328 | tf_op jit(solution)/shard_map/ppermute | solution.py:290
  93.3 14.8 %collective-permute-start.103 = (bf16[120,256]{1,0:T(8,128)(2,1)S(1)}, bf16[120,256]{1,0:T(8,128)(2,1)S(1)}, u32[]{:S(2)}, u32[]{:S(2)}) collective-permute-start(bf16[120,256]{1,0:T(8,128)(2,1)S(1)} %get-tuple-element.427), channel_id=1, source_target_pairs={{1,2},{3,4},{5,6},{7,8},{9,10},{11,12},{13,14},{2,1},{4,3},{6,5},{... | collective-permute-start | bytes 184328 | tf_op jit(solution)/shard_map/ppermute | solution.py:290
  105.5 1.3 %collective-permute-start.87 = (bf16[120,256]{1,0:T(8,128)(2,1)S(1)}, bf16[120,256]{1,0:T(8,128)(2,1)}, u32[]{:S(2)}, u32[]{:S(2)}) collective-permute-start(bf16[120,256]{1,0:T(8,128)(2,1)S(1)} %get-tuple-element.372), channel_id=1, source_target_pairs={{431,15},{415,31},{399,47},{383,63},{367,79},{351,95},{335,111},{3... | collective-permute-start | bytes 184328 | tf_op jit(solution)/shard_map/cond/branch_26_fun/ppermute | solution.py:297
  108.8 14.3 %all-to-all-start.2 = ((f32[32,8,128]{2,1,0:T(8,128)}), f32[32,8,128]{2,1,0:T(8,128)S(1)}, u32[]{:S(2)}, u32[]{:S(2)}) async-start(f32[32,8,128]{2,1,0:T(8,128)} %get-tuple-element.435), calls=%async_computation.2 | async-start | bytes 262144 | tf_op jit(solution)/shard_map/all_to_all | solution.py:339

commit v3 on v2

--- a/solution.py
+++ b/solution.py
@@ -29,6 +29,11 @@
     return lax.dot_general(left, right, (dims, ((), ())), preferred_element_type=f32)
 
 
+def put(wide, rows, columns, value):
+    for half in range(WIDTH // LANES):
+        wide[half, rows, columns, :] = value[..., half * LANES : half * LANES + LANES]
+
+
 def edges(info, grid, messages):
     block = grid[ROWS - 3 :].reshape(3 * COLS, WIDTH).astype(bf16)
     left, right = [
@@ -45,7 +50,7 @@
 
 
 def middle(info, wide, first, own, sides):
-    wide[pl.ds(first, ROWS), pl.ds(LEFT, COLS), :] = own[...].astype(f32)
+    put(wide, pl.ds(first, ROWS), pl.ds(LEFT, COLS), own[...].astype(f32))
     margin = pl.ds(0, ROWS * EDGE)
     for parity, starts in enumerate(((LEFT + COLS, 0), (0, LEFT + COLS))):
 
@@ -53,11 +58,11 @@
         def _():
             for start, side in zip(starts, sides):
                 part = side[margin, :].astype(f32).reshape(ROWS, EDGE, WIDTH)
-                wide[pl.ds(first, ROWS), pl.ds(start, EDGE), :] = part
-
-
-def rows_kernel(info, turn, own, side0, side1, *refs):
-    near, far, window, extra, wide, line = refs[-6:]
+                put(wide, pl.ds(first, ROWS), pl.ds(start, EDGE), part)
+
+
+def rows_kernel(info, turn, own, side1, side0, *refs):
+    near, far, window, extra, wide, line, strip = refs[-7:]
     middle(info, wide, 0, own, (side0, side1))
     columns = pl.ds(LEFT - 3, SPAN)
     for parity, order in enumerate(((near, far), (far, near))):
@@ -65,7 +70,9 @@
         @pl.when(info[2] == parity)
         def _():
             for message, start in zip(order, (ROWS - 3, 0)):
-                message[...] = wide[pl.ds(start, 3), columns, :].reshape(3 * SPAN, WIDTH).astype(bf16)
+                for half in range(WIDTH // LANES):
+                    part = wide[half, pl.ds(start, 3), columns, :].reshape(3 * SPAN, LANES)
+                    message[:, pl.ds(half * LANES, LANES)] = part.astype(bf16)
 
     @pl.when(info[0] == 1)
     def _():
@@ -81,16 +88,16 @@
         for column in range(COLS + 6):
             source = jnp.maximum(COLS + turn[0] - column, 0)
             for row in range(3):
-                wide[row, pl.ds(column, 1), :] = line[2 - row, pl.ds(source, 1), :]
+                strip[row, pl.ds(column, 1), :] = line[2 - row, pl.ds(source, 1), :]
             if column > COLS:
                 source = jnp.minimum((FOLD + 1) * COLS + turn[0] - column, 3 * COLS - 1)
                 for row in range(3):
-                    wide[3 + row, pl.ds(column - COLS - 1, 1), :] = line[2 - row, pl.ds(source, 1), :]
-        extra[pl.ds(0, 3 * EDGE), :] = wide[pl.ds(3, 3), pl.ds(0, EDGE), :].reshape(3 * EDGE, WIDTH).astype(bf16)
-        window[...] = wide[pl.ds(0, 3), pl.ds(0, SPAN), :].reshape(3 * SPAN, WIDTH).astype(bf16)
-
-
-def assemble(info, turn, own, side0, side1, near, far, window, extra, wide):
+                    strip[3 + row, pl.ds(column - COLS - 1, 1), :] = line[2 - row, pl.ds(source, 1), :]
+        extra[pl.ds(0, 3 * EDGE), :] = strip[pl.ds(3, 3), pl.ds(0, EDGE), :].reshape(3 * EDGE, WIDTH).astype(bf16)
+        window[...] = strip[pl.ds(0, 3), :, :].reshape(3 * SPAN, WIDTH).astype(bf16)
+
+
+def assemble(info, turn, own, side1, side0, far, near, window, extra, wide):
     middle(info, wide, 3, own, (side0, side1))
     columns = pl.ds(LEFT - 3, SPAN)
     for parity, (below, above) in enumerate(((far, near), (near, far))):
@@ -98,18 +105,18 @@
         @pl.when(info[2] == parity)
         def _():
             for part, start in ((below, 0), (above, ROWS + 3)):
-                wide[pl.ds(start, 3), columns, :] = part[...].astype(f32).reshape(3, SPAN, WIDTH)
+                put(wide, pl.ds(start, 3), columns, part[...].astype(f32).reshape(3, SPAN, WIDTH))
 
     @pl.when(info[0] == 1)
     def _():
-        wide[pl.ds(ROWS + 3, 3), columns, :] = window[...].astype(f32).reshape(3, SPAN, WIDTH)
+        put(wide, pl.ds(ROWS + 3, 3), columns, window[...].astype(f32).reshape(3, SPAN, WIDTH))
         rest = extra[pl.ds(0, 3 * EDGE), :].astype(f32).reshape(3, EDGE, WIDTH)
         for place in range(BEYOND):
             column = COLS + 1 + place
 
             @pl.when(turn[0] - column < -COLS)
             def _():
-                wide[pl.ds(ROWS + 3, 3), pl.ds(LEFT - 3 + column, 1), :] = rest[:, place : place + 1]
+                put(wide, pl.ds(ROWS + 3, 3), pl.ds(LEFT - 3 + column, 1), rest[:, place : place + 1])
 
 
 def keepers(land):
@@ -119,16 +126,16 @@
 
 
 def main_kernel(
-    info, turn, own, side0, side1, near, far, window, extra, cot, land, taps, gain, w_in, w_out,
+    info, turn, own, side1, side0, far, near, window, extra, cot, land, taps, gain, w_in, w_out,
     block_out, dconv, message0, message1, message, wide, grid, sums,
 ):
-    assemble(info, turn, own, side0, side1, near, far, window, extra, wide)
+    assemble(info, turn, own, side1, side0, far, near, window, extra, wide)
     for half in range(WIDTH // LANES):
         lanes = pl.ds(half * LANES, LANES)
         for tile in range(COLS // 8):
             total = jnp.zeros((ROWS, 8, LANES), f32)
             for b in range(7):
-                block = wide[:, pl.ds(LEFT - 3 + tile * 8 + b, 8), lanes]
+                block = wide[half, :, pl.ds(LEFT - 3 + tile * 8 + b, 8), :]
                 for a in range(7):
                     total = total + block[a : a + ROWS] * taps[a, pl.ds(b, 1), lanes][None]
             grid[:, pl.ds(tile * 8, 8), lanes] = total
@@ -178,7 +185,7 @@
         for b in range(7):
             totals = [jnp.zeros((8, LANES), f32) for _ in range(7)]
             for tile in range(COLS // 8):
-                block = wide[:, pl.ds(LEFT - 3 + tile * 8 + b, 8), lanes]
+                block = wide[half, :, pl.ds(LEFT - 3 + tile * 8 + b, 8), :]
                 here = grid[:, pl.ds(tile * 8, 8), lanes]
                 for a in range(7):
                     totals[a] = totals[a] + jnp.sum(block[a : a + ROWS] * here, 0)
@@ -195,9 +202,9 @@
 
 
 def grad_input_kernel(
-    info, turn, own, side0, side1, near, far, window, extra, cot, land, taps, grad_input, wide, upstream
+    info, turn, own, side1, side0, far, near, window, extra, cot, land, taps, grad_input, wide, upstream
 ):
-    assemble(info, turn, own, side0, side1, near, far, window, extra, wide)
+    assemble(info, turn, own, side1, side0, far, near, window, extra, wide)
     folded = info[0] == 1
     upstream[...] = keepers(land) * cot[...].astype(f32)
     for half in range(WIDTH // LANES):
@@ -205,7 +212,7 @@
         for tile in range(COLS // 8):
             total = upstream[:, pl.ds(tile * 8, 8), lanes]
             for b in range(7):
-                block = wide[:, pl.ds(LEFT - 3 + tile * 8 + b, 8), lanes]
+                block = wide[half, :, pl.ds(LEFT - 3 + tile * 8 + b, 8), :]
                 for a in range(7):
                     weight = taps[6 - a, pl.ds(6 - b, 1), lanes][None]
                     if a > 3:
@@ -298,12 +305,16 @@
 
 
 def halo(info, turn, value, messages, shift, waits=()):
-    sides = [swapped(message, "lon", start, True) for start, message in enumerate(messages)]
+    sides = [swapped(messages[start], "lon", start, True) for start in (1, 0)]
     rows = jax.ShapeDtypeStruct((3 * SPAN, WIDTH), bf16)
     near, far, window, extra = run(
         rows_kernel,
         (rows, rows, rows, jax.ShapeDtypeStruct((4 * EDGE, WIDTH), bf16)),
-        [pltpu.VMEM((ROWS, COLS + 16, WIDTH), f32), pltpu.VMEM((3, 3 * COLS, WIDTH), f32)],
+        [
+            pltpu.VMEM((WIDTH // LANES, ROWS, COLS + 16, LANES), f32),
+            pltpu.VMEM((3, 3 * COLS, WIDTH), f32),
+            pltpu.VMEM((6, SPAN, WIDTH), f32),
+        ],
         (info, turn),
         value,
         *sides,
@@ -319,7 +330,7 @@
 
     branches = [branch(k, whole) for k in range(len(moves)) for whole in (True, False)]
     chosen = 2 * (shift // (FOLD * COLS)) + (turn[0] < BEYOND)
-    return value, *sides, near, far, *lax.switch(chosen, branches, window, extra)
+    return value, *sides, far, near, *lax.switch(chosen, branches, window, extra)
 
 
 def layout():
@@ -354,7 +365,7 @@
     grid_shape = shape((ROWS, COLS, WIDTH), bf16)
     side = shape((ROWS * EDGE + 3 * COLS, WIDTH), bf16)
     edge_shapes = (side, side)
-    wide = pltpu.VMEM((ROWS + 6, COLS + 16, WIDTH), f32)
+    wide = pltpu.VMEM((WIDTH // LANES, ROWS + 6, COLS + 16, LANES), f32)
     grid = pltpu.VMEM((ROWS, COLS, WIDTH), f32)
     planes, lines = device_groups()
     plane, depth = len(planes[0]), len(lines[0])

time: 125 us -> 117 us (0.936); the launches traced: 124 us -> 118 us
  starting transfers between devices: 84.5 us -> 80.1 us
  Pallas kernels: 17.1 us -> 13.3 us
  waiting for transfers between devices: 15 us -> 17.2 us
    ppermute x8, starting transfers between devices: 59.5 us -> 54 us  [swapped(): return lax.ppermute(value, axis, pairs + [(j, i) for i, j in pairs])]
    pallas_call x8, Pallas kernels: 17.1 us -> 13.3 us  [run(): return call(*scalars, *args, *waits)]
    all_to_all x3, waiting for transfers between devices: 4.58 us -> 8.32 us  [spread(): lax.all_to_all(value, ('lon', 'lat'), 0, 0, axis_index_groups=groups, til...]
    ppermute x8, waiting for transfers between devices: 10.4 us -> 8.89 us  [swapped(): return lax.ppermute(value, axis, pairs + [(j, i) for i, j in pairs])]
  transfers between devices with their start and end apart: 13 -> 13, of which waited for: 6 -> 5; matrix products, arithmetic and copies ran while one was open for 3% -> 3% of each run, Pallas kernels for 4% -> 3%
where the time goes in v3:
time: 117 us; the launch traced here: 118 us
  starting transfers between devices  80.1 us (68%)
  waiting for transfers between devices  17.2 us (15%)
  Pallas kernels  13.3 us (11%)
  local copies, waits for them, and re-layouts  5.4 us (5%)
  between operations  1.63 us (1%)
    ppermute x8, starting transfers between devices, swapped(): return lax.ppermute(value, axis, pairs + [(j, i) for i, j in pairs])  54 us
    all_to_all x3, starting transfers between devices, spread(): lax.all_to_all(value, ('lon', 'lat'), 0, 0, axis_index_groups=groups, til...  23.5 us
    pallas_call x8, Pallas kernels, run(): return call(*scalars, *args, *waits)  13.3 us
    ppermute x8, waiting for transfers between devices, swapped(): return lax.ppermute(value, axis, pairs + [(j, i) for i, j in pairs])  8.89 us
    all_to_all x3, waiting for transfers between devices, spread(): lax.all_to_all(value, ('lon', 'lat'), 0, 0, axis_index_groups=groups, til...  8.32 us
    ppermute x2, starting transfers between devices, fold_stage(): return lambda value: lax.ppermute(value, ('lon', 'lat'), pairs)  2.58 us
    reshape x4, local copies, waits for them, and re-layouts, reordered(): split = weights.reshape(layout() + (-1, weights.shape[1]))  2.51 us
  transfers between devices with their start and end apart: 13, of which 5 were waited for; matrix products, arithmetic and copies ran while one was open for 3% of the time, Pallas kernels for 3%

profile of v3, /device:TPU:1, one launch (start us, length us, event | category | flops | bytes accessed | tf_op | source)
XLA Modules:
  0.0 117.8 jit_solution(2329375645625993223)
XLA Ops:
  0.7 0.1 pad_add_fusion.info
  0.7 0.9 copy-done
  1.6 0.6 shard_map.127
  2.2 15.9 %collective-permute-start.96 = (bf16[160,256]{1,0:T(8,128)(2,1)S(1)}, bf16[160,256]{1,0:T(8,128)(2,1)S(1)}, u32[]{:S(2)}, u32[]{:S(2)}) collective-permute-start(bf16[160,256]{1,0:T(8,128)(2,1)S(1)} %get-tuple-element.414), channel_id=1, source_target_pairs={{16,32},{48,64},{80,96},{112,128},{144,160},{176,192},{208,224},{2... | collective-permute-start | bytes 245768 | tf_op jit(solution)/shard_map/ppermute | solution.py:297
  18.1 1.9 %collective-permute-start.97 = (bf16[160,256]{1,0:T(8,128)(2,1)S(1)}, bf16[160,256]{1,0:T(8,128)(2,1)S(1)}, u32[]{:S(2)}, u32[]{:S(2)}) collective-permute-start(bf16[160,256]{1,0:T(8,128)(2,1)S(1)} %get-tuple-element.415), channel_id=1, source_target_pairs={{0,16},{32,48},{64,80},{96,112},{128,144},{160,176},{192,208},{224... | collective-permute-start | bytes 245768 | tf_op jit(solution)/shard_map/ppermute | solution.py:297
  20.0 1.2 %slice.3 = s32[1]{0:T(128)} slice(s32[1024]{0:T(1024)} %param.75), slice={[0:1]} | slice | bytes 8 | tf_op jit(solution)/shard_map/slice | solution.py:361
  21.9 1.2 %reshape.36 = bf16[8,4,4,2,2,2,256]{6,5,4,3,2,1,0:T(2,128)(2,1)S(1)} reshape(bf16[1024,256]{1,0:T(8,128)(2,1)} %param.78) | data formatting | bytes 1048576 | tf_op jit(solution)/shard_map/reshape | solution.py:354
  23.2 0.0 copy-start.6
  23.2 0.5 copy.19
  23.7 0.2 reshape.37.refs_0_.w_in
  23.9 0.3 copy-done.6
  24.2 0.2 reshape.38
  24.4 0.0 copy-start.1
  24.4 0.5 copy.18
  25.0 0.2 reshape.39.refs_1_.w_out
  25.2 0.0 copy-start.2
  25.2 0.0 copy-start.3
  25.2 0.0 copy-start.4
  25.2 0.0 copy-start.5
  25.2 0.0 collective-permute-done.96.side1
  25.2 0.0 collective-permute-done.97.side0
  25.3 0.1 copy-done.1
  25.3 0.6 shard_map.128
  25.9 8.8 %collective-permute-start.98 = (bf16[120,256]{1,0:T(8,128)(2,1)S(1)}, bf16[120,256]{1,0:T(8,128)(2,1)S(1)}, u32[]{:S(2)}, u32[]{:S(2)}) collective-permute-start(bf16[120,256]{1,0:T(8,128)(2,1)S(1)} %get-tuple-element.416), channel_id=1, source_target_pairs={{1,2},{3,4},{5,6},{7,8},{9,10},{11,12},{13,14},{2,1},{4,3},{6,5},{... | collective-permute-start | bytes 184328 | tf_op jit(solution)/shard_map/ppermute | solution.py:297
  34.7 1.9 %collective-permute-start.99 = (bf16[120,256]{1,0:T(8,128)(2,1)S(1)}, bf16[120,256]{1,0:T(8,128)(2,1)S(1)}, u32[]{:S(2)}, u32[]{:S(2)}) collective-permute-start(bf16[120,256]{1,0:T(8,128)(2,1)S(1)} %get-tuple-element.417), channel_id=1, source_target_pairs={{0,1},{2,3},{4,5},{6,7},{8,9},{10,11},{12,13},{14,15},{1,0},{3,2},... | collective-permute-start | bytes 184328 | tf_op jit(solution)/shard_map/ppermute | solution.py:297
  36.7 1.3 %conditional.2 = (bf16[120,256]{1,0:T(8,128)(2,1)}, bf16[32,256]{1,0:T(8,128)(2,1)S(1)}) conditional(s32[]{:T(128)} %clamp.4, (bf16[120,256]{1,0:T(8,128)(2,1)S(1)}, bf16[32,256]{1,0:T(8,128)(2,1)S(1)}) %tuple.264, (bf16[120,256]{1,0:T(8,128)(2,1)S(1)}, bf16[32,256]{1,0:T(8,128)(2,1)S(1)}) %tuple.264, ...), branch_computations={%region_0.1_spmd, %region_1.2_spmd, %region_2.3_spmd, %region_3.4_... | conditional | bytes 344160 | solution.py:333
  36.7 1.3 %collective-permute-start.39 = (bf16[120,256]{1,0:T(8,128)(2,1)S(1)}, bf16[120,256]{1,0:T(8,128)(2,1)}, u32[]{:S(2)}, u32[]{:S(2)}) collective-permute-start(bf16[120,256]{1,0:T(8,128)(2,1)S(1)} %get-tuple-element.308), channel_id=1, source_target_pairs={{431,15},{415,31},{399,47},{383,63},{367,79},{351,95},{335,111},{3... | collective-permute-start | bytes 184328 | tf_op jit(solution)/shard_map/cond/branch_26_fun/ppermute | solution.py:304
  38.0 0.0 collective-permute-done.39
  38.0 2.2 %collective-permute-done.98.far = bf16[120,256]{1,0:T(8,128)(2,1)S(1)} collective-permute-done((bf16[120,256]{1,0:T(8,128)(2,1)S(1)}, bf16[120,256]{1,0:T(8,128)(2,1)S(1)}, u32[]{:S(2)}, u32[]{:S(2)}) %collective-permute-start.98) | collective-permute-done | bytes 61472 | tf_op jit(solution)/shard_map/ppermute | solution.py:297
  40.3 6.8 %shard_map.129 = (bf16[8,32,256]{2,1,0:T(8,128)(2,1)}, bf16[8,32,256]{2,1,0:T(8,128)(2,1)S(1)}, bf16[160,256]{1,0:T(8,128)(2,1)S(1)}, bf16[160,256]{1,0:T(8,128)(2,1)S(1)}, bf16[32,144,128]{2,1,0:T(8,128)(2,1)}) custom-call(s32[3]{0:T(128)S(1)} %pad_add_fusion.info, s32[1]{0:T(128)} %bitcast.4.turn, bf16[8,32,256]{2,1,0:T(8,128)(2,1)S(1)} %copy-done.1, ...), custom_call_target="tpu_custom_call" | custom-call | tf_op jit(solution)/shard_map/pallas_call | solution.py:291
  47.0 9.7 %all-to-all-start = ((bf16[32,144,128]{2,1,0:T(8,128)(2,1)}), bf16[32,144,128]{2,1,0:T(8,128)(2,1)S(1)}, u32[]{:S(2)}, u32[]{:S(2)}) async-start(bf16[32,144,128]{2,1,0:T(8,128)(2,1)} %get-tuple-element.432), calls=%async_computation | async-start | bytes 2359296 | tf_op jit(solution)/shard_map/all_to_all | solution.py:350
  56.8 8.1 %collective-permute-start.100 = (bf16[160,256]{1,0:T(8,128)(2,1)S(1)}, bf16[160,256]{1,0:T(8,128)(2,1)S(1)}, u32[]{:S(2)}, u32[]{:S(2)}) collective-permute-start(bf16[160,256]{1,0:T(8,128)(2,1)S(1)} %get-tuple-element.424), channel_id=1, source_target_pairs={{16,32},{48,64},{80,96},{112,128},{144,160},{176,192},{208,224},{2... | collective-permute-start | bytes 245768 | tf_op jit(solution)/shard_map/ppermute | solution.py:297
  64.8 1.9 %collective-permute-start.101 = (bf16[160,256]{1,0:T(8,128)(2,1)S(1)}, bf16[160,256]{1,0:T(8,128)(2,1)S(1)}, u32[]{:S(2)}, u32[]{:S(2)}) collective-permute-start(bf16[160,256]{1,0:T(8,128)(2,1)S(1)} %get-tuple-element.425), channel_id=1, source_target_pairs={{0,16},{32,48},{64,80},{96,112},{128,144},{160,176},{192,208},{224... | collective-permute-start | bytes 245768 | tf_op jit(solution)/shard_map/ppermute | solution.py:297
  66.8 4.7 %collective-permute-done.100.side1.refs_0_ = bf16[160,256]{1,0:T(8,128)(2,1)S(1)} collective-permute-done((bf16[160,256]{1,0:T(8,128)(2,1)S(1)}, bf16[160,256]{1,0:T(8,128)(2,1)S(1)}, u32[]{:S(2)}, u32[]{:S(2)}) %collective-permute-start.100) | collective-permute-done | bytes 81952 | tf_op jit(solution)/shard_map/ppermute | solution.py:297
  71.4 2.0 %collective-permute-done.101.side0.refs_1_ = bf16[160,256]{1,0:T(8,128)(2,1)S(1)} collective-permute-done((bf16[160,256]{1,0:T(8,128)(2,1)S(1)}, bf16[160,256]{1,0:T(8,128)(2,1)S(1)}, u32[]{:S(2)}, u32[]{:S(2)}) %collective-permute-start.101) | collective-permute-done | bytes 81952 | tf_op jit(solution)/shard_map/ppermute | solution.py:297
  73.4 3.4 %all-to-all-done.received = bf16[32,144,128]{2,1,0:T(8,128)(2,1)S(1)} async-done(((bf16[32,144,128]{2,1,0:T(8,128)(2,1)}), bf16[32,144,128]{2,1,0:T(8,128)(2,1)S(1)}, u32[]{:S(2)}, u32[]{:S(2)}) %all-to-all-start) | async-done | bytes 1179680 | tf_op jit(solution)/shard_map/all_to_all | solution.py:350
  76.8 0.8 shard_map.132
  77.6 9.6 %all-to-all-start.1 = ((bf16[16,16,128]{2,1,0:T(8,128)(2,1)}), bf16[16,16,128]{2,1,0:T(8,128)(2,1)S(1)}, u32[]{:S(2)}, u32[]{:S(2)}) async-start(bf16[16,16,128]{2,1,0:T(8,128)(2,1)} %shard_map.132), calls=%async_computation.1 | async-start | bytes 131072 | tf_op jit(solution)/shard_map/all_to_all | solution.py:350
  87.2 0.6 shard_map.130
  87.9 13.6 %collective-permute-start.102 = (bf16[120,256]{1,0:T(8,128)(2,1)S(1)}, bf16[120,256]{1,0:T(8,128)(2,1)S(1)}, u32[]{:S(2)}, u32[]{:S(2)}) collective-permute-start(bf16[120,256]{1,0:T(8,128)(2,1)S(1)} %get-tuple-element.426), channel_id=1, source_target_pairs={{1,2},{3,4},{5,6},{7,8},{9,10},{11,12},{13,14},{2,1},{4,3},{6,5},{... | collective-permute-start | bytes 184328 | tf_op jit(solution)/shard_map/ppermute | solution.py:297
  101.4 1.9 %collective-permute-start.103 = (bf16[120,256]{1,0:T(8,128)(2,1)S(1)}, bf16[120,256]{1,0:T(8,128)(2,1)S(1)}, u32[]{:S(2)}, u32[]{:S(2)}) collective-permute-start(bf16[120,256]{1,0:T(8,128)(2,1)S(1)} %get-tuple-element.427), channel_id=1, source_target_pairs={{0,1},{2,3},{4,5},{6,7},{8,9},{10,11},{12,13},{14,15},{1,0},{3,2},... | collective-permute-start | bytes 184328 | tf_op jit(solution)/shard_map/ppermute | solution.py:297
  103.4 1.3 %conditional.3 = (bf16[120,256]{1,0:T(8,128)(2,1)}, bf16[32,256]{1,0:T(8,128)(2,1)S(1)}) conditional(s32[]{:T(128)} %clamp.4, (bf16[120,256]{1,0:T(8,128)(2,1)S(1)}, bf16[32,256]{1,0:T(8,128)(2,1)S(1)}) %tuple.265, (bf16[120,256]{1,0:T(8,128)(2,1)S(1)}, bf16[32,256]{1,0:T(8,128)(2,1)S(1)}) %tuple.265, ...), branch_computations={%region_32.33_spmd, %region_33.34_spmd, %region_34.35_spmd, %regio... | conditional | bytes 344160 | solution.py:333
  103.4 1.3 %collective-permute-start.87 = (bf16[120,256]{1,0:T(8,128)(2,1)S(1)}, bf16[120,256]{1,0:T(8,128)(2,1)}, u32[]{:S(2)}, u32[]{:S(2)}) collective-permute-start(bf16[120,256]{1,0:T(8,128)(2,1)S(1)} %get-tuple-element.372), channel_id=1, source_target_pairs={{431,15},{415,31},{399,47},{383,63},{367,79},{351,95},{335,111},{3... | collective-permute-start | bytes 184328 | tf_op jit(solution)/shard_map/cond/branch_26_fun/ppermute | solution.py:304
  104.7 0.7 shard_map.133
  105.4 4.2 %all-to-all-start.2 = ((f32[32,8,128]{2,1,0:T(8,128)}), f32[32,8,128]{2,1,0:T(8,128)S(1)}, u32[]{:S(2)}, u32[]{:S(2)}) async-start(f32[32,8,128]{2,1,0:T(8,128)} %get-tuple-element.435), calls=%async_computation.2 | async-start | bytes 262144 | tf_op jit(solution)/shard_map/all_to_all | solution.py:350
  109.6 2.6 %shard_map.131 = bf16[8,32,256]{2,1,0:T(8,128)(2,1)} custom-call(s32[3]{0:T(128)S(1)} %pad_add_fusion.info, s32[1]{0:T(128)} %bitcast.4.turn, bf16[8,32,256]{2,1,0:T(8,128)(2,1)S(1)} %get-tuple-element.423.own, bf16[160,256]{1,0:T(8,128)(2,1)S(1)} %collective-permute-done.100.side1.refs_0_, bf16[160,256]{1,0:T(8,128)(2,1)S(1)} %collective-permute-done.101.side0.refs_1_, ...), custom_call_target="tpu_custom_call" | custom-call | tf_op jit(solution)/shard_map/pallas_call | solution.py:291
  112.2 5.0 %all-to-all-done.2.received = f32[32,8,128]{2,1,0:T(8,128)S(1)} async-done(((f32[32,8,128]{2,1,0:T(8,128)}), f32[32,8,128]{2,1,0:T(8,128)S(1)}, u32[]{:S(2)}, u32[]{:S(2)}) %all-to-all-start.2) | async-done | bytes 131104 | tf_op jit(solution)/shard_map/all_to_all | solution.py:350
  117.1 0.7 shard_map.134
  (10 shorter events, 0.0 us)
Async XLA Ops:
  0.7 0.9 copy-start
  2.2 23.0 %collective-permute-start.96 = (bf16[160,256]{1,0:T(8,128)(2,1)S(1)}, bf16[160,256]{1,0:T(8,128)(2,1)S(1)}, u32[]{:S(2)}, u32[]{:S(2)}) collective-permute-start(bf16[160,256]{1,0:T(8,128)(2,1)S(1)} %get-tuple-element.414), channel_id=1, source_target_pairs={{16,32},{48,64},{80,96},{112,128},{144,160},{176,192},{208,224},{2... | collective-permute-start | bytes 245768 | tf_op jit(solution)/shard_map/ppermute | solution.py:297
  18.1 7.1 %collective-permute-start.97 = (bf16[160,256]{1,0:T(8,128)(2,1)S(1)}, bf16[160,256]{1,0:T(8,128)(2,1)S(1)}, u32[]{:S(2)}, u32[]{:S(2)}) collective-permute-start(bf16[160,256]{1,0:T(8,128)(2,1)S(1)} %get-tuple-element.415), channel_id=1, source_target_pairs={{0,16},{32,48},{64,80},{96,112},{128,144},{160,176},{192,208},{224... | collective-permute-start | bytes 245768 | tf_op jit(solution)/shard_map/ppermute | solution.py:297
  23.2 1.0 copy-start.6
  24.4 0.9 copy-start.1
  25.2 15.1 %copy-start.2 = (bf16[8,32,256]{2,1,0:T(8,128)(2,1)S(1)}, bf16[8,32,256]{2,1,0:T(8,128)(2,1)}, u32[]{:S(2)}) copy-start(bf16[8,32,256]{2,1,0:T(8,128)(2,1)} %cot.3) | copy-start | bytes 393220
  25.2 15.1 %copy-start.3 = (f32[7,7,256]{2,1,0:T(8,128)S(1)}, f32[7,7,256]{2,1,0:T(8,128)}, u32[]{:S(2)}) copy-start(f32[7,7,256]{2,1,0:T(8,128)} %taps.3) | copy-start | bytes 150532
  25.2 15.1 %copy-start.4 = (s32[8,32]{1,0:T(8,128)S(1)}, s32[8,32]{1,0:T(8,128)}, u32[]{:S(2)}) copy-start(s32[8,32]{1,0:T(8,128)} %land.3) | copy-start | bytes 3076
  25.2 15.1 %copy-start.5 = (f32[256]{0:T(256)S(1)}, f32[256]{0:T(256)}, u32[]{:S(2)}) copy-start(f32[256]{0:T(256)} %param.77) | copy-start | bytes 3076
  25.9 14.3 %collective-permute-start.98 = (bf16[120,256]{1,0:T(8,128)(2,1)S(1)}, bf16[120,256]{1,0:T(8,128)(2,1)S(1)}, u32[]{:S(2)}, u32[]{:S(2)}) collective-permute-start(bf16[120,256]{1,0:T(8,128)(2,1)S(1)} %get-tuple-element.416), channel_id=1, source_target_pairs={{1,2},{3,4},{5,6},{7,8},{9,10},{11,12},{13,14},{2,1},{4,3},{6,5},{... | collective-permute-start | bytes 184328 | tf_op jit(solution)/shard_map/ppermute | solution.py:297
  34.7 5.5 %collective-permute-start.99 = (bf16[120,256]{1,0:T(8,128)(2,1)S(1)}, bf16[120,256]{1,0:T(8,128)(2,1)S(1)}, u32[]{:S(2)}, u32[]{:S(2)}) collective-permute-start(bf16[120,256]{1,0:T(8,128)(2,1)S(1)} %get-tuple-element.417), channel_id=1, source_target_pairs={{0,1},{2,3},{4,5},{6,7},{8,9},{10,11},{12,13},{14,15},{1,0},{3,2},... | collective-permute-start | bytes 184328 | tf_op jit(solution)/shard_map/ppermute | solution.py:297
  36.7 1.3 %collective-permute-start.39 = (bf16[120,256]{1,0:T(8,128)(2,1)S(1)}, bf16[120,256]{1,0:T(8,128)(2,1)}, u32[]{:S(2)}, u32[]{:S(2)}) collective-permute-start(bf16[120,256]{1,0:T(8,128)(2,1)S(1)} %get-tuple-element.308), channel_id=1, source_target_pairs={{431,15},{415,31},{399,47},{383,63},{367,79},{351,95},{335,111},{3... | collective-permute-start | bytes 184328 | tf_op jit(solution)/shard_map/cond/branch_26_fun/ppermute | solution.py:304
  47.0 29.7 %all-to-all-start = ((bf16[32,144,128]{2,1,0:T(8,128)(2,1)}), bf16[32,144,128]{2,1,0:T(8,128)(2,1)S(1)}, u32[]{:S(2)}, u32[]{:S(2)}) async-start(bf16[32,144,128]{2,1,0:T(8,128)(2,1)} %get-tuple-element.432), calls=%async_computation | async-start | bytes 2359296 | tf_op jit(solution)/shard_map/all_to_all | solution.py:350
  56.8 14.7 %collective-permute-start.100 = (bf16[160,256]{1,0:T(8,128)(2,1)S(1)}, bf16[160,256]{1,0:T(8,128)(2,1)S(1)}, u32[]{:S(2)}, u32[]{:S(2)}) collective-permute-start(bf16[160,256]{1,0:T(8,128)(2,1)S(1)} %get-tuple-element.424), channel_id=1, source_target_pairs={{16,32},{48,64},{80,96},{112,128},{144,160},{176,192},{208,224},{2... | collective-permute-start | bytes 245768 | tf_op jit(solution)/shard_map/ppermute | solution.py:297
  64.8 8.6 %collective-permute-start.101 = (bf16[160,256]{1,0:T(8,128)(2,1)S(1)}, bf16[160,256]{1,0:T(8,128)(2,1)S(1)}, u32[]{:S(2)}, u32[]{:S(2)}) collective-permute-start(bf16[160,256]{1,0:T(8,128)(2,1)S(1)} %get-tuple-element.425), channel_id=1, source_target_pairs={{0,16},{32,48},{64,80},{96,112},{128,144},{160,176},{192,208},{224... | collective-permute-start | bytes 245768 | tf_op jit(solution)/shard_map/ppermute | solution.py:297
  77.6 27.1 %all-to-all-start.1 = ((bf16[16,16,128]{2,1,0:T(8,128)(2,1)}), bf16[16,16,128]{2,1,0:T(8,128)(2,1)S(1)}, u32[]{:S(2)}, u32[]{:S(2)}) async-start(bf16[16,16,128]{2,1,0:T(8,128)(2,1)} %shard_map.132), calls=%async_computation.1 | async-start | bytes 131072 | tf_op jit(solution)/shard_map/all_to_all | solution.py:350
  87.9 16.9 %collective-permute-start.102 = (bf16[120,256]{1,0:T(8,128)(2,1)S(1)}, bf16[120,256]{1,0:T(8,128)(2,1)S(1)}, u32[]{:S(2)}, u32[]{:S(2)}) collective-permute-start(bf16[120,256]{1,0:T(8,128)(2,1)S(1)} %get-tuple-element.426), channel_id=1, source_target_pairs={{1,2},{3,4},{5,6},{7,8},{9,10},{11,12},{13,14},{2,1},{4,3},{6,5},{... | collective-permute-start | bytes 184328 | tf_op jit(solution)/shard_map/ppermute | solution.py:297
  101.4 3.3 %collective-permute-start.103 = (bf16[120,256]{1,0:T(8,128)(2,1)S(1)}, bf16[120,256]{1,0:T(8,128)(2,1)S(1)}, u32[]{:S(2)}, u32[]{:S(2)}) collective-permute-start(bf16[120,256]{1,0:T(8,128)(2,1)S(1)} %get-tuple-element.427), channel_id=1, source_target_pairs={{0,1},{2,3},{4,5},{6,7},{8,9},{10,11},{12,13},{14,15},{1,0},{3,2},... | collective-permute-start | bytes 184328 | tf_op jit(solution)/shard_map/ppermute | solution.py:297
  103.4 1.3 %collective-permute-start.87 = (bf16[120,256]{1,0:T(8,128)(2,1)S(1)}, bf16[120,256]{1,0:T(8,128)(2,1)}, u32[]{:S(2)}, u32[]{:S(2)}) collective-permute-start(bf16[120,256]{1,0:T(8,128)(2,1)S(1)} %get-tuple-element.372), channel_id=1, source_target_pairs={{431,15},{415,31},{399,47},{383,63},{367,79},{351,95},{335,111},{3... | collective-permute-start | bytes 184328 | tf_op jit(solution)/shard_map/cond/branch_26_fun/ppermute | solution.py:304
  105.4 11.7 %all-to-all-start.2 = ((f32[32,8,128]{2,1,0:T(8,128)}), f32[32,8,128]{2,1,0:T(8,128)S(1)}, u32[]{:S(2)}, u32[]{:S(2)}) async-start(f32[32,8,128]{2,1,0:T(8,128)} %get-tuple-element.435), calls=%async_computation.2 | async-start | bytes 262144 | tf_op jit(solution)/shard_map/all_to_all | solution.py:350

commit v4 on v3

--- a/solution.py
+++ b/solution.py
@@ -97,7 +97,7 @@
         window[...] = strip[pl.ds(0, 3), :, :].reshape(3 * SPAN, WIDTH).astype(bf16)
 
 
-def assemble(info, turn, own, side1, side0, far, near, window, extra, wide):
+def assemble(info, turn, own, side1, side0, far, window, extra, near, wide):
     middle(info, wide, 3, own, (side0, side1))
     columns = pl.ds(LEFT - 3, SPAN)
     for parity, (below, above) in enumerate(((far, near), (near, far))):
@@ -126,10 +126,10 @@
 
 
 def main_kernel(
-    info, turn, own, side1, side0, far, near, window, extra, cot, land, taps, gain, w_in, w_out,
+    info, turn, own, side1, side0, far, window, extra, near, cot, land, taps, gain, w_in, w_out,
     block_out, dconv, message0, message1, message, wide, grid, sums,
 ):
-    assemble(info, turn, own, side1, side0, far, near, window, extra, wide)
+    assemble(info, turn, own, side1, side0, far, window, extra, near, wide)
     for half in range(WIDTH // LANES):
         lanes = pl.ds(half * LANES, LANES)
         for tile in range(COLS // 8):
@@ -202,9 +202,9 @@
 
 
 def grad_input_kernel(
-    info, turn, own, side1, side0, far, near, window, extra, cot, land, taps, grad_input, wide, upstream
+    info, turn, own, side1, side0, far, window, extra, near, cot, land, taps, grad_input, wide, upstream
 ):
-    assemble(info, turn, own, side1, side0, far, near, window, extra, wide)
+    assemble(info, turn, own, side1, side0, far, window, extra, near, wide)
     folded = info[0] == 1
     upstream[...] = keepers(land) * cot[...].astype(f32)
     for half in range(WIDTH // LANES):
@@ -320,17 +320,21 @@
         *sides,
         waits=waits,
     )
-    far = swapped(far, "lat", 1, False)
-    near = swapped(near, "lat", 0, False)
     lat_count, lon_count = lax.axis_size("lat"), lax.axis_size("lon")
     moves = [fold_stage(FOLD * k, lat_count, lon_count) for k in range(lon_count // FOLD)]
 
     def branch(k, whole):
-        return lambda window, extra: (moves[k](window), extra if whole else moves[k - 1](extra))
+        def exchange(far, window, extra, near):
+            far = swapped(far, "lat", 1, False)
+            window = moves[k](window)
+            extra = extra if whole else moves[k - 1](extra)
+            return far, window, extra, swapped(near, "lat", 0, False)
+
+        return exchange
 
     branches = [branch(k, whole) for k in range(len(moves)) for whole in (True, False)]
     chosen = 2 * (shift // (FOLD * COLS)) + (turn[0] < BEYOND)
-    return value, *sides, far, near, *lax.switch(chosen, branches, window, extra)
+    return value, *sides, *lax.switch(chosen, branches, far, window, extra, near)
 
 
 def layout():

time: 117 us -> 117 us (level); the launches traced: 118 us -> 115 us
  starting transfers between devices: 80.1 us -> 75.6 us
  waiting for transfers between devices: 17.2 us -> 18.7 us
    all_to_all x3, starting transfers between devices: 23.5 us -> 19.1 us  [spread(): lax.all_to_all(value, ('lon', 'lat'), 0, 0, axis_index_groups=groups, til...]
    ppermute x8, waiting for transfers between devices: 8.89 us -> 10.4 us  [swapped(): return lax.ppermute(value, axis, pairs + [(j, i) for i, j in pairs])]
  transfers between devices with their start and end apart: 13 -> 13, of which waited for: 5 -> 6; matrix products, arithmetic and copies ran while one was open for 3% -> 4% of each run, Pallas kernels for 3% -> 3%
where the time goes in v4:
time: 117 us; the launch traced here: 115 us
  starting transfers between devices  75.6 us (65%)
  waiting for transfers between devices  18.7 us (16%)
  Pallas kernels  13.5 us (12%)
  local copies, waits for them, and re-layouts  5.4 us (5%)
  between operations  1.57 us (1%)
    ppermute x8, starting transfers between devices, swapped(): return lax.ppermute(value, axis, pairs + [(j, i) for i, j in pairs])  54 us
    all_to_all x3, starting transfers between devices, spread(): lax.all_to_all(value, ('lon', 'lat'), 0, 0, axis_index_groups=groups, til...  19.1 us
    pallas_call x8, Pallas kernels, run(): return call(*scalars, *args, *waits)  13.5 us
    ppermute x8, waiting for transfers between devices, swapped(): return lax.ppermute(value, axis, pairs + [(j, i) for i, j in pairs])  10.4 us
    all_to_all x3, waiting for transfers between devices, spread(): lax.all_to_all(value, ('lon', 'lat'), 0, 0, axis_index_groups=groups, til...  8.28 us
    ppermute x2, starting transfers between devices, fold_stage(): return lambda value: lax.ppermute(value, ('lon', 'lat'), pairs)  2.56 us
    reshape x4, local copies, waits for them, and re-layouts, reordered(): split = weights.reshape(layout() + (-1, weights.shape[1]))  2.51 us
  transfers between devices with their start and end apart: 13, of which 6 were waited for; matrix products, arithmetic and copies ran while one was open for 4% of the time, Pallas kernels for 3%

profile of v4, /device:TPU:1, one launch (start us, length us, event | category | flops | bytes accessed | tf_op | source)
XLA Modules:
  0.0 115.0 jit_solution(5087534006203867942)
XLA Ops:
  0.7 0.1 pad_add_fusion.info
  0.7 0.9 copy-done
  1.6 0.6 shard_map.127
  2.2 15.9 %collective-permute-start.224 = (bf16[160,256]{1,0:T(8,128)(2,1)S(1)}, bf16[160,256]{1,0:T(8,128)(2,1)S(1)}, u32[]{:S(2)}, u32[]{:S(2)}) collective-permute-start(bf16[160,256]{1,0:T(8,128)(2,1)S(1)} %get-tuple-element.802), channel_id=1, source_target_pairs={{16,32},{48,64},{80,96},{112,128},{144,160},{176,192},{208,224},{2... | collective-permute-start | bytes 245768 | tf_op jit(solution)/shard_map/ppermute | solution.py:297
  18.1 1.9 %collective-permute-start.225 = (bf16[160,256]{1,0:T(8,128)(2,1)S(1)}, bf16[160,256]{1,0:T(8,128)(2,1)S(1)}, u32[]{:S(2)}, u32[]{:S(2)}) collective-permute-start(bf16[160,256]{1,0:T(8,128)(2,1)S(1)} %get-tuple-element.803), channel_id=1, source_target_pairs={{0,16},{32,48},{64,80},{96,112},{128,144},{160,176},{192,208},{224... | collective-permute-start | bytes 245768 | tf_op jit(solution)/shard_map/ppermute | solution.py:297
  20.0 1.2 %slice.3 = s32[1]{0:T(128)} slice(s32[1024]{0:T(1024)} %param.75), slice={[0:1]} | slice | bytes 8 | tf_op jit(solution)/shard_map/slice | solution.py:365
  21.9 1.2 %reshape.36 = bf16[8,4,4,2,2,2,256]{6,5,4,3,2,1,0:T(2,128)(2,1)S(1)} reshape(bf16[1024,256]{1,0:T(8,128)(2,1)} %param.78) | data formatting | bytes 1048576 | tf_op jit(solution)/shard_map/reshape | solution.py:358
  23.2 0.0 copy-start.6
  23.2 0.5 copy.19
  23.7 0.2 reshape.37.refs_0_.w_in
  23.9 0.3 copy-done.6
  24.2 0.2 reshape.38
  24.4 0.0 copy-start.1
  24.4 0.5 copy.18
  25.0 0.2 reshape.39.refs_1_.w_out
  25.2 0.0 copy-start.2
  25.2 0.0 copy-start.3
  25.2 0.0 copy-start.4
  25.2 0.0 copy-start.5
  25.3 0.0 collective-permute-done.225.side0
  25.3 0.1 copy-done.1
  25.3 0.6 shard_map.128
  25.9 14.5 %conditional.2 = (bf16[120,256]{1,0:T(8,128)(2,1)}, bf16[120,256]{1,0:T(8,128)(2,1)}, bf16[32,256]{1,0:T(8,128)(2,1)S(1)}, bf16[120,256]{1,0:T(8,128)(2,1)}) conditional(s32[]{:T(128)} %clamp.4, (bf16[120,256]{1,0:T(8,128)(2,1)S(1)}, bf16[120,256]{1,0:T(8,128)(2,1)S(1)}, bf16[120,256]{1,0:T(8,128)(2,1)S(1)}, ...), branch_computations={%region_0.1_spmd, %region_1.2_spmd, %region_2.3_spmd, %region_3.4_... | conditional | bytes 835776 | solution.py:337
  26.0 8.8 %collective-permute-start.14 = (bf16[120,256]{1,0:T(8,128)(2,1)S(1)}, bf16[120,256]{1,0:T(8,128)(2,1)}, u32[]{:S(2)}, u32[]{:S(2)}) collective-permute-start(bf16[120,256]{1,0:T(8,128)(2,1)S(1)} %get-tuple-element.528), channel_id=1, source_target_pairs={{1,2},{3,4},{5,6},{7,8},{9,10},{11,12},{13,14},{2,1},{4,3},{6,5},{... | collective-permute-start | bytes 184328 | tf_op jit(solution)/shard_map/cond/branch_4_fun/ppermute | solution.py:297
  34.8 1.3 %collective-permute-start.15 = (bf16[120,256]{1,0:T(8,128)(2,1)S(1)}, bf16[120,256]{1,0:T(8,128)(2,1)}, u32[]{:S(2)}, u32[]{:S(2)}) collective-permute-start(bf16[120,256]{1,0:T(8,128)(2,1)S(1)} %get-tuple-element.529), channel_id=1, source_target_pairs={{79,15},{63,31},{47,47},{31,63},{15,79},{511,95},{495,111},{479,12... | collective-permute-start | bytes 184328 | tf_op jit(solution)/shard_map/cond/branch_4_fun/ppermute | solution.py:304
  36.1 1.9 %collective-permute-start.16 = (bf16[120,256]{1,0:T(8,128)(2,1)S(1)}, bf16[120,256]{1,0:T(8,128)(2,1)}, u32[]{:S(2)}, u32[]{:S(2)}) collective-permute-start(bf16[120,256]{1,0:T(8,128)(2,1)S(1)} %get-tuple-element.531), channel_id=1, source_target_pairs={{0,1},{2,3},{4,5},{6,7},{8,9},{10,11},{12,13},{14,15},{1,0},{3,2},... | collective-permute-start | bytes 184328 | tf_op jit(solution)/shard_map/cond/branch_4_fun/ppermute | solution.py:297
  38.0 2.4 %collective-permute-done.14 = bf16[120,256]{1,0:T(8,128)(2,1)} collective-permute-done((bf16[120,256]{1,0:T(8,128)(2,1)S(1)}, bf16[120,256]{1,0:T(8,128)(2,1)}, u32[]{:S(2)}, u32[]{:S(2)}) %collective-permute-start.14) | collective-permute-done | bytes 61472 | tf_op jit(solution)/shard_map/cond/branch_4_fun/ppermute | solution.py:297
  40.4 0.0 collective-permute-done.16
  40.4 7.0 %shard_map.129 = (bf16[8,32,256]{2,1,0:T(8,128)(2,1)}, bf16[8,32,256]{2,1,0:T(8,128)(2,1)S(1)}, bf16[160,256]{1,0:T(8,128)(2,1)S(1)}, bf16[160,256]{1,0:T(8,128)(2,1)S(1)}, bf16[32,144,128]{2,1,0:T(8,128)(2,1)}) custom-call(s32[3]{0:T(128)S(1)} %pad_add_fusion.info, s32[1]{0:T(128)} %bitcast.4.turn, bf16[8,32,256]{2,1,0:T(8,128)(2,1)S(1)} %copy-done.1, ...), custom_call_target="tpu_custom_call" | custom-call | tf_op jit(solution)/shard_map/pallas_call | solution.py:291
  47.4 9.7 %all-to-all-start = ((bf16[32,144,128]{2,1,0:T(8,128)(2,1)}), bf16[32,144,128]{2,1,0:T(8,128)(2,1)S(1)}, u32[]{:S(2)}, u32[]{:S(2)}) async-start(bf16[32,144,128]{2,1,0:T(8,128)(2,1)} %get-tuple-element.824), calls=%async_computation | async-start | bytes 2359296 | tf_op jit(solution)/shard_map/all_to_all | solution.py:354
  57.2 8.1 %collective-permute-start.226 = (bf16[160,256]{1,0:T(8,128)(2,1)S(1)}, bf16[160,256]{1,0:T(8,128)(2,1)S(1)}, u32[]{:S(2)}, u32[]{:S(2)}) collective-permute-start(bf16[160,256]{1,0:T(8,128)(2,1)S(1)} %get-tuple-element.814), channel_id=1, source_target_pairs={{16,32},{48,64},{80,96},{112,128},{144,160},{176,192},{208,224},{2... | collective-permute-start | bytes 245768 | tf_op jit(solution)/shard_map/ppermute | solution.py:297
  65.2 1.9 %collective-permute-start.227 = (bf16[160,256]{1,0:T(8,128)(2,1)S(1)}, bf16[160,256]{1,0:T(8,128)(2,1)S(1)}, u32[]{:S(2)}, u32[]{:S(2)}) collective-permute-start(bf16[160,256]{1,0:T(8,128)(2,1)S(1)} %get-tuple-element.815), channel_id=1, source_target_pairs={{0,16},{32,48},{64,80},{96,112},{128,144},{160,176},{192,208},{224... | collective-permute-start | bytes 245768 | tf_op jit(solution)/shard_map/ppermute | solution.py:297
  67.2 4.7 %collective-permute-done.226.side1.refs_0_ = bf16[160,256]{1,0:T(8,128)(2,1)S(1)} collective-permute-done((bf16[160,256]{1,0:T(8,128)(2,1)S(1)}, bf16[160,256]{1,0:T(8,128)(2,1)S(1)}, u32[]{:S(2)}, u32[]{:S(2)}) %collective-permute-start.226) | collective-permute-done | bytes 81952 | tf_op jit(solution)/shard_map/ppermute | solution.py:297
  71.8 2.0 %collective-permute-done.227.side0.refs_1_ = bf16[160,256]{1,0:T(8,128)(2,1)S(1)} collective-permute-done((bf16[160,256]{1,0:T(8,128)(2,1)S(1)}, bf16[160,256]{1,0:T(8,128)(2,1)S(1)}, u32[]{:S(2)}, u32[]{:S(2)}) %collective-permute-start.227) | collective-permute-done | bytes 81952 | tf_op jit(solution)/shard_map/ppermute | solution.py:297
  73.8 3.4 %all-to-all-done.received = bf16[32,144,128]{2,1,0:T(8,128)(2,1)S(1)} async-done(((bf16[32,144,128]{2,1,0:T(8,128)(2,1)}), bf16[32,144,128]{2,1,0:T(8,128)(2,1)S(1)}, u32[]{:S(2)}, u32[]{:S(2)}) %all-to-all-start) | async-done | bytes 1179680 | tf_op jit(solution)/shard_map/all_to_all | solution.py:354
  77.2 0.8 shard_map.132
  78.0 5.6 %all-to-all-start.1 = ((bf16[16,16,128]{2,1,0:T(8,128)(2,1)}), bf16[16,16,128]{2,1,0:T(8,128)(2,1)S(1)}, u32[]{:S(2)}, u32[]{:S(2)}) async-start(bf16[16,16,128]{2,1,0:T(8,128)(2,1)} %shard_map.132), calls=%async_computation.1 | async-start | bytes 131072 | tf_op jit(solution)/shard_map/all_to_all | solution.py:354
  83.6 0.6 shard_map.130
  84.2 18.2 %conditional.3 = (bf16[120,256]{1,0:T(8,128)(2,1)}, bf16[120,256]{1,0:T(8,128)(2,1)}, bf16[32,256]{1,0:T(8,128)(2,1)S(1)}, bf16[120,256]{1,0:T(8,128)(2,1)}) conditional(s32[]{:T(128)} %clamp.4, (bf16[120,256]{1,0:T(8,128)(2,1)S(1)}, bf16[120,256]{1,0:T(8,128)(2,1)S(1)}, bf16[120,256]{1,0:T(8,128)(2,1)S(1)}, ...), branch_computations={%region_32.33_spmd, %region_33.34_spmd, %region_34.35_spmd, %regio... | conditional | bytes 835776 | solution.py:337
  84.2 13.6 %collective-permute-start.126 = (bf16[120,256]{1,0:T(8,128)(2,1)S(1)}, bf16[120,256]{1,0:T(8,128)(2,1)}, u32[]{:S(2)}, u32[]{:S(2)}) collective-permute-start(bf16[120,256]{1,0:T(8,128)(2,1)S(1)} %get-tuple-element.656), channel_id=1, source_target_pairs={{1,2},{3,4},{5,6},{7,8},{9,10},{11,12},{13,14},{2,1},{4,3},{6,5},{... | collective-permute-start | bytes 184328 | tf_op jit(solution)/shard_map/cond/branch_4_fun/ppermute | solution.py:297
  97.8 1.3 %collective-permute-start.127 = (bf16[120,256]{1,0:T(8,128)(2,1)S(1)}, bf16[120,256]{1,0:T(8,128)(2,1)}, u32[]{:S(2)}, u32[]{:S(2)}) collective-permute-start(bf16[120,256]{1,0:T(8,128)(2,1)S(1)} %get-tuple-element.657), channel_id=1, source_target_pairs={{79,15},{63,31},{47,47},{31,63},{15,79},{511,95},{495,111},{479,12... | collective-permute-start | bytes 184328 | tf_op jit(solution)/shard_map/cond/branch_4_fun/ppermute | solution.py:304
  99.1 1.9 %collective-permute-start.128 = (bf16[120,256]{1,0:T(8,128)(2,1)S(1)}, bf16[120,256]{1,0:T(8,128)(2,1)}, u32[]{:S(2)}, u32[]{:S(2)}) collective-permute-start(bf16[120,256]{1,0:T(8,128)(2,1)S(1)} %get-tuple-element.659), channel_id=1, source_target_pairs={{0,1},{2,3},{4,5},{6,7},{8,9},{10,11},{12,13},{14,15},{1,0},{3,2},... | collective-permute-start | bytes 184328 | tf_op jit(solution)/shard_map/cond/branch_4_fun/ppermute | solution.py:297
  101.0 1.3 %collective-permute-done.128 = bf16[120,256]{1,0:T(8,128)(2,1)} collective-permute-done((bf16[120,256]{1,0:T(8,128)(2,1)S(1)}, bf16[120,256]{1,0:T(8,128)(2,1)}, u32[]{:S(2)}, u32[]{:S(2)}) %collective-permute-start.128) | collective-permute-done | bytes 61472 | tf_op jit(solution)/shard_map/cond/branch_4_fun/ppermute | solution.py:297
  102.4 0.7 shard_map.133
  103.1 3.8 %all-to-all-start.2 = ((f32[32,8,128]{2,1,0:T(8,128)}), f32[32,8,128]{2,1,0:T(8,128)S(1)}, u32[]{:S(2)}, u32[]{:S(2)}) async-start(f32[32,8,128]{2,1,0:T(8,128)} %get-tuple-element.827), calls=%async_computation.2 | async-start | bytes 262144 | tf_op jit(solution)/shard_map/all_to_all | solution.py:354
  106.8 2.6 %shard_map.131 = bf16[8,32,256]{2,1,0:T(8,128)(2,1)} custom-call(s32[3]{0:T(128)S(1)} %pad_add_fusion.info, s32[1]{0:T(128)} %bitcast.4.turn, bf16[8,32,256]{2,1,0:T(8,128)(2,1)S(1)} %get-tuple-element.813.own, bf16[160,256]{1,0:T(8,128)(2,1)S(1)} %collective-permute-done.226.side1.refs_0_, bf16[160,256]{1,0:T(8,128)(2,1)S(1)} %collective-permute-done.227.side0.refs_1_, ...), custom_call_target="tpu_custom_call" | custom-call | tf_op jit(solution)/shard_map/pallas_call | solution.py:291
  109.4 4.9 %all-to-all-done.2.received = f32[32,8,128]{2,1,0:T(8,128)S(1)} async-done(((f32[32,8,128]{2,1,0:T(8,128)}), f32[32,8,128]{2,1,0:T(8,128)S(1)}, u32[]{:S(2)}, u32[]{:S(2)}) %all-to-all-start.2) | async-done | bytes 131104 | tf_op jit(solution)/shard_map/all_to_all | solution.py:354
  114.4 0.7 shard_map.134
  (10 shorter events, 0.0 us)
Async XLA Ops:
  0.7 0.9 copy-start
  2.2 23.1 %collective-permute-start.224 = (bf16[160,256]{1,0:T(8,128)(2,1)S(1)}, bf16[160,256]{1,0:T(8,128)(2,1)S(1)}, u32[]{:S(2)}, u32[]{:S(2)}) collective-permute-start(bf16[160,256]{1,0:T(8,128)(2,1)S(1)} %get-tuple-element.802), channel_id=1, source_target_pairs={{16,32},{48,64},{80,96},{112,128},{144,160},{176,192},{208,224},{2... | collective-permute-start | bytes 245768 | tf_op jit(solution)/shard_map/ppermute | solution.py:297
  18.1 7.2 %collective-permute-start.225 = (bf16[160,256]{1,0:T(8,128)(2,1)S(1)}, bf16[160,256]{1,0:T(8,128)(2,1)S(1)}, u32[]{:S(2)}, u32[]{:S(2)}) collective-permute-start(bf16[160,256]{1,0:T(8,128)(2,1)S(1)} %get-tuple-element.803), channel_id=1, source_target_pairs={{0,16},{32,48},{64,80},{96,112},{128,144},{160,176},{192,208},{224... | collective-permute-start | bytes 245768 | tf_op jit(solution)/shard_map/ppermute | solution.py:297
  23.2 1.0 copy-start.6
  24.4 0.9 copy-start.1
  25.2 15.2 %copy-start.2 = (bf16[8,32,256]{2,1,0:T(8,128)(2,1)S(1)}, bf16[8,32,256]{2,1,0:T(8,128)(2,1)}, u32[]{:S(2)}) copy-start(bf16[8,32,256]{2,1,0:T(8,128)(2,1)} %cot.3) | copy-start | bytes 393220
  25.2 15.2 %copy-start.3 = (f32[7,7,256]{2,1,0:T(8,128)S(1)}, f32[7,7,256]{2,1,0:T(8,128)}, u32[]{:S(2)}) copy-start(f32[7,7,256]{2,1,0:T(8,128)} %taps.3) | copy-start | bytes 150532
  25.2 15.2 %copy-start.4 = (s32[8,32]{1,0:T(8,128)S(1)}, s32[8,32]{1,0:T(8,128)}, u32[]{:S(2)}) copy-start(s32[8,32]{1,0:T(8,128)} %land.3) | copy-start | bytes 3076
  25.2 15.2 %copy-start.5 = (f32[256]{0:T(256)S(1)}, f32[256]{0:T(256)}, u32[]{:S(2)}) copy-start(f32[256]{0:T(256)} %param.77) | copy-start | bytes 3076
  26.0 14.4 %collective-permute-start.14 = (bf16[120,256]{1,0:T(8,128)(2,1)S(1)}, bf16[120,256]{1,0:T(8,128)(2,1)}, u32[]{:S(2)}, u32[]{:S(2)}) collective-permute-start(bf16[120,256]{1,0:T(8,128)(2,1)S(1)} %get-tuple-element.528), channel_id=1, source_target_pairs={{1,2},{3,4},{5,6},{7,8},{9,10},{11,12},{13,14},{2,1},{4,3},{6,5},{... | collective-permute-start | bytes 184328 | tf_op jit(solution)/shard_map/cond/branch_4_fun/ppermute | solution.py:297
  34.8 5.6 %collective-permute-start.15 = (bf16[120,256]{1,0:T(8,128)(2,1)S(1)}, bf16[120,256]{1,0:T(8,128)(2,1)}, u32[]{:S(2)}, u32[]{:S(2)}) collective-permute-start(bf16[120,256]{1,0:T(8,128)(2,1)S(1)} %get-tuple-element.529), channel_id=1, source_target_pairs={{79,15},{63,31},{47,47},{31,63},{15,79},{511,95},{495,111},{479,12... | collective-permute-start | bytes 184328 | tf_op jit(solution)/shard_map/cond/branch_4_fun/ppermute | solution.py:304
  36.1 4.4 %collective-permute-start.16 = (bf16[120,256]{1,0:T(8,128)(2,1)S(1)}, bf16[120,256]{1,0:T(8,128)(2,1)}, u32[]{:S(2)}, u32[]{:S(2)}) collective-permute-start(bf16[120,256]{1,0:T(8,128)(2,1)S(1)} %get-tuple-element.531), channel_id=1, source_target_pairs={{0,1},{2,3},{4,5},{6,7},{8,9},{10,11},{12,13},{14,15},{1,0},{3,2},... | collective-permute-start | bytes 184328 | tf_op jit(solution)/shard_map/cond/branch_4_fun/ppermute | solution.py:297
  47.4 29.7 %all-to-all-start = ((bf16[32,144,128]{2,1,0:T(8,128)(2,1)}), bf16[32,144,128]{2,1,0:T(8,128)(2,1)S(1)}, u32[]{:S(2)}, u32[]{:S(2)}) async-start(bf16[32,144,128]{2,1,0:T(8,128)(2,1)} %get-tuple-element.824), calls=%async_computation | async-start | bytes 2359296 | tf_op jit(solution)/shard_map/all_to_all | solution.py:354
  57.2 14.7 %collective-permute-start.226 = (bf16[160,256]{1,0:T(8,128)(2,1)S(1)}, bf16[160,256]{1,0:T(8,128)(2,1)S(1)}, u32[]{:S(2)}, u32[]{:S(2)}) collective-permute-start(bf16[160,256]{1,0:T(8,128)(2,1)S(1)} %get-tuple-element.814), channel_id=1, source_target_pairs={{16,32},{48,64},{80,96},{112,128},{144,160},{176,192},{208,224},{2... | collective-permute-start | bytes 245768 | tf_op jit(solution)/shard_map/ppermute | solution.py:297
  65.2 8.6 %collective-permute-start.227 = (bf16[160,256]{1,0:T(8,128)(2,1)S(1)}, bf16[160,256]{1,0:T(8,128)(2,1)S(1)}, u32[]{:S(2)}, u32[]{:S(2)}) collective-permute-start(bf16[160,256]{1,0:T(8,128)(2,1)S(1)} %get-tuple-element.815), channel_id=1, source_target_pairs={{0,16},{32,48},{64,80},{96,112},{128,144},{160,176},{192,208},{224... | collective-permute-start | bytes 245768 | tf_op jit(solution)/shard_map/ppermute | solution.py:297
  78.0 24.4 %all-to-all-start.1 = ((bf16[16,16,128]{2,1,0:T(8,128)(2,1)}), bf16[16,16,128]{2,1,0:T(8,128)(2,1)S(1)}, u32[]{:S(2)}, u32[]{:S(2)}) async-start(bf16[16,16,128]{2,1,0:T(8,128)(2,1)} %shard_map.132), calls=%async_computation.1 | async-start | bytes 131072 | tf_op jit(solution)/shard_map/all_to_all | solution.py:354
  84.2 16.8 %collective-permute-start.126 = (bf16[120,256]{1,0:T(8,128)(2,1)S(1)}, bf16[120,256]{1,0:T(8,128)(2,1)}, u32[]{:S(2)}, u32[]{:S(2)}) collective-permute-start(bf16[120,256]{1,0:T(8,128)(2,1)S(1)} %get-tuple-element.656), channel_id=1, source_target_pairs={{1,2},{3,4},{5,6},{7,8},{9,10},{11,12},{13,14},{2,1},{4,3},{6,5},{... | collective-permute-start | bytes 184328 | tf_op jit(solution)/shard_map/cond/branch_4_fun/ppermute | solution.py:297
  97.8 3.2 %collective-permute-start.127 = (bf16[120,256]{1,0:T(8,128)(2,1)S(1)}, bf16[120,256]{1,0:T(8,128)(2,1)}, u32[]{:S(2)}, u32[]{:S(2)}) collective-permute-start(bf16[120,256]{1,0:T(8,128)(2,1)S(1)} %get-tuple-element.657), channel_id=1, source_target_pairs={{79,15},{63,31},{47,47},{31,63},{15,79},{511,95},{495,111},{479,12... | collective-permute-start | bytes 184328 | tf_op jit(solution)/shard_map/cond/branch_4_fun/ppermute | solution.py:304
  99.1 3.3 %collective-permute-start.128 = (bf16[120,256]{1,0:T(8,128)(2,1)S(1)}, bf16[120,256]{1,0:T(8,128)(2,1)}, u32[]{:S(2)}, u32[]{:S(2)}) collective-permute-start(bf16[120,256]{1,0:T(8,128)(2,1)S(1)} %get-tuple-element.659), channel_id=1, source_target_pairs={{0,1},{2,3},{4,5},{6,7},{8,9},{10,11},{12,13},{14,15},{1,0},{3,2},... | collective-permute-start | bytes 184328 | tf_op jit(solution)/shard_map/cond/branch_4_fun/ppermute | solution.py:297
  103.1 11.3 %all-to-all-start.2 = ((f32[32,8,128]{2,1,0:T(8,128)}), f32[32,8,128]{2,1,0:T(8,128)S(1)}, u32[]{:S(2)}, u32[]{:S(2)}) async-start(f32[32,8,128]{2,1,0:T(8,128)} %get-tuple-element.827), calls=%async_computation.2 | async-start | bytes 262144 | tf_op jit(solution)/shard_map/all_to_all | solution.py:354

commit v5 on v4

--- a/solution.py
+++ b/solution.py
@@ -13,7 +13,7 @@
 ROWS, COLS, WIDTH, HIDDEN = 8, 32, 256, 1024
 CELLS = ROWS * COLS
 LANES = 128
-CHUNK = 256
+CHUNK = 512
 LEFT = 8
 ACROSS = 4
 EDGE = 8
@@ -188,7 +188,8 @@
                 block = wide[half, :, pl.ds(LEFT - 3 + tile * 8 + b, 8), :]
                 here = grid[:, pl.ds(tile * 8, 8), lanes]
                 for a in range(7):
-                    totals[a] = totals[a] + jnp.sum(block[a : a + ROWS] * here, 0)
+                    for row in range(ROWS):
+                        totals[a] = totals[a] + block[a + row] * here[row]
             for a in range(7):
                 tap = 7 * a + b
                 sums[tap // 2, pl.ds(2 * (tap % 2) + half, 1), :] = jnp.sum(totals[a], 0, keepdims=True)

time: 117 us -> 118 us (level); the launches traced: 115 us -> 119 us
  starting transfers between devices: 75.6 us -> 81.5 us
  waiting for transfers between devices: 18.7 us -> 17.3 us
    all_to_all x3, starting transfers between devices: 19.1 us -> 23.6 us  [spread(): lax.all_to_all(value, ('lon', 'lat'), 0, 0, axis_index_groups=groups, til...]
    ppermute x8, waiting for transfers between devices: 10.4 us -> 9.05 us  [swapped(): return lax.ppermute(value, axis, pairs + [(j, i) for i, j in pairs])]
    ppermute x2 -> x4, starting transfers between devices: 2.56 us -> 3.89 us  [fold_stage(): return lambda value: lax.ppermute(value, ('lon', 'lat'), pairs)]
  transfers between devices with their start and end apart: 13 -> 15, of which waited for: 6 -> 6; matrix products, arithmetic and copies ran while one was open for 4% -> 3% of each run, Pallas kernels for 3% -> 3%
where the time goes in v5:
time: 118 us; the launch traced here: 119 us
  starting transfers between devices  81.5 us (69%)
  waiting for transfers between devices  17.3 us (15%)
  Pallas kernels  13.3 us (11%)
  local copies, waits for them, and re-layouts  5.41 us (5%)
  between operations  1.57 us (1%)
    ppermute x8, starting transfers between devices, swapped(): return lax.ppermute(value, axis, pairs + [(j, i) for i, j in pairs])  54 us
    all_to_all x3, starting transfers between devices, spread(): lax.all_to_all(value, ('lon', 'lat'), 0, 0, axis_index_groups=groups, til...  23.6 us
    pallas_call x8, Pallas kernels, run(): return call(*scalars, *args, *waits)  13.3 us
    ppermute x8, waiting for transfers between devices, swapped(): return lax.ppermute(value, axis, pairs + [(j, i) for i, j in pairs])  9.05 us
    all_to_all x3, waiting for transfers between devices, spread(): lax.all_to_all(value, ('lon', 'lat'), 0, 0, axis_index_groups=groups, til...  8.28 us
    ppermute x4, starting transfers between devices, fold_stage(): return lambda value: lax.ppermute(value, ('lon', 'lat'), pairs)  3.89 us
    reshape x4, local copies, waits for them, and re-layouts, reordered(): split = weights.reshape(layout() + (-1, weights.shape[1]))  2.51 us
  transfers between devices with their start and end apart: 15, of which 6 were waited for; matrix products, arithmetic and copies ran while one was open for 3% of the time, Pallas kernels for 3%

profile of v5, /device:TPU:1, one launch (start us, length us, event | category | flops | bytes accessed | tf_op | source)
XLA Modules:
  0.0 119.3 jit_solution(9512385921030172526)
XLA Ops:
  0.7 0.1 pad_add_fusion.info
  0.7 0.9 copy-done
  1.6 0.6 shard_map.127
  2.2 15.9 %collective-permute-start.224 = (bf16[160,256]{1,0:T(8,128)(2,1)S(1)}, bf16[160,256]{1,0:T(8,128)(2,1)S(1)}, u32[]{:S(2)}, u32[]{:S(2)}) collective-permute-start(bf16[160,256]{1,0:T(8,128)(2,1)S(1)} %get-tuple-element.802), channel_id=1, source_target_pairs={{16,32},{48,64},{80,96},{112,128},{144,160},{176,192},{208,224},{2... | collective-permute-start | bytes 245768 | tf_op jit(solution)/shard_map/ppermute | solution.py:298
  18.1 1.9 %collective-permute-start.225 = (bf16[160,256]{1,0:T(8,128)(2,1)S(1)}, bf16[160,256]{1,0:T(8,128)(2,1)S(1)}, u32[]{:S(2)}, u32[]{:S(2)}) collective-permute-start(bf16[160,256]{1,0:T(8,128)(2,1)S(1)} %get-tuple-element.803), channel_id=1, source_target_pairs={{0,16},{32,48},{64,80},{96,112},{128,144},{160,176},{192,208},{224... | collective-permute-start | bytes 245768 | tf_op jit(solution)/shard_map/ppermute | solution.py:298
  20.0 1.2 %slice.3 = s32[1]{0:T(128)} slice(s32[1024]{0:T(1024)} %param.75), slice={[0:1]} | slice | bytes 8 | tf_op jit(solution)/shard_map/slice | solution.py:366
  21.9 1.2 %reshape.36 = bf16[8,4,4,2,2,2,256]{6,5,4,3,2,1,0:T(2,128)(2,1)S(1)} reshape(bf16[1024,256]{1,0:T(8,128)(2,1)} %param.78) | data formatting | bytes 1048576 | tf_op jit(solution)/shard_map/reshape | solution.py:359
  23.2 0.0 copy-start.6
  23.2 0.5 copy.19
  23.7 0.2 reshape.37.refs_0_.w_in
  23.9 0.3 copy-done.6
  24.2 0.2 reshape.38
  24.4 0.0 copy-start.1
  24.4 0.5 copy.18
  25.0 0.2 reshape.39.refs_1_.w_out
  25.2 0.0 copy-start.2
  25.2 0.0 copy-start.3
  25.2 0.0 copy-start.4
  25.2 0.0 copy-start.5
  25.3 0.1 copy-done.1
  25.3 0.6 shard_map.128
  25.9 14.5 %conditional.2 = (bf16[120,256]{1,0:T(8,128)(2,1)}, bf16[120,256]{1,0:T(8,128)(2,1)}, bf16[32,256]{1,0:T(8,128)(2,1)S(1)}, bf16[120,256]{1,0:T(8,128)(2,1)}) conditional(s32[]{:T(128)} %clamp.4, (bf16[120,256]{1,0:T(8,128)(2,1)S(1)}, bf16[120,256]{1,0:T(8,128)(2,1)S(1)}, bf16[120,256]{1,0:T(8,128)(2,1)S(1)}, ...), branch_computations={%region_0.1_spmd, %region_1.2_spmd, %region_2.3_spmd, %region_3.4_... | conditional | bytes 835776 | solution.py:338
  26.0 8.8 %collective-permute-start.101 = (bf16[120,256]{1,0:T(8,128)(2,1)S(1)}, bf16[120,256]{1,0:T(8,128)(2,1)}, u32[]{:S(2)}, u32[]{:S(2)}) collective-permute-start(bf16[120,256]{1,0:T(8,128)(2,1)S(1)} %get-tuple-element.628), channel_id=1, source_target_pairs={{1,2},{3,4},{5,6},{7,8},{9,10},{11,12},{13,14},{2,1},{4,3},{6,5},{... | collective-permute-start | bytes 184328 | tf_op jit(solution)/shard_map/cond/branch_29_fun/ppermute | solution.py:298
  34.8 1.3 %collective-permute-start.102 = (bf16[120,256]{1,0:T(8,128)(2,1)S(1)}, bf16[120,256]{1,0:T(8,128)(2,1)}, u32[]{:S(2)}, u32[]{:S(2)}) collective-permute-start(bf16[120,256]{1,0:T(8,128)(2,1)S(1)} %get-tuple-element.629), channel_id=1, source_target_pairs={{463,15},{447,31},{431,47},{415,63},{399,79},{383,95},{367,111},{3... | collective-permute-start | bytes 184328 | tf_op jit(solution)/shard_map/cond/branch_29_fun/ppermute | solution.py:305
  36.1 1.9 %collective-permute-start.104 = (bf16[120,256]{1,0:T(8,128)(2,1)S(1)}, bf16[120,256]{1,0:T(8,128)(2,1)}, u32[]{:S(2)}, u32[]{:S(2)}) collective-permute-start(bf16[120,256]{1,0:T(8,128)(2,1)S(1)} %get-tuple-element.631), channel_id=1, source_target_pairs={{0,1},{2,3},{4,5},{6,7},{8,9},{10,11},{12,13},{14,15},{1,0},{3,2},... | collective-permute-start | bytes 184328 | tf_op jit(solution)/shard_map/cond/branch_29_fun/ppermute | solution.py:298
  38.0 0.7 collective-permute-start.103
  38.7 1.7 %collective-permute-done.101 = bf16[120,256]{1,0:T(8,128)(2,1)} collective-permute-done((bf16[120,256]{1,0:T(8,128)(2,1)S(1)}, bf16[120,256]{1,0:T(8,128)(2,1)}, u32[]{:S(2)}, u32[]{:S(2)}) %collective-permute-start.101) | collective-permute-done | bytes 61472 | tf_op jit(solution)/shard_map/cond/branch_29_fun/ppermute | solution.py:298
  40.5 6.7 %shard_map.129 = (bf16[8,32,256]{2,1,0:T(8,128)(2,1)}, bf16[8,32,256]{2,1,0:T(8,128)(2,1)S(1)}, bf16[160,256]{1,0:T(8,128)(2,1)S(1)}, bf16[160,256]{1,0:T(8,128)(2,1)S(1)}, bf16[32,144,128]{2,1,0:T(8,128)(2,1)}) custom-call(s32[3]{0:T(128)S(1)} %pad_add_fusion.info, s32[1]{0:T(128)} %bitcast.4.turn, bf16[8,32,256]{2,1,0:T(8,128)(2,1)S(1)} %copy-done.1, ...), custom_call_target="tpu_custom_call" | custom-call | tf_op jit(solution)/shard_map/pallas_call | solution.py:292
  47.2 9.7 %all-to-all-start = ((bf16[32,144,128]{2,1,0:T(8,128)(2,1)}), bf16[32,144,128]{2,1,0:T(8,128)(2,1)S(1)}, u32[]{:S(2)}, u32[]{:S(2)}) async-start(bf16[32,144,128]{2,1,0:T(8,128)(2,1)} %get-tuple-element.824), calls=%async_computation | async-start | bytes 2359296 | tf_op jit(solution)/shard_map/all_to_all | solution.py:355
  56.9 8.1 %collective-permute-start.226 = (bf16[160,256]{1,0:T(8,128)(2,1)S(1)}, bf16[160,256]{1,0:T(8,128)(2,1)S(1)}, u32[]{:S(2)}, u32[]{:S(2)}) collective-permute-start(bf16[160,256]{1,0:T(8,128)(2,1)S(1)} %get-tuple-element.814), channel_id=1, source_target_pairs={{16,32},{48,64},{80,96},{112,128},{144,160},{176,192},{208,224},{2... | collective-permute-start | bytes 245768 | tf_op jit(solution)/shard_map/ppermute | solution.py:298
  65.0 1.9 %collective-permute-start.227 = (bf16[160,256]{1,0:T(8,128)(2,1)S(1)}, bf16[160,256]{1,0:T(8,128)(2,1)S(1)}, u32[]{:S(2)}, u32[]{:S(2)}) collective-permute-start(bf16[160,256]{1,0:T(8,128)(2,1)S(1)} %get-tuple-element.815), channel_id=1, source_target_pairs={{0,16},{32,48},{64,80},{96,112},{128,144},{160,176},{192,208},{224... | collective-permute-start | bytes 245768 | tf_op jit(solution)/shard_map/ppermute | solution.py:298
  66.9 4.7 %collective-permute-done.226.side1.refs_0_ = bf16[160,256]{1,0:T(8,128)(2,1)S(1)} collective-permute-done((bf16[160,256]{1,0:T(8,128)(2,1)S(1)}, bf16[160,256]{1,0:T(8,128)(2,1)S(1)}, u32[]{:S(2)}, u32[]{:S(2)}) %collective-permute-start.226) | collective-permute-done | bytes 81952 | tf_op jit(solution)/shard_map/ppermute | solution.py:298
  71.6 2.0 %collective-permute-done.227.side0.refs_1_ = bf16[160,256]{1,0:T(8,128)(2,1)S(1)} collective-permute-done((bf16[160,256]{1,0:T(8,128)(2,1)S(1)}, bf16[160,256]{1,0:T(8,128)(2,1)S(1)}, u32[]{:S(2)}, u32[]{:S(2)}) %collective-permute-start.227) | collective-permute-done | bytes 81952 | tf_op jit(solution)/shard_map/ppermute | solution.py:298
  73.6 3.4 %all-to-all-done.received = bf16[32,144,128]{2,1,0:T(8,128)(2,1)S(1)} async-done(((bf16[32,144,128]{2,1,0:T(8,128)(2,1)}), bf16[32,144,128]{2,1,0:T(8,128)(2,1)S(1)}, u32[]{:S(2)}, u32[]{:S(2)}) %all-to-all-start) | async-done | bytes 1179680 | tf_op jit(solution)/shard_map/all_to_all | solution.py:355
  76.9 0.8 shard_map.132
  77.7 10.1 %all-to-all-start.1 = ((bf16[16,16,128]{2,1,0:T(8,128)(2,1)}), bf16[16,16,128]{2,1,0:T(8,128)(2,1)S(1)}, u32[]{:S(2)}, u32[]{:S(2)}) async-start(bf16[16,16,128]{2,1,0:T(8,128)(2,1)} %shard_map.132), calls=%async_computation.1 | async-start | bytes 131072 | tf_op jit(solution)/shard_map/all_to_all | solution.py:355
  87.9 0.6 shard_map.130
  88.5 18.2 %conditional.3 = (bf16[120,256]{1,0:T(8,128)(2,1)}, bf16[120,256]{1,0:T(8,128)(2,1)}, bf16[32,256]{1,0:T(8,128)(2,1)S(1)}, bf16[120,256]{1,0:T(8,128)(2,1)}) conditional(s32[]{:T(128)} %clamp.4, (bf16[120,256]{1,0:T(8,128)(2,1)S(1)}, bf16[120,256]{1,0:T(8,128)(2,1)S(1)}, bf16[120,256]{1,0:T(8,128)(2,1)S(1)}, ...), branch_computations={%region_32.33_spmd, %region_33.34_spmd, %region_34.35_spmd, %regio... | conditional | bytes 835776 | solution.py:338
  88.6 13.6 %collective-permute-start.213 = (bf16[120,256]{1,0:T(8,128)(2,1)S(1)}, bf16[120,256]{1,0:T(8,128)(2,1)}, u32[]{:S(2)}, u32[]{:S(2)}) collective-permute-start(bf16[120,256]{1,0:T(8,128)(2,1)S(1)} %get-tuple-element.756), channel_id=1, source_target_pairs={{1,2},{3,4},{5,6},{7,8},{9,10},{11,12},{13,14},{2,1},{4,3},{6,5},{... | collective-permute-start | bytes 184328 | tf_op jit(solution)/shard_map/cond/branch_29_fun/ppermute | solution.py:298
  102.1 1.3 %collective-permute-start.214 = (bf16[120,256]{1,0:T(8,128)(2,1)S(1)}, bf16[120,256]{1,0:T(8,128)(2,1)}, u32[]{:S(2)}, u32[]{:S(2)}) collective-permute-start(bf16[120,256]{1,0:T(8,128)(2,1)S(1)} %get-tuple-element.757), channel_id=1, source_target_pairs={{463,15},{447,31},{431,47},{415,63},{399,79},{383,95},{367,111},{3... | collective-permute-start | bytes 184328 | tf_op jit(solution)/shard_map/cond/branch_29_fun/ppermute | solution.py:305
  103.4 1.9 %collective-permute-start.216 = (bf16[120,256]{1,0:T(8,128)(2,1)S(1)}, bf16[120,256]{1,0:T(8,128)(2,1)}, u32[]{:S(2)}, u32[]{:S(2)}) collective-permute-start(bf16[120,256]{1,0:T(8,128)(2,1)S(1)} %get-tuple-element.759), channel_id=1, source_target_pairs={{0,1},{2,3},{4,5},{6,7},{8,9},{10,11},{12,13},{14,15},{1,0},{3,2},... | collective-permute-start | bytes 184328 | tf_op jit(solution)/shard_map/cond/branch_29_fun/ppermute | solution.py:298
  105.3 0.7 collective-permute-start.215
  106.1 0.6 collective-permute-done.216
  106.7 0.7 shard_map.133
  107.4 3.8 %all-to-all-start.2 = ((f32[32,8,128]{2,1,0:T(8,128)}), f32[32,8,128]{2,1,0:T(8,128)S(1)}, u32[]{:S(2)}, u32[]{:S(2)}) async-start(f32[32,8,128]{2,1,0:T(8,128)} %get-tuple-element.827), calls=%async_computation.2 | async-start | bytes 262144 | tf_op jit(solution)/shard_map/all_to_all | solution.py:355
  111.1 2.6 %shard_map.131 = bf16[8,32,256]{2,1,0:T(8,128)(2,1)} custom-call(s32[3]{0:T(128)S(1)} %pad_add_fusion.info, s32[1]{0:T(128)} %bitcast.4.turn, bf16[8,32,256]{2,1,0:T(8,128)(2,1)S(1)} %get-tuple-element.813.own, bf16[160,256]{1,0:T(8,128)(2,1)S(1)} %collective-permute-done.226.side1.refs_0_, bf16[160,256]{1,0:T(8,128)(2,1)S(1)} %collective-permute-done.227.side0.refs_1_, ...), custom_call_target="tpu_custom_call" | custom-call | tf_op jit(solution)/shard_map/pallas_call | solution.py:292
  113.8 4.9 %all-to-all-done.2.received = f32[32,8,128]{2,1,0:T(8,128)S(1)} async-done(((f32[32,8,128]{2,1,0:T(8,128)}), f32[32,8,128]{2,1,0:T(8,128)S(1)}, u32[]{:S(2)}, u32[]{:S(2)}) %all-to-all-start.2) | async-done | bytes 131104 | tf_op jit(solution)/shard_map/all_to_all | solution.py:355
  118.7 0.7 shard_map.134
  (16 shorter events, 0.0 us)
Async XLA Ops:
  0.7 0.9 copy-start
  2.2 23.1 %collective-permute-start.224 = (bf16[160,256]{1,0:T(8,128)(2,1)S(1)}, bf16[160,256]{1,0:T(8,128)(2,1)S(1)}, u32[]{:S(2)}, u32[]{:S(2)}) collective-permute-start(bf16[160,256]{1,0:T(8,128)(2,1)S(1)} %get-tuple-element.802), channel_id=1, source_target_pairs={{16,32},{48,64},{80,96},{112,128},{144,160},{176,192},{208,224},{2... | collective-permute-start | bytes 245768 | tf_op jit(solution)/shard_map/ppermute | solution.py:298
  18.1 7.2 %collective-permute-start.225 = (bf16[160,256]{1,0:T(8,128)(2,1)S(1)}, bf16[160,256]{1,0:T(8,128)(2,1)S(1)}, u32[]{:S(2)}, u32[]{:S(2)}) collective-permute-start(bf16[160,256]{1,0:T(8,128)(2,1)S(1)} %get-tuple-element.803), channel_id=1, source_target_pairs={{0,16},{32,48},{64,80},{96,112},{128,144},{160,176},{192,208},{224... | collective-permute-start | bytes 245768 | tf_op jit(solution)/shard_map/ppermute | solution.py:298
  23.2 1.0 copy-start.6
  24.4 0.9 copy-start.1
  25.2 15.2 %copy-start.2 = (bf16[8,32,256]{2,1,0:T(8,128)(2,1)S(1)}, bf16[8,32,256]{2,1,0:T(8,128)(2,1)}, u32[]{:S(2)}) copy-start(bf16[8,32,256]{2,1,0:T(8,128)(2,1)} %cot.3) | copy-start | bytes 393220
  25.2 15.2 %copy-start.3 = (f32[7,7,256]{2,1,0:T(8,128)S(1)}, f32[7,7,256]{2,1,0:T(8,128)}, u32[]{:S(2)}) copy-start(f32[7,7,256]{2,1,0:T(8,128)} %taps.3) | copy-start | bytes 150532
  25.2 15.2 %copy-start.4 = (s32[8,32]{1,0:T(8,128)S(1)}, s32[8,32]{1,0:T(8,128)}, u32[]{:S(2)}) copy-start(s32[8,32]{1,0:T(8,128)} %land.3) | copy-start | bytes 3076
  25.2 15.2 %copy-start.5 = (f32[256]{0:T(256)S(1)}, f32[256]{0:T(256)}, u32[]{:S(2)}) copy-start(f32[256]{0:T(256)} %param.77) | copy-start | bytes 3076
  26.0 14.4 %collective-permute-start.101 = (bf16[120,256]{1,0:T(8,128)(2,1)S(1)}, bf16[120,256]{1,0:T(8,128)(2,1)}, u32[]{:S(2)}, u32[]{:S(2)}) collective-permute-start(bf16[120,256]{1,0:T(8,128)(2,1)S(1)} %get-tuple-element.628), channel_id=1, source_target_pairs={{1,2},{3,4},{5,6},{7,8},{9,10},{11,12},{13,14},{2,1},{4,3},{6,5},{... | collective-permute-start | bytes 184328 | tf_op jit(solution)/shard_map/cond/branch_29_fun/ppermute | solution.py:298
  34.8 5.6 %collective-permute-start.102 = (bf16[120,256]{1,0:T(8,128)(2,1)S(1)}, bf16[120,256]{1,0:T(8,128)(2,1)}, u32[]{:S(2)}, u32[]{:S(2)}) collective-permute-start(bf16[120,256]{1,0:T(8,128)(2,1)S(1)} %get-tuple-element.629), channel_id=1, source_target_pairs={{463,15},{447,31},{431,47},{415,63},{399,79},{383,95},{367,111},{3... | collective-permute-start | bytes 184328 | tf_op jit(solution)/shard_map/cond/branch_29_fun/ppermute | solution.py:305
  36.1 4.4 %collective-permute-start.104 = (bf16[120,256]{1,0:T(8,128)(2,1)S(1)}, bf16[120,256]{1,0:T(8,128)(2,1)}, u32[]{:S(2)}, u32[]{:S(2)}) collective-permute-start(bf16[120,256]{1,0:T(8,128)(2,1)S(1)} %get-tuple-element.631), channel_id=1, source_target_pairs={{0,1},{2,3},{4,5},{6,7},{8,9},{10,11},{12,13},{14,15},{1,0},{3,2},... | collective-permute-start | bytes 184328 | tf_op jit(solution)/shard_map/cond/branch_29_fun/ppermute | solution.py:298
  38.0 0.7 collective-permute-start.103
  47.2 29.7 %all-to-all-start = ((bf16[32,144,128]{2,1,0:T(8,128)(2,1)}), bf16[32,144,128]{2,1,0:T(8,128)(2,1)S(1)}, u32[]{:S(2)}, u32[]{:S(2)}) async-start(bf16[32,144,128]{2,1,0:T(8,128)(2,1)} %get-tuple-element.824), calls=%async_computation | async-start | bytes 2359296 | tf_op jit(solution)/shard_map/all_to_all | solution.py:355
  56.9 14.7 %collective-permute-start.226 = (bf16[160,256]{1,0:T(8,128)(2,1)S(1)}, bf16[160,256]{1,0:T(8,128)(2,1)S(1)}, u32[]{:S(2)}, u32[]{:S(2)}) collective-permute-start(bf16[160,256]{1,0:T(8,128)(2,1)S(1)} %get-tuple-element.814), channel_id=1, source_target_pairs={{16,32},{48,64},{80,96},{112,128},{144,160},{176,192},{208,224},{2... | collective-permute-start | bytes 245768 | tf_op jit(solution)/shard_map/ppermute | solution.py:298
  65.0 8.6 %collective-permute-start.227 = (bf16[160,256]{1,0:T(8,128)(2,1)S(1)}, bf16[160,256]{1,0:T(8,128)(2,1)S(1)}, u32[]{:S(2)}, u32[]{:S(2)}) collective-permute-start(bf16[160,256]{1,0:T(8,128)(2,1)S(1)} %get-tuple-element.815), channel_id=1, source_target_pairs={{0,16},{32,48},{64,80},{96,112},{128,144},{160,176},{192,208},{224... | collective-permute-start | bytes 245768 | tf_op jit(solution)/shard_map/ppermute | solution.py:298
  77.7 29.0 %all-to-all-start.1 = ((bf16[16,16,128]{2,1,0:T(8,128)(2,1)}), bf16[16,16,128]{2,1,0:T(8,128)(2,1)S(1)}, u32[]{:S(2)}, u32[]{:S(2)}) async-start(bf16[16,16,128]{2,1,0:T(8,128)(2,1)} %shard_map.132), calls=%async_computation.1 | async-start | bytes 131072 | tf_op jit(solution)/shard_map/all_to_all | solution.py:355
  88.6 17.5 %collective-permute-start.213 = (bf16[120,256]{1,0:T(8,128)(2,1)S(1)}, bf16[120,256]{1,0:T(8,128)(2,1)}, u32[]{:S(2)}, u32[]{:S(2)}) collective-permute-start(bf16[120,256]{1,0:T(8,128)(2,1)S(1)} %get-tuple-element.756), channel_id=1, source_target_pairs={{1,2},{3,4},{5,6},{7,8},{9,10},{11,12},{13,14},{2,1},{4,3},{6,5},{... | collective-permute-start | bytes 184328 | tf_op jit(solution)/shard_map/cond/branch_29_fun/ppermute | solution.py:298
  102.1 3.9 %collective-permute-start.214 = (bf16[120,256]{1,0:T(8,128)(2,1)S(1)}, bf16[120,256]{1,0:T(8,128)(2,1)}, u32[]{:S(2)}, u32[]{:S(2)}) collective-permute-start(bf16[120,256]{1,0:T(8,128)(2,1)S(1)} %get-tuple-element.757), channel_id=1, source_target_pairs={{463,15},{447,31},{431,47},{415,63},{399,79},{383,95},{367,111},{3... | collective-permute-start | bytes 184328 | tf_op jit(solution)/shard_map/cond/branch_29_fun/ppermute | solution.py:305
  103.4 3.3 %collective-permute-start.216 = (bf16[120,256]{1,0:T(8,128)(2,1)S(1)}, bf16[120,256]{1,0:T(8,128)(2,1)}, u32[]{:S(2)}, u32[]{:S(2)}) collective-permute-start(bf16[120,256]{1,0:T(8,128)(2,1)S(1)} %get-tuple-element.759), channel_id=1, source_target_pairs={{0,1},{2,3},{4,5},{6,7},{8,9},{10,11},{12,13},{14,15},{1,0},{3,2},... | collective-permute-start | bytes 184328 | tf_op jit(solution)/shard_map/cond/branch_29_fun/ppermute | solution.py:298
  105.3 0.7 collective-permute-start.215
  107.4 11.3 %all-to-all-start.2 = ((f32[32,8,128]{2,1,0:T(8,128)}), f32[32,8,128]{2,1,0:T(8,128)S(1)}, u32[]{:S(2)}, u32[]{:S(2)}) async-start(f32[32,8,128]{2,1,0:T(8,128)} %get-tuple-element.827), calls=%async_computation.2 | async-start | bytes 262144 | tf_op jit(solution)/shard_map/all_to_all | solution.py:355
